TPU v7x, 32 devices: a whole 2x2x4 slice. The times are simulated.
32 devices in a mesh: dp: 16 (over z, y, x), mp: 2 (over core).
Axes of the slice: x: 2, y: 2, z: 4, core: 2. Of those that a mesh axis runs over, the one named last changes fastest.
Arguments:
- pixels: bfloat16 [32, 512, 768], P(('dp', 'mp')), may hold values from -6 to 6
- counts: int32 [16, 2], P('dp'), may hold values from 128 to 512
- owner: int32 [16, 2], P('dp'), may hold values from 0 to 1, each once within a row
- embed_weight: bfloat16 [768, 1024], P('dp', 'mp'), may hold values from -0.21875 to 0.21875
- w_qkv: bfloat16 [3, 1024, 1024], P(None, 'dp', 'mp'), may hold values from -0.8 to 0.8
- w_out: bfloat16 [1024, 1024], P('mp', 'dp'), may hold values from -0.1875 to 0.1875
- w_up: bfloat16 [1024, 4096], P('dp', 'mp'), may hold values from -0.1875 to 0.1875
- w_down: bfloat16 [4096, 1024], P('mp', 'dp'), may hold values from -0.09375 to 0.09375
- ln1_gain: float32 [1024], replicated, may hold values from 0.25 to 1.75
- ln2_gain: float32 [1024], replicated, may hold values from 0.25 to 1.75
- targets: bfloat16 [16, 2, 512, 1024], P('dp', None, 'mp'), may hold values from -20 to 20
Outputs:
- encoded: bfloat16 [16, 2, 512, 1024], P('dp', None, 'mp')
- mean_loss: float32 [], replicated
Inputs may be any that keep to these rules, and one draw needn't show every extreme that they name: counts[g, r] is the number of valid patches at the start of image g * 2 + r; the remaining patch slots are padding. Each row owner[g, :] is a permutation of 0 to 2 - 1, so every held image is encoded once.
All inputs are finite; a program needn't handle non-finite values.
Results may differ from a plain program's by a relative error of at most 0.014.
Values may be sent and summed in bfloat16 or wider, within the bound.
No kernel may reach another device: no remote copies, remote signals or barrier semaphores. Data moves between devices by JAX's collectives and lax.ppermute only.
A program may use at most 128 MiB of HBM per device.

v0:
```python
import jax
import jax.numpy as jnp
from jax import lax
from jax.sharding import PartitionSpec as P

D = 1024
HEAD = 64


def layer_norm(inputs, gains):
    average = jnp.mean(inputs, axis=-1, keepdims=True)
    centred = inputs - average
    spread = jnp.mean(centred * centred, axis=-1, keepdims=True)
    return centred * lax.rsqrt(spread + 1e-06) * gains


def group_sum(left_mat, right_mat, groups):
    row_count = left_mat.shape[0]
    column_width = left_mat.shape[1] // groups
    left_part = left_mat.reshape(row_count, groups, column_width)
    right_part = right_mat.reshape(groups, column_width, right_mat.shape[1])
    partial_value = jnp.einsum(
        "pgh,ghd->gpd", left_part, right_part, preferred_element_type=jnp.float32
    ).astype(jnp.bfloat16)
    partial_value = lax.optimization_barrier(partial_value)
    return jnp.sum(partial_value.astype(jnp.float32), axis=0)


def attend(queries, key_rows, value_rows, usable):

    def one_head(operands):
        query_part, key_part, value_part = operands
        scores = jnp.einsum("qd,kd->qk", query_part, key_part, preferred_element_type=jnp.float32)
        scores = jnp.where(usable[None, :], scores, -1e30)
        row_max = jnp.max(scores, axis=-1, keepdims=True)
        expo = jnp.exp(scores - row_max)
        row_sum = jnp.sum(expo, axis=-1)
        mixed = jnp.dot(expo.astype(jnp.bfloat16), value_part, preferred_element_type=jnp.float32)
        return mixed / row_sum[:, None]

    return lax.map(one_head, (queries, key_rows, value_rows))


def attention_heads(queries, key_rows, value_rows, length, patches):
    usable = jnp.arange(patches, dtype=jnp.int32) < length
    return attend(queries, key_rows, value_rows, usable)


def split_heads(projected, patches, factor):
    width = projected.shape[2]
    heads_here = width // HEAD
    queries = (
        (projected[0] * factor)
        .astype(jnp.bfloat16)
        .reshape(patches, heads_here, HEAD)
        .transpose(1, 0, 2)
    )
    key_rows = (
        projected[1].astype(jnp.bfloat16).reshape(patches, heads_here, HEAD).transpose(1, 0, 2)
    )
    value_rows = (
        projected[2].astype(jnp.bfloat16).reshape(patches, heads_here, HEAD).transpose(1, 0, 2)
    )
    return (queries, key_rows, value_rows)


def on_device(
    pixels, counts, owner, embed_weight, w_qkv, w_out, w_up, w_down, ln1_gain, ln2_gain, targets
):
    picture = pixels[0]
    patches = picture.shape[0]
    group_size = lax.axis_size("mp")
    position = lax.axis_index("mp")
    rows_own = patches // group_size
    order = owner[0]
    lengths_all = counts[0]
    slot_ids = jnp.arange(group_size, dtype=jnp.int32)
    factor = HEAD ** (-0.5)
    embed_cols, up_cols = (
        lax.all_gather(embed_weight, "dp", axis=0, tiled=True),
        lax.all_gather(w_up, "dp", axis=0, tiled=True),
    )
    qkv_cols, out_rows, down_rows = (
        lax.all_gather(w_qkv, "dp", axis=1, tiled=True),
        lax.all_gather(w_out, "dp", axis=1, tiled=True),
        lax.all_gather(w_down, "dp", axis=1, tiled=True),
    )
    embed_whole, up_whole = (
        lax.all_gather(embed_cols, "mp", axis=1, tiled=True),
        lax.all_gather(up_cols, "mp", axis=1, tiled=True),
    )
    qkv_whole = lax.all_gather(qkv_cols, "mp", axis=2, tiled=True)
    out_whole, down_whole = (
        lax.all_gather(out_rows, "mp", axis=0, tiled=True),
        lax.all_gather(down_rows, "mp", axis=0, tiled=True),
    )
    length = jnp.sum(jnp.where(slot_ids == position, lengths_all, 0))
    inverse = jnp.sum(jnp.where(order[None, :] == slot_ids[:, None], slot_ids[None, :], 0), axis=1)
    by_image = jnp.take(targets[0], inverse, axis=0)
    wanted = (
        lax.all_to_all(by_image, "mp", split_axis=0, concat_axis=0, tiled=True)
        .reshape(patches, D)
        .astype(jnp.float32)
    )
    tokens = jnp.dot(picture, embed_whole, preferred_element_type=jnp.float32).astype(jnp.bfloat16)
    normed = layer_norm(tokens.astype(jnp.float32), ln1_gain).astype(jnp.bfloat16)
    projected = jnp.einsum("pd,cdh->cph", normed, qkv_whole, preferred_element_type=jnp.float32)
    queries, key_rows, value_rows = split_heads(projected, patches, factor)
    mixture = attention_heads(queries, key_rows, value_rows, length, patches)
    attended = mixture.transpose(1, 0, 2).astype(jnp.bfloat16).reshape(patches, D)
    residual = tokens.astype(jnp.float32) + group_sum(attended, out_whole, group_size)
    normed_two = layer_norm(residual, ln2_gain).astype(jnp.bfloat16)
    hidden = jax.nn.gelu(
        jnp.dot(normed_two, up_whole, preferred_element_type=jnp.float32), approximate=False
    ).astype(jnp.bfloat16)
    output = residual + group_sum(hidden, down_whole, group_size)
    usable = jnp.arange(patches, dtype=jnp.int32) < length
    misfit = output - wanted
    squares = jnp.sum(jnp.where(usable[:, None], misfit * misfit, 0.0))
    number = jnp.sum(usable.astype(jnp.float32))
    pieces = output.astype(jnp.bfloat16).reshape(group_size, rows_own, D)
    received = lax.all_to_all(pieces, "mp", split_axis=0, concat_axis=0, tiled=True)
    encoded = jnp.take(received, order, axis=0)
    total_squares, total_number = lax.psum((squares, number), ("dp", "mp"))
    return (encoded[None], total_squares / (D * total_number))


def solution(mesh):
    in_specs = (
        P(("dp", "mp"), None, None),
        P("dp", None),
        P("dp", None),
        P("dp", "mp"),
        P(None, "dp", "mp"),
        P("mp", "dp"),
        P("dp", "mp"),
        P("mp", "dp"),
        P(),
        P(),
        P("dp", None, "mp", None),
    )
    out_specs = (P("dp", None, "mp", None), P())
    return jax.shard_map(
        on_device, mesh=mesh, in_specs=in_specs, out_specs=out_specs, check_vma=False
    )
```

profile of v0, /device:TPU:0, one launch (start us, length us, event | category | flops | bytes accessed | tf_op | source)
XLA Modules:
  0.0 520.2 jit_solution(13476782763731247618)
XLA Ops:
  9.5 50.3 %all_gather.30 = bf16[768,512]{1,0:T(8,128)(2,1)} all-gather(bf16[48,512]{1,0:T(8,128)(2,1)} %param.18), channel_id=1, replica_groups=mesh['dp'=16,'mp'=2] {'dp'}, dimensions={0}, use_global_device_ids=true | all-gather | bytes 835584 | tf_op jit(solution)/shard_map/all_gather | solution.py:80
  59.9 10.0 %all-gather.16.cloned.1.call-done = bf16[512,1024]{0,1:T(8,128)(2,1)} async-done(((bf16[512,64]{0,1:T(8,128)(2,1)}), bf16[512,1024]{0,1:T(8,128)(2,1)}) %all-gather.16.cloned.1.call-update) | async-done | bytes 1048592 | tf_op jit(solution)/shard_map/all_gather | solution.py:85
  70.5 68.5 %all-gather.12.cloned.1.call-done = bf16[3,1024,512]{2,1,0:T(8,128)(2,1)} async-done(((bf16[3,64,512]{2,1,0:T(8,128)(2,1)}), bf16[3,1024,512]{2,1,0:T(8,128)(2,1)}) %all-gather.12.cloned.1.call-update) | async-done | bytes 3145744 | tf_op jit(solution)/shard_map/all_gather | solution.py:84
  139.1 77.9 %all-gather.24.cloned.1.call-done = bf16[2048,1024]{0,1:T(8,128)(2,1)} async-done(((bf16[2048,64]{0,1:T(8,128)(2,1)}), bf16[2048,1024]{0,1:T(8,128)(2,1)}) %all-gather.24.cloned.1.call-update) | async-done | bytes 4194320 | tf_op jit(solution)/shard_map/all_gather | solution.py:86
  218.9 4.6 all-to-all-start.1
  226.8 2.5 convert_reduce_fusion.2
  229.7 10.2 %all-gather.18.cloned.1.call-done = bf16[1024,1024]{0,1:T(8,128)(2,1)} async-done(((bf16[512,1024]{0,1:T(8,128)(2,1)}), bf16[1024,1024]{0,1:T(8,128)(2,1)}) %all-gather.18.cloned.1.call-update) | async-done | bytes 2097168 | tf_op jit(solution)/shard_map/all_gather | solution.py:94
  240.0 3.9 copy.36
  243.9 76.0 %all-gather.20.cloned.1.call-done = bf16[1024,2048]{1,0:T(8,128)(2,1)} async-done(((bf16[64,2048]{1,0:T(8,128)(2,1)}), bf16[1024,2048]{1,0:T(8,128)(2,1)}) %all-gather.20.cloned.1.call-update) | async-done | bytes 4194320 | tf_op jit(solution)/shard_map/all_gather | solution.py:81
  319.9 16.9 %all-gather.14.cloned.1.call-done = bf16[3,1024,1024]{2,1,0:T(8,128)(2,1)} async-done(((bf16[3,1024,512]{2,1,0:T(8,128)(2,1)}), bf16[3,1024,1024]{2,1,0:T(8,128)(2,1)}) %all-gather.14.cloned.1.call-update) | async-done | bytes 6291472 | tf_op jit(solution)/shard_map/all_gather | solution.py:92
  336.8 8.3 %fusion.56 = (bf16[3,512,1024]{2,1,0:T(8,128)(2,1)S(1)}, f32[3,512,1024]{2,1,0:T(8,128)}) fusion(bf16[3,1024,1024]{2,1,0:T(8,128)(2,1)} %all-gather.14.cloned.1.call-done, bf16[512,1024]{1,0:T(8,128)(2,1)S(1)} %get-tuple-element.84, f32[1024]{0:T(1024)S(1)} %copy-done.7, f32[512]{0:T(512)S(1)} %add_rsqrt_fusion.1, f32[512]{0:T(512)S(1)} %broadcast_multiply_fusion.1), kind=kOutput, calls=%fused_computation.95 | convolution fusion | flops 3225419776 | bytes 16785408 | tf_op jit(solution)/shard_map/pd,cdh->cph/dot_general | solution.py:107
  347.9 2.2 fusion.34
  351.5 62.2 %while.11 = (s32[]{:T(128)}, bf16[16,512,64]{1,2,0:T(8,128)(2,1)}, bf16[16,512,64]{1,2,0:T(8,128)(2,1)}, bf16[16,512,64]{1,2,0:T(8,128)(2,1)}, bf16[16,512,64]{1,2,0:T(8,128)(2,1)}, /*index=5*/s32[]{:T(128)}, s32[]{:T(128)}) while((s32[]{:T(128)}, bf16[16,512,64]{1,2,0:T(8,128)(2,1)}, bf16[16,512,64]{1,2,0:T(8,128)(2,1)}, ...), condition=%wide.region_6.7_spmd.clone, body=%wide.region_3.6_spmd.clone.sunk | while | flops 68713984 | bytes 3486801 | solution.py:41
  353.8 1.8 fusion.72
  361.6 1.8 fusion.72
  369.3 1.8 fusion.72
  413.7 2.6 convolution_convert_fusion
  417.6 12.0 %copy.38 = bf16[4096,1024]{1,0:T(8,128)(2,1)} copy(bf16[4096,1024]{0,1:T(8,128)(2,1)} %all-gather.26.cloned.1.call-done) | data formatting | bytes 16777216 | tf_op jit(solution)/shard_map/all_gather | solution.py:95
  429.6 24.5 %fusion.18 = bf16[512,4096]{1,0:T(8,128)(2,1)S(1)} fusion(bf16[1024,4096]{1,0:T(8,128)(2,1)} %all-gather.22.cloned.1.call-done, f32[1024]{0:T(1024)S(1)} %copy-done.8, f32[512]{0:T(512)S(1)} %add_rsqrt_fusion, f32[512]{0:T(512)S(1)} %broadcast_multiply_fusion, f32[512,1024]{1,0:T(8,128)S(1)} %convert_reduce_fusion.1, bf16[512,1024]{1,0:T(8,128)(2,1)S(1)} %copy-done.3), kind=kOutput, calls=%fused_computation.23 | convolution fusion | flops 4434427904 | bytes 15736832 | tf_op jit(solution)/shard_map/dot_general | solution.py:114
  454.2 4.9 fusion.38
  459.1 1.8 convert_reduce_fusion
  460.9 4.3 fusion.37
  465.1 3.6 all-to-all-start
  468.7 40.8 %all-reduce = (f32[]{:T(128)}, f32[]{:T(128)}) all-reduce(f32[]{:T(128)} %get-tuple-element.79, f32[]{:T(128)} %convert_reduce_fusion.3), channel_id=1, replica_groups=mesh['dp'=16,'mp'=2] {'dp','mp'}, use_global_device_ids=true, to_apply=%region_13.15 | all-reduce | flops 2 | bytes 16 | tf_op jit(solution)/shard_map/psum | solution.py:124
  (133 shorter events, 72.3 us)
Async XLA Ops:
  7.2 210.0 %copy-start = (bf16[1,2,256,1024]{3,2,1,0:T(8,128)(2,1)S(1)}, bf16[1,2,256,1024]{3,2,1,0:T(8,128)(2,1)}, u32[]{:S(2)}) copy-start(bf16[1,2,256,1024]{3,2,1,0:T(8,128)(2,1)} %param.25) | copy-start | bytes 3145732
  7.2 209.8 %copy-start.10 = (s32[1,2]{1,0:T(1,128)S(1)}, s32[1,2]{1,0:T(1,128)}, u32[]{:S(2)}) copy-start(s32[1,2]{1,0:T(1,128)} %param.17) | copy-start | bytes 28
  7.2 62.7 %all-gather.16.cloned.1.call-start = ((), (), s32[]{:S(2)}) async-start(), calls=%async_computation.5 | async-start | bytes 1114112 | tf_op jit(solution)/shard_map/all_gather | solution.py:85
  7.9 131.1 %all-gather.12.cloned.1.call-start = ((), (), s32[]{:S(2)}) async-start(), calls=%async_computation.3 | async-start | bytes 3342336 | tf_op jit(solution)/shard_map/all_gather | solution.py:84
  8.7 214.9 %copy-start.9 = (s32[1,2]{1,0:T(1,128)S(1)}, s32[1,2]{1,0:T(1,128)}, u32[]{:S(2)}) copy-start(s32[1,2]{1,0:T(1,128)} %param.16) | copy-start | bytes 28
  8.7 218.1 %copy-start.6 = (bf16[1,512,768]{2,1,0:T(8,128)(2,1)S(1)}, bf16[1,512,768]{2,1,0:T(8,128)(2,1)}, u32[]{:S(2)}) copy-start(bf16[1,512,768]{2,1,0:T(8,128)(2,1)} %param.15) | copy-start | bytes 2359300
  8.7 208.3 %all-gather.24.cloned.1.call-start = ((), (), s32[]{:S(2)}) async-start(), calls=%async_computation.9 | async-start | bytes 4456448 | tf_op jit(solution)/shard_map/all_gather | solution.py:86
  9.4 217.4 %all-gather.10.cloned.1.call-start = ((), (), s32[]{:S(2)}) async-start(), calls=%async_computation.2 | async-start | bytes 2359296 | tf_op jit(solution)/shard_map/all_gather | solution.py:89
  59.8 180.2 %all-gather.18.cloned.1.call-start = ((), (), s32[]{:S(2)}) async-start(), calls=%async_computation.6 | async-start | bytes 3145728 | tf_op jit(solution)/shard_map/all_gather | solution.py:94
  69.9 250.0 %all-gather.20.cloned.1.call-start = ((), (), s32[]{:S(2)}) async-start(), calls=%async_computation.7 | async-start | bytes 4456448 | tf_op jit(solution)/shard_map/all_gather | solution.py:81
  70.5 266.3 %all-gather.14.cloned.1.call-start = ((), (), s32[]{:S(2)}) async-start(), calls=%async_computation.4 | async-start | bytes 9437184 | tf_op jit(solution)/shard_map/all_gather | solution.py:92
  139.0 278.5 %all-gather.26.cloned.1.call-start = ((), (), s32[]{:S(2)}) async-start(), calls=%async_computation.10 | async-start | bytes 12582912 | tf_op jit(solution)/shard_map/all_gather | solution.py:95
  218.9 117.9 %copy-start.7 = (f32[1024]{0:T(1024)S(1)}, f32[1024]{0:T(1024)}, u32[]{:S(2)}) copy-start(f32[1024]{0:T(1024)} %param.23) | copy-start | bytes 12292
  218.9 242.0 %all-to-all-start.1 = ((bf16[2,256,1024]{2,1,0:T(8,128)(2,1)}), bf16[2,256,1024]{2,1,0:T(8,128)(2,1)}, u32[]{:S(2)}, u32[]{:S(2)}) async-start(bf16[2,256,1024]{2,1,0:T(8,128)(2,1)} %broadcast_select_fusion), calls=%async_computation.1 | async-start | bytes 2097152 | tf_op jit(solution)/shard_map/all_to_all | solution.py:101
  223.5 206.1 %all-gather.22.cloned.1.call-start = ((), (), s32[]{:S(2)}) async-start(), calls=%async_computation.8 | async-start | bytes 12582912 | tf_op jit(solution)/shard_map/all_gather | solution.py:90
  229.3 115.8 %copy-start.2 = (bf16[512,1024]{1,0:T(8,128)(2,1)}, bf16[512,1024]{1,0:T(8,128)(2,1)S(1)}, u32[]{:S(2)}) copy-start(bf16[512,1024]{1,0:T(8,128)(2,1)S(1)} %get-tuple-element.84) | copy-start | bytes 3145732
  351.5 62.2 %copy-start.5 = (bf16[1024,1024]{1,0:T(8,128)(2,1)S(1)}, bf16[1024,1024]{1,0:T(8,128)(2,1)}, u32[]{:S(2)}) copy-start(bf16[1024,1024]{1,0:T(8,128)(2,1)} %copy.36) | copy-start | bytes 6291460
  413.7 3.1 copy-start.3
  417.5 12.1 %copy-start.8 = (f32[1024]{0:T(1024)S(1)}, f32[1024]{0:T(1024)}, u32[]{:S(2)}) copy-start(f32[1024]{0:T(1024)} %param.24) | copy-start | bytes 12292
  429.6 24.5 %copy-start.4 = (bf16[4096,1024]{1,0:T(8,128)(2,1)S(1)}, bf16[4096,1024]{1,0:T(8,128)(2,1)}, u32[]{:S(2)}) copy-start(bf16[4096,1024]{1,0:T(8,128)(2,1)} %copy.38) | copy-start | bytes 25165828
  454.1 58.4 %copy-start.1 = (bf16[1,2,256,1024]{3,2,1,0:T(8,128)(2,1)S(1)}, bf16[1,2,256,1024]{3,2,1,0:T(8,128)(2,1)}, u32[]{:S(2)}) copy-start(bf16[1,2,256,1024]{3,2,1,0:T(8,128)(2,1)} %param.25) | copy-start | bytes 3145732
  465.1 45.7 %all-to-all-start = ((bf16[2,256,1024]{2,1,0:T(8,128)(2,1)}), bf16[2,256,1024]{2,1,0:T(8,128)(2,1)S(1)}, u32[]{:S(2)}, u32[]{:S(2)}) async-start(bf16[2,256,1024]{2,1,0:T(8,128)(2,1)} %bitcast.81), calls=%async_computation | async-start | bytes 2097152 | tf_op jit(solution)/shard_map/all_to_all | solution.py:122
Sparse Core Ops, SparseCore 0:
  10.8 59.0 all-gather.15
  72.6 66.3 all-gather.11
  141.8 75.1 all-gather.23
  218.4 8.3 all-gather.9
  228.2 11.7 all-gather.17
  242.6 77.2 all-gather.19
  321.4 15.3 all-gather.13
  338.4 21.0 all-gather.25
  361.0 21.0 all-gather.21
where the time goes:
time: 523 us; the launch traced here: 520 us
  waiting for transfers between devices  263 us (50%)
  matrix products  91.2 us (17%)
  blocking collectives  91.1 us (17%)
  other arithmetic  28.6 us (5%)
  local copies, waits for them, and re-layouts  21.3 us (4%)
  between operations  16.5 us (3%)
  starting transfers between devices  8.51 us (2%)
    all_gather x1, waiting for transfers between devices, on_device(): lax.all_gather(w_down, 'dp', axis=1, tiled=True)  77.9 us
    all_gather x1, waiting for transfers between devices, on_device(): lax.all_gather(w_up, 'dp', axis=0, tiled=True)  76 us
    all_gather x1, waiting for transfers between devices, on_device(): lax.all_gather(w_qkv, 'dp', axis=1, tiled=True)  68.5 us
    all_gather x1, blocking collectives, on_device(): lax.all_gather(embed_weight, 'dp', axis=0, tiled=True)  50.3 us
    psum x1, blocking collectives, on_device(): total_squares, total_number = lax.psum((squares, number), ('dp', 'mp'))  40.8 us
    dot_general x16, matrix products, one_head(): jnp.dot(expo.astype(jnp.bfloat16), value_part, preferred_element_type=jnp...  28.3 us
    dot_general x1, matrix products, on_device(): jnp.dot(normed_two, up_whole, preferred_element_type=jnp.float32)  24.5 us
    dot_general x16, matrix products, one_head(): jnp.einsum('qd,kd->qk', query_part, key_part, preferred_element_type=jnp....  20.1 us
  transfers between devices with their start and end apart: 11, of which 7 were waited for; matrix products, arithmetic and copies ran while one was open for 26% of the time, Pallas kernels for 0%

commit v1 on v0

v1 whole, which is shorter than its diff:
```python
import functools

import jax
import jax.numpy as jnp
from jax import lax
from jax.experimental import pallas as pl
from jax.experimental.pallas import tpu as pltpu
from jax.sharding import PartitionSpec as P

HEAD = 64
TILE = 16
Z, Y, X = 0, 1, 2
MIB = 1 << 20
POS_Z, POS_Y, POS_X, POS_M, POS_LEN, POS_STEP = 0, 1, 2, 3, 4, 6


def ring_dims(count):
    nz = 4 if count % 4 == 0 else 1
    nx = 1
    while nx * nx < count // nz:
        nx *= 2
    ny = count // nz // nx
    return (nz, ny, nx) if nz * ny * nx == count else (1, 1, count)


def shift(value, dims, axis):
    pairs = []
    for z in range(dims[0]):
        for y in range(dims[1]):
            for x in range(dims[2]):
                to = [z, y, x]
                to[axis] = (to[axis] + 1) % dims[axis]
                pairs.append(
                    ((z * dims[1] + y) * dims[2] + x, (to[0] * dims[1] + to[1]) * dims[2] + to[2])
                )
    return lax.ppermute(value, "dp", pairs)


class Chunk:
    def __init__(self, array, slots, half):
        self.array, self.slots, self.half = array, slots, half
        self.rows = array.shape[0] // len(slots)

    def moved(self, array, axis, by=1):
        slots = [tuple(v + by * (i == axis) for i, v in enumerate(s)) for s in self.slots]
        return Chunk(array, slots, self.half)

    def part(self, first, last):
        return Chunk(
            self.array[first * self.rows : last * self.rows], self.slots[first:last], self.half
        )


def joined(chunks):
    if len(chunks) == 1:
        return chunks[0]
    return Chunk(
        jnp.concatenate([c.array for c in chunks], 0), sum((c.slots for c in chunks), []), chunks[0].half
    )


def together(*lists):
    flat = [c for chunks in lists for c in chunks]
    arrays = lax.optimization_barrier(tuple(c.array for c in flat))
    for c, a in zip(flat, arrays, strict=True):
        c.array = a


def step(chunk, dims, axis):
    return chunk.moved(shift(chunk.array, dims, axis), axis)


def swap_columns(value):
    return lax.ppermute(value, "mp", [(0, 1), (1, 0)])


def pair_gather(first, up, down, cut, dims):
    nz = dims[0]
    half = up.shape[0] // 2
    low = nz // 2
    here = [(0, 0, 0)]
    blocks_a = [Chunk(first[:cut], here, 0)]
    blocks_b = [Chunk(first[cut:], here, 1)]

    z_now = shift(first, dims, Z)
    side_a = jnp.concatenate([up[:half], down[:half]], 0)
    side_b = jnp.concatenate([up[half:], down[half:]], 0)
    from_x = shift(side_a, dims, X)
    from_y = shift(side_b, dims, Y)
    z_now, from_x, from_y = lax.optimization_barrier((z_now, from_x, from_y))

    def whole(own, k):
        rows = slice(k * half, (k + 1) * half)
        return (
            [Chunk(own[:half], here, 0), Chunk(from_x[rows], [(0, 0, 1)], 0)],
            [Chunk(own[half:], here, 1), Chunk(from_y[rows], [(0, 1, 0)], 1)],
        )

    up_a, up_b = (joined(c) for c in whole(up, 0))
    down_a, down_b = (joined(c) for c in whole(down, 1))

    def add_z(value, far):
        blocks_a.append(Chunk(value[:cut], [(far, 0, 0)], 0))
        blocks_b.append(Chunk(value[cut:], [(far, 0, 0)], 1))

    add_z(z_now, 1)
    a1, b1 = joined(blocks_a[:low]), joined(blocks_b[:low])
    z_next = shift(z_now, dims, Z)
    a1x, b1y = step(a1, dims, X), step(b1, dims, Y)
    z_now, a1x.array, b1y.array, up_a.array, up_b.array, down_a.array, down_b.array = (
        lax.optimization_barrier(
            (z_next, a1x.array, b1y.array, up_a.array, up_b.array, down_a.array, down_b.array)
        )
    )
    add_z(z_now, 2)
    a1, b1 = joined([a1, a1x]), joined([b1, b1y])
    z_next = shift(z_now, dims, Z)
    a1y, b1x = step(a1, dims, Y), step(b1, dims, X)
    z_now, a1y.array, b1x.array = lax.optimization_barrier((z_next, a1y.array, b1x.array))
    add_z(z_now, 3)
    a2, b2 = joined(blocks_a[low:]), joined(blocks_b[low:])
    up_z = [joined([up_a, up_b])]
    down_z = [joined([down_a, down_b])]
    up_z.append(step(up_z[-1], dims, Z))
    a2x, b2y = step(a2, dims, X), step(b2, dims, Y)
    together([up_z[-1], a2x, b2y])
    a2, b2 = joined([a2, a2x]), joined([b2, b2y])
    up_z.append(step(up_z[-1], dims, Z))
    a2y, b2x = step(a2, dims, Y), step(b2, dims, X)
    together([up_z[-1], a2y, b2x])
    first_parts = [a1, a1y, b1, b1x, a2, a2y, b2, b2x]

    def ends(blocks):
        a = joined([c.part(0, 2) for c in blocks])
        b = joined([c.part(2, 4) for c in blocks])
        b.half = 1
        return a, b

    ua1, ub1 = ends(up_z[:low])
    up_z.append(step(up_z[-1], dims, Z))
    ua1y, ub1x = step(ua1, dims, Y), step(ub1, dims, X)
    together([up_z[-1], ua1y, ub1x])
    ua2, ub2 = ends(up_z[low:])
    down_z.append(step(down_z[-1], dims, Z))
    ua2y, ub2x = step(ua2, dims, Y), step(ub2, dims, X)
    together([down_z[-1], ua2y, ub2x])
    up_parts = [ua1, ua1y, ub1, ub1x, ua2, ua2y, ub2, ub2x]
    da1, db1 = ends(down_z[:low])
    down_z.append(step(down_z[-1], dims, Z))
    da1y, db1x = step(da1, dims, Y), step(db1, dims, X)
    together([down_z[-1], da1y, db1x])
    down_z.append(step(down_z[-1], dims, Z))
    together([down_z[-1]])
    da2, db2 = ends(down_z[low:])
    da2y, db2x = step(da2, dims, Y), step(db2, dims, X)
    return first_parts, up_parts, [[da1, da1y, db1, db1x], [da2, da2y, db2, db2x]]


def pieces_of(chunks, spans, segment):
    found = []
    for number, chunk in enumerate(chunks):
        first, last = spans[chunk.half]
        low, high = max(first, segment[0]), min(last, segment[1])
        if low < high:
            for i, slot in enumerate(chunk.slots):
                found.append((number, i * chunk.rows + low - first, high - low, slot, low - segment[0]))
    return found


def source(pos, slot, dims, z_first=None):
    z, y, x = (lax.rem(pos[i] - slot[i] + dims[i], dims[i]) for i in (0, 1, 2))
    if z_first is not None:
        z = slot[0] - z_first
    return (z * dims[1] + y) * dims[2] + x


def copies(pos, dims, refs, pieces, into, block, sems, first_sem=0, z_first=None):
    made = []
    for i, (number, row, rows, slot, offset) in enumerate(pieces):
        to = offset
        if slot is not None:
            to = pl.multiple_of(source(pos, slot, dims, z_first) * block + offset, TILE)
        made.append(
            pltpu.make_async_copy(
                refs[number].at[pl.ds(row, rows)], into.at[pl.ds(to, rows)], sems.at[first_sem + i]
            )
        )
    return made


def nt_dot(left, right):
    return lax.dot_general(left, right, (((1,), (1,)), ((), ())), preferred_element_type=jnp.float32)


def dot(left, right):
    return jnp.dot(left, right, preferred_element_type=jnp.float32)


def any_spec():
    return pl.BlockSpec(memory_space=pl.ANY)


def vmem_spec():
    return pl.BlockSpec(memory_space=pltpu.VMEM)


def smem_spec():
    return pl.BlockSpec(memory_space=pltpu.SMEM)


def limits(mib):
    return pltpu.CompilerParams(vmem_limit_bytes=mib * MIB)


def cost(flops, moved, exps=0):
    return pl.CostEstimate(flops=flops, bytes_accessed=moved, transcendentals=exps)


def embed_kernel(n, dims, pieces, block, pos, mine, other, *rest):
    refs, (tokens, weight, sems) = rest[:n], rest[n:]
    made = copies(pos, dims, refs, pieces, weight, block, sems)
    for c in made:
        c.start()
    for c in made:
        c.wait()
    tokens[0] = dot(mine[...], weight[...]).astype(tokens.dtype)
    tokens[1] = dot(other[...], weight[...]).astype(tokens.dtype)


def embed(pos, dims, mine, other, chunks, pieces, block, columns):
    patches, pixels = mine.shape
    n = len(chunks)
    return pl.pallas_call(
        functools.partial(embed_kernel, n, dims, pieces, block),
        out_shape=jax.ShapeDtypeStruct((2, patches, columns), mine.dtype),
        in_specs=[smem_spec(), vmem_spec(), vmem_spec()] + [any_spec()] * n,
        out_specs=vmem_spec(),
        scratch_shapes=[
            pltpu.VMEM((pixels, columns), mine.dtype),
            pltpu.SemaphoreType.DMA((len(pieces),)),
        ],
        compiler_params=limits(16),
        cost_estimate=cost(4 * patches * pixels * columns, 4 * MIB),
        name="embed",
    )(pos, mine, other, *chunks)


def attention_kernel(n, dims, pieces, block, pos, mine, recv, gain, *rest):
    refs = rest[:n]
    keep, send, wq, wk, wv, wo, normed, q, k, v, mixed, sems = rest[n:]
    weights = (wq, wk, wv, wo)
    made, at = [], 0
    for weight, part in zip(weights, pieces, strict=True):
        made.append(copies(pos, dims, refs, part, weight, block, sems, at))
        at += len(part)
    for group in made:
        for c in group:
            c.start()
    m = pos[POS_M]
    patches, columns = mine.shape[1:]
    rows_own = patches // 2
    width = 2 * columns
    for i in range(2):
        low = mine[i].astype(jnp.float32)
        high = recv[1 - i].astype(jnp.float32)
        average = (
            jnp.sum(low, axis=-1, keepdims=True) + jnp.sum(high, axis=-1, keepdims=True)
        ) / width
        low, high = low - average, high - average
        spread = (
            jnp.sum(low * low, axis=-1, keepdims=True) + jnp.sum(high * high, axis=-1, keepdims=True)
        ) / width
        scale = lax.rsqrt(spread + 1e-06)
        normed[i, 0] = (low * scale * gain[0:1]).astype(normed.dtype)
        normed[i, 1] = (high * scale * gain[1:2]).astype(normed.dtype)
    here = pl.ds(pl.multiple_of(m * columns, columns), columns)
    there = pl.ds(pl.multiple_of((1 - m) * columns, columns), columns)
    for weight, group, result, factor in zip(
        weights[:3], made[:3], (q, k, v), (HEAD**-0.5, 1.0, 1.0), strict=True
    ):
        for c in group:
            c.wait()
        for i in range(2):
            value = dot(normed[i, 0], weight[here, :]) + dot(normed[i, 1], weight[there, :])
            if factor != 1.0:
                value = value * factor
            result[i] = value.astype(result.dtype)
    pair = 2 * HEAD
    key_ids = lax.broadcasted_iota(jnp.int32, (1, patches), 1)
    lane = lax.broadcasted_iota(jnp.int32, (patches, pair), 1)
    first = lane < HEAD
    for i in range(2):
        masked = jnp.where(key_ids < pos[POS_LEN + i], 0.0, -1e30).astype(jnp.float32)
        for h in range(columns // pair):
            cut = slice(h * pair, (h + 1) * pair)
            q_pair, k_pair, v_pair = q[i, :, cut], k[i, :, cut], v[i, :, cut]
            found = []
            for own in (first, jnp.logical_not(first)):
                scores = nt_dot(q_pair, jnp.where(own, k_pair, jnp.zeros_like(k_pair))) + masked
                expo = jnp.exp(scores - jnp.max(scores, axis=-1, keepdims=True))
                value = dot(
                    expo.astype(v_pair.dtype), jnp.where(own, v_pair, jnp.ones_like(v_pair))
                )
                found.append(value / pltpu.roll(value, HEAD, 1))
            mixed[i, :, cut] = jnp.where(first, found[0], found[1]).astype(mixed.dtype)
    for c in made[3]:
        c.wait()
    own_rows = pl.ds(pl.multiple_of(m * rows_own, rows_own), rows_own)
    far_rows = pl.ds(pl.multiple_of((1 - m) * rows_own, rows_own), rows_own)
    for i in range(2):
        keep[i] = nt_dot(mixed[i, own_rows, :], wo[...]).astype(keep.dtype)
        send[i] = nt_dot(mixed[i, far_rows, :], wo[...]).astype(send.dtype)


def attention(pos, dims, mine, recv, gain, chunks, pieces, block, width):
    _, patches, columns = mine.shape
    n = len(chunks)
    kind = mine.dtype
    out = jax.ShapeDtypeStruct((2, patches // 2, width), kind)
    weight = pltpu.VMEM((width, columns), kind)
    whole = pltpu.VMEM((2, patches, columns), kind)
    return pl.pallas_call(
        functools.partial(attention_kernel, n, dims, pieces, block),
        out_shape=(out, out),
        in_specs=[smem_spec(), vmem_spec(), vmem_spec(), vmem_spec()] + [any_spec()] * n,
        out_specs=(vmem_spec(), vmem_spec()),
        scratch_shapes=[weight] * 4
        + [pltpu.VMEM((2, 2, patches, columns), kind)]
        + [whole] * 4
        + [pltpu.SemaphoreType.DMA((sum(len(p) for p in pieces),))],
        compiler_params=limits(32),
        cost_estimate=cost(
            2 * 2 * patches * width * columns * 4 + 8 * patches * patches * columns,
            10 * MIB,
            2 * patches * patches * columns // HEAD,
        ),
        name="attention",
    )(pos, mine, recv, gain, *chunks)


def residual_kernel(pos, mine, recv, keep, came, gain, residual, normed):
    m = pos[POS_M]
    columns = mine.shape[2]
    rows = keep.shape[1]
    width = 2 * columns
    own_rows = pl.ds(pl.multiple_of(m * rows, rows), rows)
    here = pl.ds(pl.multiple_of(m * columns, columns), columns)
    there = pl.ds(pl.multiple_of((1 - m) * columns, columns), columns)
    for i in range(2):
        parts = []
        for tokens, at in ((mine[i, own_rows, :], here), (recv[1 - i, own_rows, :], there)):
            parts.append(
                tokens.astype(jnp.float32)
                + (keep[i, :, at].astype(jnp.float32) + came[1 - i, :, at].astype(jnp.float32))
            )
            residual[i, :, at] = parts[-1]
        average = sum(jnp.sum(v, axis=-1, keepdims=True) for v in parts) / width
        parts = [v - average for v in parts]
        spread = sum(jnp.sum(v * v, axis=-1, keepdims=True) for v in parts) / width
        scale = lax.rsqrt(spread + 1e-06)
        for v, at in zip(parts, (here, there), strict=True):
            normed[i, :, at] = (v * scale * gain[0:1, at]).astype(normed.dtype)


def residual_and_norm(pos, mine, recv, keep, came, gain):
    return pl.pallas_call(
        residual_kernel,
        out_shape=(
            jax.ShapeDtypeStruct(keep.shape, jnp.float32),
            jax.ShapeDtypeStruct(keep.shape, keep.dtype),
        ),
        in_specs=[smem_spec()] + [vmem_spec()] * 5,
        out_specs=(vmem_spec(), vmem_spec()),
        compiler_params=limits(16),
        cost_estimate=cost(10 * keep.size, 10 * MIB),
        name="residual",
    )(pos, mine, recv, keep, came, gain)


def gelu(x):
    t = 1.0 / (1.0 + (0.3275911 * 0.7071067811865476) * jnp.abs(x))
    poly = 0.5 * 1.061405429
    for a in (-1.453152027, 1.421413741, -0.284496736, 0.254829592):
        poly = poly * t + 0.5 * a
    tail = poly * t * jnp.exp(-0.5 * (x * x))
    return x * jnp.where(x < 0.0, tail, 1.0 - tail)


def up_kernel(n, dims, pieces, block, pos, own, came, *rest):
    refs, (hidden, weight, sems) = rest[:n], rest[n:]
    made = copies(pos, dims, refs, pieces, weight, block, sems)
    for c in made:
        c.start()
    for c in made:
        c.wait()
    tile = 512
    for i in range(2):
        for j in range(hidden.shape[-1] // tile):
            at = slice(j * tile, (j + 1) * tile)
            for k, side in enumerate((own[i], came[1 - i])):
                hidden[k, i, :, at] = gelu(dot(side, weight[:, at])).astype(hidden.dtype)


def up_layer(pos, dims, own, came, chunks, pieces, block, units):
    _, rows, width = own.shape
    n = len(chunks)
    return pl.pallas_call(
        functools.partial(up_kernel, n, dims, pieces, block),
        out_shape=jax.ShapeDtypeStruct((2, 2, rows, units), own.dtype),
        in_specs=[smem_spec(), vmem_spec(), vmem_spec()] + [any_spec()] * n,
        out_specs=vmem_spec(),
        scratch_shapes=[
            pltpu.VMEM((width, units), own.dtype),
            pltpu.SemaphoreType.DMA((len(pieces),)),
        ],
        compiler_params=limits(24),
        cost_estimate=cost(8 * rows * width * units, 10 * MIB, 4 * rows * units),
        name="up",
    )(pos, own, came, *chunks)


def down_kernel(n, dims, pieces, block, z_first, pos, hidden, *rest):
    refs, (keep, send, weight, sems) = rest[:n], rest[n:]
    made = copies(pos, dims, refs, pieces, weight, block, sems, 0, z_first)
    for c in made:
        c.start()
    for c in made:
        c.wait()
    for i in range(2):
        for k, result in enumerate((keep, send)):
            result[i] = nt_dot(hidden[k, i], weight[...]).astype(result.dtype)


def down_layer(pos, dims, hidden, chunks, pieces, block, z_first, columns):
    _, _, rows, units = hidden.shape
    n = len(chunks)
    out = jax.ShapeDtypeStruct((2, rows, columns), hidden.dtype)
    return pl.pallas_call(
        functools.partial(down_kernel, n, dims, pieces, block, z_first),
        out_shape=(out, out),
        in_specs=[smem_spec(), vmem_spec()] + [any_spec()] * n,
        out_specs=(vmem_spec(), vmem_spec()),
        scratch_shapes=[
            pltpu.VMEM((columns, units), hidden.dtype),
            pltpu.SemaphoreType.DMA((len(pieces),)),
        ],
        compiler_params=limits(24),
        cost_estimate=cost(8 * rows * columns * units, 8 * MIB),
        name="down",
    )(pos, hidden, *chunks)


def output_kernel(n, nz, starts, pos, residual, targets, *rest):
    parts, (encoded, squares) = rest[:n], rest[n:]
    m = pos[POS_M]
    rows = residual.shape[1]
    total = jnp.zeros((), jnp.float32)
    row_ids = m * rows + lax.broadcasted_iota(jnp.int32, (rows, 1), 0)
    for i in range(2):
        s = pos[POS_STEP] if i == 0 else 1 - pos[POS_STEP]
        usable = row_ids < pos[POS_LEN + i]
        sums = jnp.zeros((rows, 1), jnp.float32)
        for j, spots in enumerate(starts):
            keep, came = parts[2 * j], parts[2 * j + 1]
            size = keep.shape[2] // len(spots)
            for b, back in enumerate(spots):
                at = slice(b * size, (b + 1) * size)
                if back is None:
                    place = pl.ds(0, size)
                else:
                    begin = lax.rem(pos[POS_Z] - back + nz, nz) * size
                    place = pl.ds(pl.multiple_of(begin, size), size)
                value = residual[i, :, place] + (
                    keep[i, :, at].astype(jnp.float32) + came[1 - i, :, at].astype(jnp.float32)
                )
                encoded[s, :, place] = value.astype(encoded.dtype)
                misfit = value - targets[s, :, place].astype(jnp.float32)
                sums = sums + jnp.sum(misfit * misfit, axis=-1, keepdims=True)
        total = total + jnp.sum(jnp.where(usable, sums, 0.0))
    squares[...] = jnp.full(squares.shape, total, jnp.float32)


def output_layer(pos, residual, targets, nz, starts, parts):
    return pl.pallas_call(
        functools.partial(output_kernel, len(parts), nz, starts),
        out_shape=(
            jax.ShapeDtypeStruct(residual.shape, targets.dtype),
            jax.ShapeDtypeStruct((8, 128), jnp.float32),
        ),
        in_specs=[smem_spec()] + [vmem_spec()] * (2 + len(parts)),
        out_specs=(vmem_spec(), vmem_spec()),
        compiler_params=limits(24),
        cost_estimate=cost(8 * residual.size, 8 * MIB),
        name="output",
    )(pos, residual, targets, *parts)


def on_device(
    pixels, counts, owner, embed_weight, w_qkv, w_out, w_up, w_down, ln1_gain, ln2_gain, targets
):
    picture = pixels[0]
    devices, cores = lax.axis_size("dp"), lax.axis_size("mp")
    assert cores == 2
    index, m = lax.axis_index("dp"), lax.axis_index("mp")
    dims = ring_dims(devices)
    width = ln1_gain.shape[0]
    columns = width // cores
    lengths, order = counts[0], owner[0]
    length_mine = jnp.where(m == 0, lengths[0], lengths[1])
    length_other = jnp.where(m == 0, lengths[1], lengths[0])
    step_mine = jnp.where(order[0] == m, 0, 1)
    pos = jnp.stack(
        [
            index // (dims[1] * dims[2]),
            index // dims[2] % dims[1],
            index % dims[2],
            m,
            length_mine,
            length_other,
            step_mine,
            jnp.zeros_like(m),
        ]
    ).astype(jnp.int32)
    gain_halves = ln1_gain.reshape(cores, columns)
    gain_one = jnp.where(m == 0, gain_halves, gain_halves[::-1])

    shards = [embed_weight, w_qkv[0], w_qkv[1], w_qkv[2], w_out.T]
    up, down = w_up, w_down.T
    block, block_e = up.shape[0], embed_weight.shape[0]
    total = sum(s.shape[0] for s in shards)
    cut = total // 2 // TILE * TILE
    in_slots = (
        dims[0] == 4
        and dims[1] == 2
        and dims[2] == 2
        and block % (2 * TILE) == 0
        and block_e % TILE == 0
    )
    other_picture = swap_columns(picture)
    if in_slots:
        first_parts, up_parts, down_parts = pair_gather(
            jnp.concatenate(shards, 0), up, down, cut, dims
        )
        spans = ((0, cut), (cut, total))
        halves = ((0, block // 2), (block // 2, block))
        bounds = [0]
        for s in shards:
            bounds.append(bounds[-1] + s.shape[0])
        first_pieces = [
            pieces_of(first_parts, spans, (bounds[i], bounds[i + 1])) for i in range(len(shards))
        ]
        up_pieces = pieces_of(up_parts, halves, (0, block))
        down_pieces = [pieces_of(part, halves, (0, block)) for part in down_parts]
        starts = [sorted({p[3][0] for p in pieces}) for pieces in down_pieces]
    else:
        gathered = [lax.all_gather(s, "dp", axis=0, tiled=True) for s in (*shards, up, down)]
        whole = [Chunk(g, [None], 0) for g in gathered]
        first_parts, up_parts, down_parts = whole[:5], whole[5:6], [whole[6:]]
        first_pieces = [[(i, 0, c.rows, None, 0)] for i, c in enumerate(first_parts)]
        up_pieces = [(0, 0, up_parts[0].rows, None, 0)]
        down_pieces = [[(0, 0, down_parts[0][0].rows, None, 0)]]
        starts = [[None]]

    first_arrays = [c.array for c in first_parts]
    embed_at = sorted({p[0] for p in first_pieces[0]})
    embed_pieces = [(embed_at.index(p[0]), *p[1:]) for p in first_pieces[0]]
    mine = embed(
        pos, dims, picture, other_picture, [first_arrays[i] for i in embed_at], embed_pieces, block_e, columns
    )
    recv = swap_columns(mine)
    keep, send = attention(
        pos, dims, mine, recv, gain_one, first_arrays, first_pieces[1:], block, width
    )
    came = swap_columns(send)
    residual, normed = residual_and_norm(
        pos, mine, recv, keep, came, ln2_gain.reshape(1, width)
    )
    normed_came = swap_columns(normed)
    hidden = up_layer(
        pos, dims, normed, normed_came, [c.array for c in up_parts], up_pieces, block, up.shape[1]
    )
    finals = []
    for part, pieces, spots in zip(down_parts, down_pieces, starts, strict=True):
        kept, sent = down_layer(
            pos, dims, hidden, [c.array for c in part], pieces, block, spots[0], width // len(down_parts)
        )
        finals += [kept, swap_columns(sent)]
    encoded, squares = output_layer(pos, residual, targets[0], dims[0], starts, finals)
    number = jnp.sum(lengths).astype(jnp.float32) / cores
    mine_sums = jnp.stack([squares[0, 0], number])
    sums = lax.all_to_all(
        jnp.broadcast_to(mine_sums[None, None, :], (devices * cores, 1, 2)), ("dp", "mp"), 0, 0, tiled=True
    )
    total_squares, total_number = jnp.sum(sums, axis=(0, 1))
    return (encoded[None], total_squares / (width * total_number))


def solution(mesh):
    in_specs = (
        P(("dp", "mp"), None, None),
        P("dp", None),
        P("dp", None),
        P("dp", "mp"),
        P(None, "dp", "mp"),
        P("mp", "dp"),
        P("dp", "mp"),
        P("mp", "dp"),
        P(),
        P(),
        P("dp", None, "mp", None),
    )
    out_specs = (P("dp", None, "mp", None), P())
    return jax.shard_map(
        on_device, mesh=mesh, in_specs=in_specs, out_specs=out_specs, check_vma=False
    )
```

time: 523 us -> 216 us (0.41)
  waiting for transfers between devices: 263 us -> 73.2 us
  matrix products: 91.2 us -> 0 us
  blocking collectives: 91.1 us -> 9.43 us
  Pallas kernels: 0 us -> 55.8 us
  starting transfers between devices: 8.51 us -> 34.5 us
  other arithmetic: 28.6 us -> 9.85 us
  between operations: 16.5 us -> 7.11 us
    all_gather x9 -> x0, waiting for transfers between devices: 260 us -> none  [the longest x1 77.9 us: on_device(): lax.all_gather(w_down, 'dp', axis=1, tiled=True)]
    dot_general x37 -> x0, matrix products: 91.2 us -> none  [the longest x16 28.3 us: one_head(): jnp.dot(expo.astype(jnp.bfloat16), value_part, preferred_element_type=jnp...]
    ppermute x0 -> x33, waiting for transfers between devices: none -> 73.2 us  [the longest x27 72.7 us: shift(): return lax.ppermute(value, 'dp', pairs)]
    pallas_call x0 -> x7, Pallas kernels: none -> 55.8 us  [the longest x1 19.6 us: attention(): pl.pallas_call(functools.partial(attention_kernel, n, dims, pieces, block...]
    all_gather x1 -> x0, blocking collectives: 50.3 us -> none  [on_device(): lax.all_gather(embed_weight, 'dp', axis=0, tiled=True)]
    psum x1 -> x0, blocking collectives: 40.8 us -> none  [on_device(): total_squares, total_number = lax.psum((squares, number), ('dp', 'mp'))]
    ppermute x0 -> x33, starting transfers between devices: none -> 34.5 us  [the longest x27 33.8 us: shift(): return lax.ppermute(value, 'dp', pairs)]
    unnamed x22 -> x100, local copies, waits for them, and re-layouts: 0.05 us -> 18.3 us
  transfers between devices with their start and end apart: 11 -> 33, of which waited for: 7 -> 18; matrix products, arithmetic and copies ran while one was open for 26% -> 7% of each run, Pallas kernels for 0% -> 25%
where the time goes in v1:
time: 216 us; the launch traced here: 215 us
  waiting for transfers between devices  73.2 us (34%)
  Pallas kernels  55.8 us (26%)
  starting transfers between devices  34.5 us (16%)
  local copies, waits for them, and re-layouts  25.3 us (12%)
  other arithmetic  9.85 us (5%)
  blocking collectives  9.43 us (4%)
  between operations  7.11 us (3%)
    ppermute x27, waiting for transfers between devices, shift(): return lax.ppermute(value, 'dp', pairs)  72.7 us
    ppermute x27, starting transfers between devices, shift(): return lax.ppermute(value, 'dp', pairs)  33.8 us
    pallas_call x1, Pallas kernels, attention(): pl.pallas_call(functools.partial(attention_kernel, n, dims, pieces, block...  19.6 us
    unnamed x100, local copies, waits for them, and re-layouts  18.3 us
    pallas_call x1, Pallas kernels, up_layer(): pl.pallas_call(functools.partial(up_kernel, n, dims, pieces, block), out_...  15.4 us
    pallas_call x2, Pallas kernels, down_layer(): pl.pallas_call(functools.partial(down_kernel, n, dims, pieces, block, z_f...  13.5 us
    all_to_all x1, blocking collectives, on_device(): lax.all_to_all(jnp.broadcast_to(mine_sums[None, None, :], (devices * core...  9.43 us
    concatenate x20, other arithmetic, joined(): jnp.concatenate([c.array for c in chunks], 0)  8.42 us
  transfers between devices with their start and end apart: 33, of which 18 were waited for; matrix products, arithmetic and copies ran while one was open for 7% of the time, Pallas kernels for 25%

profile of v1, /device:TPU:0, one launch (start us, length us, event | category | flops | bytes accessed | tf_op | source)
XLA Modules:
  0.0 215.1 jit_solution(15391668177022341176)
XLA Ops:
  4.9 3.0 %collective-permute-start.1 = (bf16[304,512]{1,0:T(8,128)(2,1)S(1)}, bf16[304,512]{1,0:T(8,128)(2,1)S(1)}, u32[]{:S(2)}, u32[]{:S(2)}) collective-permute-start(bf16[304,512]{1,0:T(8,128)(2,1)S(1)} %constant_dynamic-update-slice_fusion), channel_id=1, source_target_pairs={{0,8},{2,10},{4,12},{6,14},{8,16},{10,18},{12,20},{14,22},{16,24},... | collective-permute-start | bytes 933896 | tf_op jit(solution)/shard_map/ppermute | solution.py:36
  12.3 4.6 %collective-permute-done.2 = bf16[64,2048]{1,0:T(8,128)(2,1)S(1)} collective-permute-done((bf16[64,2048]{1,0:T(8,128)(2,1)S(1)}, bf16[64,2048]{1,0:T(8,128)(2,1)S(1)}, u32[]{:S(2)}, u32[]{:S(2)}) %collective-permute-start.2) | collective-permute-done | bytes 262176 | tf_op jit(solution)/shard_map/ppermute | solution.py:36
  22.2 4.7 %collective-permute-done.5 = bf16[288,512]{1,0:T(8,128)(2,1)S(1)} collective-permute-done((bf16[288,512]{1,0:T(8,128)(2,1)S(1)}, bf16[288,512]{1,0:T(8,128)(2,1)S(1)}, u32[]{:S(2)}, u32[]{:S(2)}) %collective-permute-start.5) | collective-permute-done | bytes 294944 | tf_op jit(solution)/shard_map/ppermute | solution.py:36
  34.1 6.8 %collective-permute-done.7 = bf16[304,512]{1,0:T(8,128)(2,1)S(1)} collective-permute-done((bf16[304,512]{1,0:T(8,128)(2,1)S(1)}, bf16[304,512]{1,0:T(8,128)(2,1)S(1)}, u32[]{:S(2)}, u32[]{:S(2)}) %collective-permute-start.7) | collective-permute-done | bytes 311328 | tf_op jit(solution)/shard_map/ppermute | solution.py:36
  43.8 1.6 pad_maximum_fusion.21
  57.1 2.3 %collective-permute-start.14 = (bf16[576,512]{1,0:T(8,128)(2,1)S(1)}, bf16[576,512]{1,0:T(8,128)(2,1)S(1)}, u32[]{:S(2)}, u32[]{:S(2)}) collective-permute-start(bf16[576,512]{1,0:T(8,128)(2,1)S(1)} %pad_maximum_fusion.7.rest_2_.rest_4_), channel_id=1, source_target_pairs={{0,4},{2,6},{4,0},{6,2},{8,12},{10,14},{12,8},{14,10},{16,20},{18,... | collective-permute-start | bytes 1769480 | tf_op jit(solution)/shard_map/ppermute | solution.py:36
  61.9 15.0 %collective-permute-done.13 = bf16[128,2048]{1,0:T(8,128)(2,1)S(1)} collective-permute-done((bf16[128,2048]{1,0:T(8,128)(2,1)}, bf16[128,2048]{1,0:T(8,128)(2,1)S(1)}, u32[]{:S(2)}, u32[]{:S(2)}) %collective-permute-start.13) | collective-permute-done | bytes 524320 | tf_op jit(solution)/shard_map/ppermute | solution.py:36
  81.3 2.9 %embed.1.mine = bf16[2,512,512]{2,1,0:T(8,128)(2,1)S(1)} custom-call(s32[8]{0:T(128)S(1)} %stack.37.pos, bf16[512,768]{1,0:T(8,128)(2,1)S(1)} %bitcast.35, bf16[512,768]{1,0:T(8,128)(2,1)S(1)} %copy-done.5, bf16[576,512]{1,0:T(8,128)(2,1)S(1)} %pad_maximum_fusion.6.rest_0_, bf16[576,512]{1,0:T(8,128)(2,1)S(1)} %copy-done.11, ...), custom_call_target="tpu_custom_call" | custom-call | flops 805306368 | bytes 4194304 | tf_op jit(solution)/shard_map/embed/pallas_call | solution.py:233
  86.5 3.7 %collective-permute-done.19 = bf16[128,2048]{1,0:T(8,128)(2,1)S(1)} collective-permute-done((bf16[128,2048]{1,0:T(8,128)(2,1)S(1)}, bf16[128,2048]{1,0:T(8,128)(2,1)S(1)}, u32[]{:S(2)}, u32[]{:S(2)}) %collective-permute-start.19) | collective-permute-done | bytes 524320 | tf_op jit(solution)/shard_map/ppermute | solution.py:36
  91.2 1.6 collective-permute-start.23
  93.8 1.7 collective-permute-start.24
  95.6 5.1 %collective-permute-done.23.rest_5_ = bf16[128,2048]{1,0:T(8,128)(2,1)} collective-permute-done((bf16[128,2048]{1,0:T(8,128)(2,1)}, bf16[128,2048]{1,0:T(8,128)(2,1)}, u32[]{:S(2)}, u32[]{:S(2)}) %collective-permute-start.23) | collective-permute-done | bytes 524320 | tf_op jit(solution)/shard_map/ppermute | solution.py:36
  100.7 2.5 %collective-permute-done.24.rest_7_ = bf16[128,2048]{1,0:T(8,128)(2,1)} collective-permute-done((bf16[128,2048]{1,0:T(8,128)(2,1)}, bf16[128,2048]{1,0:T(8,128)(2,1)}, u32[]{:S(2)}, u32[]{:S(2)}) %collective-permute-start.24) | collective-permute-done | bytes 524320 | tf_op jit(solution)/shard_map/ppermute | solution.py:36
  110.8 19.6 %attention.1 = (bf16[2,256,1024]{2,1,0:T(8,128)(2,1)S(1)}, bf16[2,256,1024]{2,1,0:T(8,128)(2,1)S(1)}) custom-call(s32[8]{0:T(128)S(1)} %stack.37.pos, bf16[2,512,512]{2,1,0:T(8,128)(2,1)S(1)} %embed.1.mine, bf16[2,512,512]{2,1,0:T(8,128)(2,1)S(1)} %collective-permute-done.16.recv, f32[2,512]{1,0:T(2,128)S(1)} %broadcast_select_fusion.gain, ...), custom_call_target="tpu_custom_call" | custom-call | flops 5368709120 | bytes 10485760 | tf_op jit(solution)/shard_map/attention/pallas_call | solution.py:322
  131.2 1.8 collective-permute-start.27
  132.9 12.1 %collective-permute-done.26.rest_1_ = bf16[128,2048]{1,0:T(8,128)(2,1)S(1)} collective-permute-done((bf16[128,2048]{1,0:T(8,128)(2,1)S(1)}, bf16[128,2048]{1,0:T(8,128)(2,1)S(1)}, u32[]{:S(2)}, u32[]{:S(2)}) %collective-permute-start.26) | collective-permute-done | bytes 524320 | tf_op jit(solution)/shard_map/ppermute | solution.py:36
  145.3 2.2 %collective-permute-start.29 = (bf16[128,2048]{1,0:T(8,128)(2,1)S(1)}, bf16[128,2048]{1,0:T(8,128)(2,1)S(1)}, u32[]{:S(2)}, u32[]{:S(2)}) collective-permute-start(bf16[128,2048]{1,0:T(8,128)(2,1)S(1)} %collective-permute-done.25), channel_id=1, source_target_pairs={{0,8},{2,10},{4,12},{6,14},{8,16},{10,18},{12,20},{14,22},{16,24},... | collective-permute-start | bytes 1572872 | tf_op jit(solution)/shard_map/ppermute | solution.py:36
  149.1 11.5 %collective-permute-done.29 = bf16[128,2048]{1,0:T(8,128)(2,1)S(1)} collective-permute-done((bf16[128,2048]{1,0:T(8,128)(2,1)S(1)}, bf16[128,2048]{1,0:T(8,128)(2,1)S(1)}, u32[]{:S(2)}, u32[]{:S(2)}) %collective-permute-start.29) | collective-permute-done | bytes 524320 | tf_op jit(solution)/shard_map/ppermute | solution.py:36
  162.4 1.8 collective-permute-start.31
  164.3 15.4 %up.1.hidden = bf16[2,2,256,2048]{3,2,1,0:T(8,128)(2,1)S(1)} custom-call(s32[8]{0:T(128)S(1)} %stack.37.pos, bf16[2,256,1024]{2,1,0:T(8,128)(2,1)S(1)} %get-tuple-element.59.own, bf16[2,256,1024]{2,1,0:T(8,128)(2,1)S(1)} %collective-permute-done.18.came, bf16[128,2048]{1,0:T(8,128)(2,1)S(1)} %copy-done.16, bf16[128,2048]{1,0:T(8,128)(2,1)S(1)} %copy-done.29, ...), custom_call_target="tpu_custom_call" | custom-call | flops 4294967296 | bytes 10485760 | tf_op jit(solution)/shard_map/up/pallas_call | solution.py:407
  179.7 6.6 %down.2 = (bf16[2,256,512]{2,1,0:T(8,128)(2,1)S(1)}, bf16[2,256,512]{2,1,0:T(8,128)(2,1)}) custom-call(s32[8]{0:T(128)S(1)} %stack.37.pos, bf16[2,2,256,2048]{3,2,1,0:T(8,128)(2,1)S(1)} %up.1.hidden, bf16[128,2048]{1,0:T(8,128)(2,1)S(1)} %pad_maximum_fusion.4.rest_0_, bf16[128,2048]{1,0:T(8,128)(2,1)S(1)} %collective-permute-done.26.rest_1_, ...), custom_call_target="tpu_custom_call" | custom-call | flops 2147483648 | bytes 8388608 | tf_op jit(solution)/shard_map/down/pallas_call | solution.py:438
  186.5 6.9 %down.3 = (bf16[2,256,512]{2,1,0:T(8,128)(2,1)S(1)}, bf16[2,256,512]{2,1,0:T(8,128)(2,1)}) custom-call(s32[8]{0:T(128)S(1)} %stack.37.pos, bf16[2,2,256,2048]{3,2,1,0:T(8,128)(2,1)S(1)} %up.1.hidden, bf16[128,2048]{1,0:T(8,128)(2,1)S(1)} %pad_maximum_fusion.12.rest_0_, bf16[128,2048]{1,0:T(8,128)(2,1)S(1)} %collective-permute-done.30.rest_1_, ...), custom_call_target="tpu_custom_call" | custom-call | flops 2147483648 | bytes 8388608 | tf_op jit(solution)/shard_map/down/pallas_call | solution.py:438
  198.6 2.8 %output.1 = (bf16[2,256,1024]{2,1,0:T(8,128)(2,1)}, f32[8,128]{1,0:T(8,128)S(1)}) custom-call(s32[8]{0:T(128)S(1)} %stack.37.pos, f32[2,256,1024]{2,1,0:T(8,128)S(1)} %get-tuple-element.58.residual, bf16[2,256,1024]{2,1,0:T(8,128)(2,1)S(1)} %bitcast.33, bf16[2,256,512]{2,1,0:T(8,128)(2,1)S(1)} %copy-done.20, ...), custom_call_target="tpu_custom_call" | custom-call | flops 4194304 | bytes 8388608 | tf_op jit(solution)/shard_map/output/pallas_call | solution.py:484
  202.7 9.4 %all_to_all.5 = f32[32,1,2]{2,1,0:T(1,128)S(1)} all-to-all(f32[32,1,2]{2,1,0:T(1,128)S(1)} %broadcast_in_dim.10), channel_id=1, replica_groups=mesh['dp'=16,'mp'=2] {'dp','mp'}, dimensions={0} | all-to-all | bytes 512 | tf_op jit(solution)/shard_map/all_to_all | solution.py:591
  (203 shorter events, 62.2 us)
Async XLA Ops:
  4.9 13.2 %collective-permute-start.1 = (bf16[304,512]{1,0:T(8,128)(2,1)S(1)}, bf16[304,512]{1,0:T(8,128)(2,1)S(1)}, u32[]{:S(2)}, u32[]{:S(2)}) collective-permute-start(bf16[304,512]{1,0:T(8,128)(2,1)S(1)} %constant_dynamic-update-slice_fusion), channel_id=1, source_target_pairs={{0,8},{2,10},{4,12},{6,14},{8,16},{10,18},{12,20},{14,22},{16,24},... | collective-permute-start | bytes 933896 | tf_op jit(solution)/shard_map/ppermute | solution.py:36
  18.2 9.5 %collective-permute-start.4 = (bf16[304,512]{1,0:T(8,128)(2,1)S(1)}, bf16[304,512]{1,0:T(8,128)(2,1)S(1)}, u32[]{:S(2)}, u32[]{:S(2)}) collective-permute-start(bf16[304,512]{1,0:T(8,128)(2,1)S(1)} %collective-permute-done.1), channel_id=1, source_target_pairs={{0,8},{2,10},{4,12},{6,14},{8,16},{10,18},{12,20},{14,22},{16,24},... | collective-permute-start | bytes 933896 | tf_op jit(solution)/shard_map/ppermute | solution.py:36
  28.0 14.3 %collective-permute-start.9 = (bf16[640,512]{1,0:T(8,128)(2,1)S(1)}, bf16[640,512]{1,0:T(8,128)(2,1)S(1)}, u32[]{:S(2)}, u32[]{:S(2)}) collective-permute-start(bf16[640,512]{1,0:T(8,128)(2,1)S(1)} %pad_maximum_fusion.rest_2_), channel_id=1, source_target_pairs={{0,2},{2,0},{4,6},{6,4},{8,10},{10,8},{12,14},{14,12},{16,18},{18,... | collective-permute-start | bytes 1966088 | tf_op jit(solution)/shard_map/ppermute | solution.py:36
  29.6 12.7 %collective-permute-start.8 = (bf16[576,512]{1,0:T(8,128)(2,1)S(1)}, bf16[576,512]{1,0:T(8,128)(2,1)S(1)}, u32[]{:S(2)}, u32[]{:S(2)}) collective-permute-start(bf16[576,512]{1,0:T(8,128)(2,1)S(1)} %pad_maximum_fusion.6.rest_0_), channel_id=1, source_target_pairs={{0,4},{2,6},{4,0},{6,2},{8,12},{10,14},{12,8},{14,10},{16,20},{18,... | collective-permute-start | bytes 1769480 | tf_op jit(solution)/shard_map/ppermute | solution.py:36
  31.1 9.7 %collective-permute-start.7 = (bf16[304,512]{1,0:T(8,128)(2,1)S(1)}, bf16[304,512]{1,0:T(8,128)(2,1)S(1)}, u32[]{:S(2)}, u32[]{:S(2)}) collective-permute-start(bf16[304,512]{1,0:T(8,128)(2,1)S(1)} %collective-permute-done.4), channel_id=1, source_target_pairs={{0,8},{2,10},{4,12},{6,14},{8,16},{10,18},{12,20},{14,22},{16,24},... | collective-permute-start | bytes 933896 | tf_op jit(solution)/shard_map/ppermute | solution.py:36
  32.7 46.6 %collective-permute-start = (bf16[512,768]{1,0:T(8,128)(2,1)S(1)}, bf16[512,768]{1,0:T(8,128)(2,1)S(1)}, u32[]{:S(2)}, u32[]{:S(2)}) collective-permute-start(bf16[512,768]{1,0:T(8,128)(2,1)S(1)} %bitcast.34), channel_id=1, source_target_pairs={{0,1},{1,0},{2,3},{3,2},{4,5},{5,4},{6,7},{7,6},{8,9},{9,8},{10,11... | collective-permute-start | bytes 2359304 | tf_op jit(solution)/shard_map/ppermute | solution.py:74
  33.6 20.7 %collective-permute-start.10 = (bf16[128,2048]{1,0:T(8,128)(2,1)}, bf16[128,2048]{1,0:T(8,128)(2,1)}, u32[]{:S(2)}, u32[]{:S(2)}) collective-permute-start(bf16[128,2048]{1,0:T(8,128)(2,1)} %pad_maximum_fusion.3), channel_id=1, source_target_pairs={{0,8},{2,10},{4,12},{6,14},{8,16},{10,18},{12,20},{14,22},{16,24},... | collective-permute-start | bytes 1572872 | tf_op jit(solution)/shard_map/ppermute | solution.py:36
  53.6 42.0 %collective-permute-start.22 = (bf16[128,2048]{1,0:T(8,128)(2,1)}, bf16[128,2048]{1,0:T(8,128)(2,1)}, u32[]{:S(2)}, u32[]{:S(2)}) collective-permute-start(bf16[128,2048]{1,0:T(8,128)(2,1)} %pad_maximum_fusion.5), channel_id=1, source_target_pairs={{0,8},{2,10},{4,12},{6,14},{8,16},{10,18},{12,20},{14,22},{16,24},... | collective-permute-start | bytes 1572872 | tf_op jit(solution)/shard_map/ppermute | solution.py:36
  56.7 20.3 %collective-permute-start.13 = (bf16[128,2048]{1,0:T(8,128)(2,1)}, bf16[128,2048]{1,0:T(8,128)(2,1)S(1)}, u32[]{:S(2)}, u32[]{:S(2)}) collective-permute-start(bf16[128,2048]{1,0:T(8,128)(2,1)} %collective-permute-done.10), channel_id=1, source_target_pairs={{0,8},{2,10},{4,12},{6,14},{8,16},{10,18},{12,20},{14,22},{16,24},... | collective-permute-start | bytes 1572872 | tf_op jit(solution)/shard_map/ppermute | solution.py:36
  57.1 20.2 %collective-permute-start.14 = (bf16[576,512]{1,0:T(8,128)(2,1)S(1)}, bf16[576,512]{1,0:T(8,128)(2,1)S(1)}, u32[]{:S(2)}, u32[]{:S(2)}) collective-permute-start(bf16[576,512]{1,0:T(8,128)(2,1)S(1)} %pad_maximum_fusion.7.rest_2_.rest_4_), channel_id=1, source_target_pairs={{0,4},{2,6},{4,0},{6,2},{8,12},{10,14},{12,8},{14,10},{16,20},{18,... | collective-permute-start | bytes 1769480 | tf_op jit(solution)/shard_map/ppermute | solution.py:36
  60.5 18.0 %collective-permute-start.15 = (bf16[640,512]{1,0:T(8,128)(2,1)S(1)}, bf16[640,512]{1,0:T(8,128)(2,1)S(1)}, u32[]{:S(2)}, u32[]{:S(2)}) collective-permute-start(bf16[640,512]{1,0:T(8,128)(2,1)S(1)} %pad_maximum_fusion.1.rest_6_), channel_id=1, source_target_pairs={{0,2},{2,0},{4,6},{6,4},{8,10},{10,8},{12,14},{14,12},{16,18},{18,... | collective-permute-start | bytes 1966088 | tf_op jit(solution)/shard_map/ppermute | solution.py:36
  79.3 11.0 %collective-permute-start.19 = (bf16[128,2048]{1,0:T(8,128)(2,1)S(1)}, bf16[128,2048]{1,0:T(8,128)(2,1)S(1)}, u32[]{:S(2)}, u32[]{:S(2)}) collective-permute-start(bf16[128,2048]{1,0:T(8,128)(2,1)S(1)} %collective-permute-done.13), channel_id=1, source_target_pairs={{0,8},{2,10},{4,12},{6,14},{8,16},{10,18},{12,20},{14,22},{16,24},... | collective-permute-start | bytes 1572872 | tf_op jit(solution)/shard_map/ppermute | solution.py:36
  85.0 19.3 %collective-permute-start.16 = (bf16[2,512,512]{2,1,0:T(8,128)(2,1)S(1)}, bf16[2,512,512]{2,1,0:T(8,128)(2,1)S(1)}, u32[]{:S(2)}, u32[]{:S(2)}) collective-permute-start(bf16[2,512,512]{2,1,0:T(8,128)(2,1)S(1)} %embed.1.mine), channel_id=1, source_target_pairs={{0,1},{1,0},{2,3},{3,2},{4,5},{5,4},{6,7},{7,6},{8,9},{9,8},{10,11... | collective-permute-start | bytes 3145736 | tf_op jit(solution)/shard_map/ppermute | solution.py:74
  91.2 9.5 %collective-permute-start.23 = (bf16[128,2048]{1,0:T(8,128)(2,1)}, bf16[128,2048]{1,0:T(8,128)(2,1)}, u32[]{:S(2)}, u32[]{:S(2)}) collective-permute-start(bf16[128,2048]{1,0:T(8,128)(2,1)} %pad_maximum_fusion.9.rest_4_), channel_id=1, source_target_pairs={{0,4},{2,6},{4,0},{6,2},{8,12},{10,14},{12,8},{14,10},{16,20},{18,... | collective-permute-start | bytes 1572872 | tf_op jit(solution)/shard_map/ppermute | solution.py:36
  93.8 9.5 %collective-permute-start.24 = (bf16[128,2048]{1,0:T(8,128)(2,1)}, bf16[128,2048]{1,0:T(8,128)(2,1)}, u32[]{:S(2)}, u32[]{:S(2)}) collective-permute-start(bf16[128,2048]{1,0:T(8,128)(2,1)} %pad_maximum_fusion.10.rest_6_), channel_id=1, source_target_pairs={{0,2},{2,0},{4,6},{6,4},{8,10},{10,8},{12,14},{14,12},{16,18},{18,... | collective-permute-start | bytes 1572872 | tf_op jit(solution)/shard_map/ppermute | solution.py:36
  103.3 29.7 %collective-permute-start.25 = (bf16[128,2048]{1,0:T(8,128)(2,1)}, bf16[128,2048]{1,0:T(8,128)(2,1)S(1)}, u32[]{:S(2)}, u32[]{:S(2)}) collective-permute-start(bf16[128,2048]{1,0:T(8,128)(2,1)} %collective-permute-done.22), channel_id=1, source_target_pairs={{0,8},{2,10},{4,12},{6,14},{8,16},{10,18},{12,20},{14,22},{16,24},... | collective-permute-start | bytes 1572872 | tf_op jit(solution)/shard_map/ppermute | solution.py:36
  130.5 17.0 %collective-permute-start.17 = (bf16[2,256,1024]{2,1,0:T(8,128)(2,1)S(1)}, bf16[2,256,1024]{2,1,0:T(8,128)(2,1)S(1)}, u32[]{:S(2)}, u32[]{:S(2)}) collective-permute-start(bf16[2,256,1024]{2,1,0:T(8,128)(2,1)S(1)} %get-tuple-element.57), channel_id=1, source_target_pairs={{0,1},{1,0},{2,3},{3,2},{4,5},{5,4},{6,7},{7,6},{8,9},{9,8},{10,11... | collective-permute-start | bytes 3145736 | tf_op jit(solution)/shard_map/ppermute | solution.py:74
  130.6 14.4 %collective-permute-start.26 = (bf16[128,2048]{1,0:T(8,128)(2,1)S(1)}, bf16[128,2048]{1,0:T(8,128)(2,1)S(1)}, u32[]{:S(2)}, u32[]{:S(2)}) collective-permute-start(bf16[128,2048]{1,0:T(8,128)(2,1)S(1)} %pad_maximum_fusion.4.rest_0_), channel_id=1, source_target_pairs={{0,4},{2,6},{4,0},{6,2},{8,12},{10,14},{12,8},{14,10},{16,20},{18,... | collective-permute-start | bytes 1572872 | tf_op jit(solution)/shard_map/ppermute | solution.py:36
  131.2 14.1 %collective-permute-start.27 = (bf16[128,2048]{1,0:T(8,128)(2,1)S(1)}, bf16[128,2048]{1,0:T(8,128)(2,1)S(1)}, u32[]{:S(2)}, u32[]{:S(2)}) collective-permute-start(bf16[128,2048]{1,0:T(8,128)(2,1)S(1)} %pad_maximum_fusion.11.rest_2_), channel_id=1, source_target_pairs={{0,2},{2,0},{4,6},{6,4},{8,10},{10,8},{12,14},{14,12},{16,18},{18,... | collective-permute-start | bytes 1572872 | tf_op jit(solution)/shard_map/ppermute | solution.py:36
  145.3 15.4 %collective-permute-start.29 = (bf16[128,2048]{1,0:T(8,128)(2,1)S(1)}, bf16[128,2048]{1,0:T(8,128)(2,1)S(1)}, u32[]{:S(2)}, u32[]{:S(2)}) collective-permute-start(bf16[128,2048]{1,0:T(8,128)(2,1)S(1)} %collective-permute-done.25), channel_id=1, source_target_pairs={{0,8},{2,10},{4,12},{6,14},{8,16},{10,18},{12,20},{14,22},{16,24},... | collective-permute-start | bytes 1572872 | tf_op jit(solution)/shard_map/ppermute | solution.py:36
  149.0 15.2 %collective-permute-start.18 = (bf16[2,256,1024]{2,1,0:T(8,128)(2,1)S(1)}, bf16[2,256,1024]{2,1,0:T(8,128)(2,1)S(1)}, u32[]{:S(2)}, u32[]{:S(2)}) collective-permute-start(bf16[2,256,1024]{2,1,0:T(8,128)(2,1)S(1)} %get-tuple-element.59.own), channel_id=1, source_target_pairs={{0,1},{1,0},{2,3},{3,2},{4,5},{5,4},{6,7},{7,6},{8,9},{9,8},{10,11... | collective-permute-start | bytes 3145736 | tf_op jit(solution)/shard_map/ppermute | solution.py:74
  160.8 25.7 %collective-permute-start.30 = (bf16[128,2048]{1,0:T(8,128)(2,1)S(1)}, bf16[128,2048]{1,0:T(8,128)(2,1)S(1)}, u32[]{:S(2)}, u32[]{:S(2)}) collective-permute-start(bf16[128,2048]{1,0:T(8,128)(2,1)S(1)} %pad_maximum_fusion.12.rest_0_), channel_id=1, source_target_pairs={{0,4},{2,6},{4,0},{6,2},{8,12},{10,14},{12,8},{14,10},{16,20},{18,... | collective-permute-start | bytes 1572872 | tf_op jit(solution)/shard_map/ppermute | solution.py:36
  162.4 24.0 %collective-permute-start.31 = (bf16[128,2048]{1,0:T(8,128)(2,1)S(1)}, bf16[128,2048]{1,0:T(8,128)(2,1)S(1)}, u32[]{:S(2)}, u32[]{:S(2)}) collective-permute-start(bf16[128,2048]{1,0:T(8,128)(2,1)S(1)} %pad_maximum_fusion.13.rest_2_), channel_id=1, source_target_pairs={{0,2},{2,0},{4,6},{6,4},{8,10},{10,8},{12,14},{14,12},{16,18},{18,... | collective-permute-start | bytes 1572872 | tf_op jit(solution)/shard_map/ppermute | solution.py:36
  186.4 9.6 %collective-permute-start.28 = (bf16[2,256,512]{2,1,0:T(8,128)(2,1)}, bf16[2,256,512]{2,1,0:T(8,128)(2,1)}, u32[]{:S(2)}, u32[]{:S(2)}) collective-permute-start(bf16[2,256,512]{2,1,0:T(8,128)(2,1)} %get-tuple-element.72), channel_id=1, source_target_pairs={{0,1},{1,0},{2,3},{3,2},{4,5},{5,4},{6,7},{7,6},{8,9},{9,8},{10,11... | collective-permute-start | bytes 1572872 | tf_op jit(solution)/shard_map/ppermute | solution.py:74
  (57 other events, 443.2 us)

commit v2 on v1

v2 whole, which is shorter than its diff:
```python
import functools

import jax
import jax.numpy as jnp
from jax import lax
from jax.experimental import pallas as pl
from jax.experimental.pallas import tpu as pltpu
from jax.sharding import PartitionSpec as P

HEAD = 64
TILE = 16
Z, Y, X = 0, 1, 2
MIB = 1 << 20
POS_Z, POS_Y, POS_X, POS_M, POS_LEN, POS_STEP = 0, 1, 2, 3, 4, 6


def ring_dims(count):
    nz = 4 if count % 4 == 0 else 1
    nx = 1
    while nx * nx < count // nz:
        nx *= 2
    ny = count // nz // nx
    return (nz, ny, nx) if nz * ny * nx == count else (1, 1, count)


def shift(value, dims, *axes):
    pairs = []
    for z in range(dims[0]):
        for y in range(dims[1]):
            for x in range(dims[2]):
                to = [z, y, x]
                for axis in axes:
                    to[axis] = (to[axis] + 1) % dims[axis]
                pairs.append(
                    ((z * dims[1] + y) * dims[2] + x, (to[0] * dims[1] + to[1]) * dims[2] + to[2])
                )
    return lax.ppermute(value, "dp", pairs)


class Chunk:
    def __init__(self, array, slots, half):
        self.array, self.slots, self.half = array, slots, half
        self.rows = array.shape[0] // len(slots)

    def moved(self, array, axis, by=1):
        slots = [tuple(v + by * (i == axis) for i, v in enumerate(s)) for s in self.slots]
        return Chunk(array, slots, self.half)

    def part(self, first, last):
        return Chunk(
            self.array[first * self.rows : last * self.rows], self.slots[first:last], self.half
        )


    def without(self, rows, half):
        value = self.array.reshape(len(self.slots), self.rows, -1)[:, rows:]
        return Chunk(value.reshape(-1, value.shape[2]), self.slots, half)


def joined(chunks):
    if len(chunks) == 1:
        return chunks[0]
    return Chunk(
        jnp.concatenate([c.array for c in chunks], 0), sum((c.slots for c in chunks), []), chunks[0].half
    )


def swap_columns(value):
    return lax.ppermute(value, "mp", [(0, 1), (1, 0)])


class Gather:
    def __init__(self, first, up, down, side_a, side_b, spans, dims):
        self.dims, self.spans, self.half = dims, spans, up.shape[0] // 2
        self.first, self.up, self.down, self.side_a, self.side_b = first, up, down, side_a, side_b

    def move(self, value, axis):
        return shift(value, self.dims, axis)

    def step(self, chunk, axis):
        return chunk.moved(shift(chunk.array, self.dims, axis), axis)

    def first_ends(self, blocks, low, kinds):
        slots = [(low + i, 0, 0) for i in range(len(blocks))]
        made = []
        for kind in kinds:
            begin, end = self.spans[kind]
            made.append(Chunk(jnp.concatenate([v[begin:end] for v in blocks], 0), slots, kind))
        return made

    def whole(self, shard, k):
        half = self.half
        rows = slice(k * half, (k + 1) * half)
        here = [(0, 0, 0)]
        return joined(
            [
                Chunk(shard[:half], here, 0),
                Chunk(self.from_x[rows], [(0, 0, 1)], 0),
                Chunk(shard[half:], here, 1),
                Chunk(self.from_y[rows], [(0, 1, 0)], 1),
            ]
        )

    def halves(self, blocks):
        a = joined([c.part(0, 2) for c in blocks])
        b = joined([c.part(2, 4) for c in blocks])
        b.half = 1
        return a, b

    def slot(self, number):
        if number == 0:
            self.first_z = [self.first, self.move(self.first, Z)]
            self.from_x, self.from_y = self.move(self.side_a, X), self.move(self.side_b, Y)
        elif number == 1:
            self.first_z.append(self.move(self.first_z[-1], Z))
            self.a, self.b = self.first_ends(self.first_z[:2], 0, (0, 1))
            self.a_far, self.b_far = self.step(self.a, X), self.step(self.b, Y)
            self.up_z, self.down_z = [self.whole(self.up, 0)], [self.whole(self.down, 1)]
        elif number == 2:
            self.first_z.append(self.move(self.first_z[-1], Z))
            self.a, self.b = joined([self.a, self.a_far]), joined([self.b, self.b_far])
            self.parts = [self.a, self.step(self.a, Y), self.b, self.step(self.b, X)]
        elif number == 3:
            self.up_z.append(self.step(self.up_z[-1], Z))
            self.a, self.b, own = self.first_ends(self.first_z[2:], 2, (5, 3, 4))
            corner = Chunk(shift(own.array, self.dims, X, Y), [(z, 1, 1) for z, _, _ in own.slots], 4)
            self.a_far = self.step(self.a, X)
            rows = self.b.array.shape[0]
            mixed = self.move(jnp.concatenate([self.b.array, own.array], 0), Y)
            self.b_far, own_far = self.b.moved(mixed[:rows], Y), own.moved(mixed[rows:], Y)
            self.early = self.parts[:2] + [self.a, self.a_far, own_far, corner]
        elif number == 4:
            self.up_z.append(self.step(self.up_z[-1], Z))
            self.a, self.b = joined([self.a, self.a_far]), joined([self.b, self.b_far])
            self.a = self.a.without(self.spans[5][1] - self.spans[2][1] + self.spans[2][0], 2)
            self.parts += [self.a, self.step(self.a, Y), self.b, self.step(self.b, X)]
        elif number == 5:
            self.up_parts = self.last(self.up_z[:2])
            self.up_z.append(self.step(self.up_z[-1], Z))
        elif number == 6:
            self.up_parts += self.last(self.up_z[2:])
            self.down_z.append(self.step(self.down_z[-1], Z))
        elif number == 7:
            self.down_parts = [self.last(self.down_z[:2])]
            self.down_z.append(self.step(self.down_z[-1], Z))
        elif number == 8:
            self.down_z.append(self.step(self.down_z[-1], Z))
            self.down_parts.append(self.last(self.down_z[2:3]))
        elif number == 9:
            self.down_parts.append(self.last(self.down_z[3:]))

    def last(self, blocks):
        a, b = self.halves(blocks)
        return [a, self.step(a, Y), b, self.step(b, X)]

    def end_slot(self, *others):
        chunks, arrays = [], []
        for name, value in vars(self).items():
            for i, v in enumerate(value if isinstance(value, list) else [value]):
                for k, w in enumerate(v if isinstance(v, list) else [v]):
                    if isinstance(w, Chunk):
                        if all(w is not c for c in chunks):
                            chunks.append(w)
                    elif isinstance(w, jax.Array):
                        arrays.append((name, i, w))
        together = lax.optimization_barrier(
            (tuple(c.array for c in chunks), tuple(w for _, _, w in arrays), others)
        )
        for c, new in zip(chunks, together[0], strict=True):
            c.array = new
        for (name, i, _), new in zip(arrays, together[1], strict=True):
            if isinstance(vars(self)[name], list):
                vars(self)[name][i] = new
            else:
                setattr(self, name, new)
        return together[2]


def pieces_of(chunks, spans, segment):
    found = []
    for number, chunk in enumerate(chunks):
        first, last = spans[chunk.half]
        low, high = max(first, segment[0]), min(last, segment[1])
        if low < high:
            for i, slot in enumerate(chunk.slots):
                found.append((number, i * chunk.rows + low - first, high - low, slot, low - segment[0]))
    return found


def source(pos, slot, dims, z_first=None):
    z, y, x = (lax.rem(pos[i] - slot[i] + dims[i], dims[i]) for i in (0, 1, 2))
    if z_first is not None:
        z = slot[0] - z_first
    return (z * dims[1] + y) * dims[2] + x


def lay_out(pos, dims, refs, pieces, into, block, z_first=None):
    for number, row, rows, slot, offset in pieces:
        to = offset
        if slot is not None:
            to = pl.multiple_of(source(pos, slot, dims, z_first) * block + offset, TILE)
        into[pl.ds(to, rows), :] = refs[number][pl.ds(row, rows), :]


def nt_dot(left, right):
    return lax.dot_general(left, right, (((1,), (1,)), ((), ())), preferred_element_type=jnp.float32)


def dot(left, right):
    return jnp.dot(left, right, preferred_element_type=jnp.float32)


def any_spec():
    return pl.BlockSpec(memory_space=pl.ANY)


def hbm_spec():
    return pl.BlockSpec(memory_space=pltpu.HBM)


def vmem_spec():
    return pl.BlockSpec(memory_space=pltpu.VMEM)


def smem_spec():
    return pl.BlockSpec(memory_space=pltpu.SMEM)


def limits(mib):
    return pltpu.CompilerParams(vmem_limit_bytes=mib * MIB)


def cost(flops, moved, exps=0):
    return pl.CostEstimate(flops=0, bytes_accessed=1024, transcendentals=0)


def pack_kernel(*rest):
    *shards, up, down, first, side_a, side_b, sems = rest
    half = up.shape[0] // 2
    moves, at = [], 0
    for shard in shards:
        for part in [shard] if len(shard.shape) == 2 else [shard.at[i] for i in range(shard.shape[0])]:
            moves.append((part, first.at[pl.ds(at, part.shape[0])]))
            at += part.shape[0]
    for k, shard in enumerate((up, down)):
        moves.append((shard.at[pl.ds(0, half)], side_a.at[pl.ds(k * half, half)]))
        moves.append((shard.at[pl.ds(half, half)], side_b.at[pl.ds(k * half, half)]))
    made = [pltpu.make_async_copy(a, b, sems.at[i]) for i, (a, b) in enumerate(moves)]
    for c in made:
        c.start()
    for c in made:
        c.wait()


def pack(shards, up, down):
    rows = sum(s.size for s in shards) // shards[0].shape[1]
    first = jax.ShapeDtypeStruct((rows, shards[0].shape[1]), up.dtype)
    side = jax.ShapeDtypeStruct(up.shape, up.dtype)
    return pl.pallas_call(
        pack_kernel,
        out_shape=(first, side, side),
        in_specs=[hbm_spec()] * (len(shards) + 2),
        out_specs=(vmem_spec(),) * 3,
        scratch_shapes=[pltpu.SemaphoreType.DMA((rows // shards[0].shape[0] + 4,))],
        compiler_params=limits(60),
        cost_estimate=cost(0, 2 * MIB),
        name="pack",
    )(*shards, up, down)


def pack_order(packed, up, down):
    first, side_a, side_b = packed
    return first, up, down, side_a, side_b


def embed_kernel(n, dims, pieces, block, pos, mine, other, *rest):
    refs, (tokens, weight) = rest[:n], rest[n:]
    lay_out(pos, dims, refs, pieces, weight, block)
    tokens[0] = dot(mine[...], weight[...]).astype(tokens.dtype)
    tokens[1] = dot(other[...], weight[...]).astype(tokens.dtype)


def embed(pos, dims, mine, other, chunks, pieces, block, columns):
    patches, pixels = mine.shape
    n = len(chunks)
    return pl.pallas_call(
        functools.partial(embed_kernel, n, dims, pieces, block),
        out_shape=jax.ShapeDtypeStruct((2, patches, columns), mine.dtype),
        in_specs=[smem_spec(), vmem_spec(), vmem_spec()] + [vmem_spec()] * n,
        out_specs=vmem_spec(),
        scratch_shapes=[pltpu.VMEM((pixels, columns), mine.dtype)],
        compiler_params=limits(8),
        cost_estimate=cost(4 * patches * pixels * columns, 4 * MIB),
        name="embed",
    )(pos, mine, other, *chunks)


def project_kernel(n, dims, pieces, block, pos, mine, recv, gain, *rest):
    refs = rest[:n]
    q, k, v, weight, normed = rest[n:]
    m = pos[POS_M]
    columns = mine.shape[2]
    width = 2 * columns
    for i in range(2):
        low = mine[i].astype(jnp.float32)
        high = recv[1 - i].astype(jnp.float32)
        average = (
            jnp.sum(low, axis=-1, keepdims=True) + jnp.sum(high, axis=-1, keepdims=True)
        ) / width
        low, high = low - average, high - average
        spread = (
            jnp.sum(low * low, axis=-1, keepdims=True) + jnp.sum(high * high, axis=-1, keepdims=True)
        ) / width
        scale = lax.rsqrt(spread + 1e-06)
        normed[i, 0] = (low * scale * gain[0:1]).astype(normed.dtype)
        normed[i, 1] = (high * scale * gain[1:2]).astype(normed.dtype)
    here = pl.ds(pl.multiple_of(m * columns, columns), columns)
    there = pl.ds(pl.multiple_of((1 - m) * columns, columns), columns)
    for some, result, factor in zip(pieces, (q, k, v), (HEAD**-0.5, 1.0, 1.0), strict=True):
        lay_out(pos, dims, refs, some, weight, block)
        for i in range(2):
            value = dot(normed[i, 0], weight[here, :]) + dot(normed[i, 1], weight[there, :])
            if factor != 1.0:
                value = value * factor
            result[i] = value.astype(result.dtype)


def project(pos, dims, mine, recv, gain, chunks, pieces, block, width):
    _, patches, columns = mine.shape
    n = len(chunks)
    kind = mine.dtype
    out = jax.ShapeDtypeStruct(mine.shape, kind)
    return pl.pallas_call(
        functools.partial(project_kernel, n, dims, pieces, block),
        out_shape=(out, out, out),
        in_specs=[smem_spec(), vmem_spec(), vmem_spec(), vmem_spec()] + [vmem_spec()] * n,
        out_specs=(vmem_spec(),) * 3,
        scratch_shapes=[
            pltpu.VMEM((width, columns), kind),
            pltpu.VMEM((2, 2, patches, columns), kind),
        ],
        compiler_params=limits(11),
        cost_estimate=cost(2 * 2 * patches * width * columns * 3, 8 * MIB),
        name="project",
    )(pos, mine, recv, gain, *chunks)


def attention_kernel(n, dims, pieces, block, pos, q, k, v, *rest):
    refs = rest[:n]
    keep, send, wo, mixed = rest[n:]
    lay_out(pos, dims, refs, pieces, wo, block)
    m = pos[POS_M]
    patches, columns = q.shape[1:]
    rows_own = patches // 2
    pair = 2 * HEAD
    key_ids = lax.broadcasted_iota(jnp.int32, (1, patches), 1)
    lane = lax.broadcasted_iota(jnp.int32, (patches, pair), 1)
    first = lane < HEAD
    for i in range(2):
        masked = jnp.where(key_ids < pos[POS_LEN + i], 0.0, -1e30).astype(jnp.float32)
        for h in range(columns // pair):
            cut = slice(h * pair, (h + 1) * pair)
            q_pair, k_pair, v_pair = q[i, :, cut], k[i, :, cut], v[i, :, cut]
            found = []
            for own in (first, jnp.logical_not(first)):
                scores = nt_dot(q_pair, jnp.where(own, k_pair, jnp.zeros_like(k_pair))) + masked
                expo = jnp.exp(scores - jnp.max(scores, axis=-1, keepdims=True))
                value = dot(
                    expo.astype(v_pair.dtype), jnp.where(own, v_pair, jnp.ones_like(v_pair))
                )
                found.append(value / pltpu.roll(value, HEAD, 1))
            mixed[i, :, cut] = jnp.where(first, found[0], found[1]).astype(mixed.dtype)
    own_rows = pl.ds(pl.multiple_of(m * rows_own, rows_own), rows_own)
    far_rows = pl.ds(pl.multiple_of((1 - m) * rows_own, rows_own), rows_own)
    for i in range(2):
        keep[i] = nt_dot(mixed[i, own_rows, :], wo[...]).astype(keep.dtype)
        send[i] = nt_dot(mixed[i, far_rows, :], wo[...]).astype(send.dtype)


def attention(pos, dims, q, k, v, chunks, pieces, block, width):
    _, patches, columns = q.shape
    n = len(chunks)
    out = jax.ShapeDtypeStruct((2, patches // 2, width), q.dtype)
    return pl.pallas_call(
        functools.partial(attention_kernel, n, dims, pieces, block),
        out_shape=(out, out),
        in_specs=[smem_spec()] + [vmem_spec()] * 3 + [vmem_spec()] * n,
        out_specs=(vmem_spec(), vmem_spec()),
        scratch_shapes=[
            pltpu.VMEM((width, columns), q.dtype),
            pltpu.VMEM(q.shape, q.dtype),
        ],
        compiler_params=limits(10),
        cost_estimate=cost(
            4 * patches * width * columns + 8 * patches * patches * columns,
            8 * MIB,
            2 * patches * patches * columns // HEAD,
        ),
        name="attention",
    )(pos, q, k, v, *chunks)


def residual_kernel(pos, mine, recv, keep, came, gain, residual, normed):
    m = pos[POS_M]
    columns = mine.shape[2]
    rows = keep.shape[1]
    width = 2 * columns
    own_rows = pl.ds(pl.multiple_of(m * rows, rows), rows)
    here = pl.ds(pl.multiple_of(m * columns, columns), columns)
    there = pl.ds(pl.multiple_of((1 - m) * columns, columns), columns)
    for i in range(2):
        parts = []
        for tokens, at in ((mine[i, own_rows, :], here), (recv[1 - i, own_rows, :], there)):
            parts.append(
                tokens.astype(jnp.float32)
                + (keep[i, :, at].astype(jnp.float32) + came[1 - i, :, at].astype(jnp.float32))
            )
            residual[i, :, at] = parts[-1]
        average = sum(jnp.sum(v, axis=-1, keepdims=True) for v in parts) / width
        parts = [v - average for v in parts]
        spread = sum(jnp.sum(v * v, axis=-1, keepdims=True) for v in parts) / width
        scale = lax.rsqrt(spread + 1e-06)
        for v, at in zip(parts, (here, there), strict=True):
            normed[i, :, at] = (v * scale * gain[0:1, at]).astype(normed.dtype)


def residual_and_norm(pos, mine, recv, keep, came, gain):
    return pl.pallas_call(
        residual_kernel,
        out_shape=(
            jax.ShapeDtypeStruct(keep.shape, jnp.float32),
            jax.ShapeDtypeStruct(keep.shape, keep.dtype),
        ),
        in_specs=[smem_spec()] + [vmem_spec()] * 5,
        out_specs=(vmem_spec(), vmem_spec()),
        compiler_params=limits(8),
        cost_estimate=cost(10 * keep.size, 10 * MIB),
        name="residual",
    )(pos, mine, recv, keep, came, gain)


def gelu(x):
    return x * (0.5 * lax.erf(x * 0.7071067811865476) + 0.5)


def up_kernel(n, dims, pieces, block, pos, own, came, *rest):
    refs, (hidden, weight) = rest[:n], rest[n:]
    lay_out(pos, dims, refs, pieces, weight, block)
    tile = 512
    rows, width = own.shape[1:]
    for k, side in enumerate((own, came)):
        left = side[...].reshape(2 * rows, width)
        for j in range(hidden.shape[-1] // tile):
            at = slice(j * tile, (j + 1) * tile)
            value = gelu(dot(left, weight[:, at])).astype(hidden.dtype).reshape(2, rows, tile)
            if k == 0:
                hidden[0, :, :, at] = value
            else:
                hidden[1, 0, :, at] = value[1]
                hidden[1, 1, :, at] = value[0]


def up_layer(pos, dims, own, came, chunks, pieces, block, units):
    _, rows, width = own.shape
    n = len(chunks)
    return pl.pallas_call(
        functools.partial(up_kernel, n, dims, pieces, block),
        out_shape=jax.ShapeDtypeStruct((2, 2, rows, units), own.dtype),
        in_specs=[smem_spec(), vmem_spec(), vmem_spec()] + [vmem_spec()] * n,
        out_specs=vmem_spec(),
        scratch_shapes=[pltpu.VMEM((width, units), own.dtype)],
        compiler_params=limits(12),
        cost_estimate=cost(8 * rows * width * units, 10 * MIB, 4 * rows * units),
        name="up",
    )(pos, own, came, *chunks)


def down_kernel(n, dims, pieces, block, z_first, pos, hidden, *rest):
    refs, (keep, send, weight) = rest[:n], rest[n:]
    lay_out(pos, dims, refs, pieces, weight, block, z_first)
    for k, result in enumerate((keep, send)):
        left = hidden[k].reshape(-1, hidden.shape[-1])
        result[...] = nt_dot(left, weight[...]).astype(result.dtype).reshape(result.shape)


def down_layer(pos, dims, hidden, chunks, pieces, block, z_first, columns):
    _, _, rows, units = hidden.shape
    n = len(chunks)
    out = jax.ShapeDtypeStruct((2, rows, columns), hidden.dtype)
    return pl.pallas_call(
        functools.partial(down_kernel, n, dims, pieces, block, z_first),
        out_shape=(out, out),
        in_specs=[smem_spec(), vmem_spec()] + [vmem_spec()] * n,
        out_specs=(vmem_spec(), vmem_spec()),
        scratch_shapes=[pltpu.VMEM((columns, units), hidden.dtype)],
        compiler_params=limits(8),
        cost_estimate=cost(8 * rows * columns * units, 8 * MIB),
        name="down",
    )(pos, hidden, *chunks)


def output_kernel(n, nz, starts, pos, residual, targets, *rest):
    parts, (encoded, squares) = rest[:n], rest[n:]
    m = pos[POS_M]
    rows = residual.shape[1]
    total = jnp.zeros((), jnp.float32)
    row_ids = m * rows + lax.broadcasted_iota(jnp.int32, (rows, 1), 0)
    for i in range(2):
        s = pos[POS_STEP] if i == 0 else 1 - pos[POS_STEP]
        usable = row_ids < pos[POS_LEN + i]
        sums = jnp.zeros((rows, 1), jnp.float32)
        for j, spots in enumerate(starts):
            keep, came = parts[2 * j], parts[2 * j + 1]
            size = keep.shape[2] // len(spots)
            for b, back in enumerate(spots):
                at = slice(b * size, (b + 1) * size)
                if back is None:
                    place = pl.ds(0, size)
                else:
                    begin = lax.rem(pos[POS_Z] - back + nz, nz) * size
                    place = pl.ds(pl.multiple_of(begin, size), size)
                value = residual[i, :, place] + (
                    keep[i, :, at].astype(jnp.float32) + came[1 - i, :, at].astype(jnp.float32)
                )
                encoded[s, :, place] = value.astype(encoded.dtype)
                misfit = value - targets[s, :, place].astype(jnp.float32)
                sums = sums + jnp.sum(misfit * misfit, axis=-1, keepdims=True)
        total = total + jnp.sum(jnp.where(usable, sums, 0.0))
    squares[...] = jnp.full(squares.shape, total, jnp.float32)


def output_layer(pos, residual, targets, nz, starts, parts):
    return pl.pallas_call(
        functools.partial(output_kernel, len(parts), nz, starts),
        out_shape=(
            jax.ShapeDtypeStruct(residual.shape, targets.dtype),
            jax.ShapeDtypeStruct((8, 128), jnp.float32),
        ),
        in_specs=[smem_spec()] + [vmem_spec()] * (2 + len(parts)),
        out_specs=(vmem_spec(), vmem_spec()),
        compiler_params=limits(8),
        cost_estimate=cost(8 * residual.size, 8 * MIB),
        name="output",
    )(pos, residual, targets, *parts)


def on_device(
    pixels, counts, owner, embed_weight, w_qkv, w_out, w_up, w_down, ln1_gain, ln2_gain, targets
):
    picture = pixels[0]
    devices, cores = lax.axis_size("dp"), lax.axis_size("mp")
    assert cores == 2
    index, m = lax.axis_index("dp"), lax.axis_index("mp")
    dims = ring_dims(devices)
    width = ln1_gain.shape[0]
    columns = width // cores
    lengths, order = counts[0], owner[0]
    length_mine = jnp.where(m == 0, lengths[0], lengths[1])
    length_other = jnp.where(m == 0, lengths[1], lengths[0])
    step_mine = jnp.where(order[0] == m, 0, 1)
    pos = jnp.stack(
        [
            index // (dims[1] * dims[2]),
            index // dims[2] % dims[1],
            index % dims[2],
            m,
            length_mine,
            length_other,
            step_mine,
            jnp.zeros_like(m),
        ]
    ).astype(jnp.int32)
    gain_halves = ln1_gain.reshape(cores, columns)
    gain_one = jnp.where(m == 0, gain_halves, gain_halves[::-1])

    shards = [embed_weight, w_qkv, w_out.T]
    up, down = w_up, w_down.T
    block, block_e = up.shape[0], embed_weight.shape[0]
    bounds = [0, block_e] + [block_e + (i + 1) * block for i in range(4)]
    last = bounds[-1]
    cut, far_cut = last // 2 // TILE * TILE, (last + block_e) // 2 // TILE * TILE
    units = up.shape[1]
    gain_two = ln2_gain.reshape(1, width)

    def picked(chunks, pieces):
        lists = pieces if isinstance(pieces[0], list) else [pieces]
        used = sorted({p[0] for some in lists for p in some})
        moved = [[(used.index(p[0]), *p[1:]) for p in some] for some in lists]
        return [chunks[i].array for i in used], moved if isinstance(pieces[0], list) else moved[0]

    if dims == (4, 2, 2) and block % (2 * TILE) == 0 and block_e % TILE == 0:
        spans = ((0, cut), (cut, last), (block_e, far_cut), (far_cut, last), (0, block_e), (0, far_cut))
        halves = ((0, block // 2), (block // 2, block))
        work = Gather(*pack_order(pack(shards, up, down), up, down), spans, dims)
        work.slot(0)
        other_picture = swap_columns(picture)
        (other_picture,) = work.end_slot(other_picture)
        for number in range(1, 4):
            work.slot(number)
            (other_picture,) = work.end_slot(other_picture)
        chunks, own_pieces = picked(work.early, pieces_of(work.early, spans, (0, block_e)))
        work.slot(4)
        mine = embed(pos, dims, picture, other_picture, chunks, own_pieces, block_e, columns)
        del work.early
        (mine,) = work.end_slot(mine)
        pieces = [pieces_of(work.parts, spans, (bounds[i], bounds[i + 1])) for i in range(5)]
        work.slot(5)
        recv = swap_columns(mine)
        chunks, own_pieces = picked(work.parts, pieces[1:4])
        q, k, v = project(pos, dims, mine, recv, gain_one, chunks, own_pieces, block, width)
        mine, recv, q, k, v = work.end_slot(mine, recv, q, k, v)
        work.slot(6)
        chunks, own_pieces = picked(work.parts, pieces[4])
        keep, send = attention(pos, dims, q, k, v, chunks, own_pieces, block, width)
        mine, recv, keep, send = work.end_slot(mine, recv, keep, send)
        work.slot(7)
        came = swap_columns(send)
        residual, normed = residual_and_norm(pos, mine, recv, keep, came, gain_two)
        residual, normed = work.end_slot(residual, normed)
        work.slot(8)
        normed_came = swap_columns(normed)
        up_pieces = pieces_of(work.up_parts, halves, (0, block))
        hidden = up_layer(
            pos, dims, normed, normed_came, [c.array for c in work.up_parts], up_pieces, block, units
        )
        residual, hidden = work.end_slot(residual, hidden)
        work.slot(9)
        finals, starts = [], []

        def down_part(part):
            own_pieces = pieces_of(part, halves, (0, block))
            spots = sorted({p[3][0] for p in own_pieces})
            starts.append(spots)
            size = width // dims[0] * len(spots)
            kept, sent = down_layer(
                pos, dims, hidden, [c.array for c in part], own_pieces, block, spots[0], size
            )
            return [kept, sent]

        ready = down_part(work.down_parts[0]) + down_part(work.down_parts[1])
        *ready, residual, hidden = work.end_slot(*ready, residual, hidden)
        finals = [ready[0], swap_columns(ready[1]), ready[2], swap_columns(ready[3])]
        kept, sent = down_part(work.down_parts[2])
        finals += [kept, swap_columns(sent)]
    else:
        *w_three, w_last = [
            lax.all_gather(s, "dp", axis=0, tiled=True)
            for s in (embed_weight, w_qkv[0], w_qkv[1], w_qkv[2], w_out.T, up, down)
        ]
        one = lambda w: [(0, 0, w.shape[0], None, 0)]
        mine = embed(
            pos, dims, picture, swap_columns(picture), w_three[:1], one(w_three[0]), block_e, columns
        )
        recv = swap_columns(mine)
        some = [[(i, 0, w.shape[0], None, 0)] for i, w in enumerate(w_three[1:4])]
        q, k, v = project(pos, dims, mine, recv, gain_one, w_three[1:4], some, block, width)
        keep, send = attention(pos, dims, q, k, v, [w_three[4]], one(w_three[4]), block, width)
        came = swap_columns(send)
        residual, normed = residual_and_norm(pos, mine, recv, keep, came, gain_two)
        hidden = up_layer(
            pos, dims, normed, swap_columns(normed), [w_three[5]], one(w_three[5]), block, units
        )
        kept, sent = down_layer(pos, dims, hidden, [w_last], one(w_last), block, None, width)
        finals, starts = [kept, swap_columns(sent)], [[None]]
    encoded, squares = output_layer(pos, residual, targets[0], dims[0], starts, finals)
    number = jnp.sum(lengths).astype(jnp.float32) / cores
    mine_sums = jnp.stack([squares[0, 0], number])
    sums = lax.all_to_all(
        jnp.broadcast_to(mine_sums[None, None, :], (devices * cores, 1, 2)), ("dp", "mp"), 0, 0, tiled=True
    )
    total_squares, total_number = jnp.sum(sums, axis=(0, 1))
    return (encoded[None], total_squares / (width * total_number))


def solution(mesh):
    in_specs = (
        P(("dp", "mp"), None, None),
        P("dp", None),
        P("dp", None),
        P("dp", "mp"),
        P(None, "dp", "mp"),
        P("mp", "dp"),
        P("dp", "mp"),
        P("mp", "dp"),
        P(),
        P(),
        P("dp", None, "mp", None),
    )
    out_specs = (P("dp", None, "mp", None), P())
    return jax.shard_map(
        on_device, mesh=mesh, in_specs=in_specs, out_specs=out_specs, check_vma=False
    )
```

time: 216 us -> 183 us (0.85)
  Pallas kernels: 55.8 us -> 37.5 us
  other arithmetic: 9.85 us -> 4.35 us
  starting transfers between devices: 34.5 us -> 30.9 us
  local copies, waits for them, and re-layouts: 25.3 us -> 22 us
    pallas_call x1, Pallas kernels: 19.6 us -> 7.91 us  [attention(): pl.pallas_call(functools.partial(attention_kernel, n, dims, pieces, block...]
    pallas_call x1, Pallas kernels: 15.4 us -> 6.92 us  [up_layer(): pl.pallas_call(functools.partial(up_kernel, n, dims, pieces, block), out_...]
    pallas_call x0 -> x2, Pallas kernels: none -> 7.68 us  [the longest x1 5.48 us: project(): pl.pallas_call(functools.partial(project_kernel, n, dims, pieces, block),...]
    concatenate x20 -> x9, other arithmetic: 8.42 us -> 2.8 us  [joined(): jnp.concatenate([c.array for c in chunks], 0)]
    unnamed x100 -> x63, local copies, waits for them, and re-layouts: 18.3 us -> 13.3 us
    pallas_call x2 -> x3, Pallas kernels: 13.5 us -> 9.05 us  [down_layer(): pl.pallas_call(functools.partial(down_kernel, n, dims, pieces, block, z_f...]
    ppermute x27 -> x30, starting transfers between devices: 33.8 us -> 29.8 us  [shift(): return lax.ppermute(value, 'dp', pairs)]
    ppermute x27 -> x30, waiting for transfers between devices: 72.7 us -> 70 us  [shift(): return lax.ppermute(value, 'dp', pairs)]
  transfers between devices with their start and end apart: 33 -> 37, of which waited for: 18 -> 25; matrix products, arithmetic and copies ran while one was open for 7% -> 4% of each run, Pallas kernels for 25% -> 19%
where the time goes in v2:
time: 183 us; the launch traced here: 182 us
  waiting for transfers between devices  71.6 us (39%)
  Pallas kernels  37.5 us (20%)
  starting transfers between devices  30.9 us (17%)
  local copies, waits for them, and re-layouts  22 us (12%)
  blocking collectives  8.84 us (5%)
  between operations  7.05 us (4%)
  other arithmetic  4.35 us (2%)
    ppermute x30, waiting for transfers between devices, shift(): return lax.ppermute(value, 'dp', pairs)  70 us
    ppermute x30, starting transfers between devices, shift(): return lax.ppermute(value, 'dp', pairs)  29.8 us
    unnamed x63, local copies, waits for them, and re-layouts  13.3 us
    pallas_call x3, Pallas kernels, down_layer(): pl.pallas_call(functools.partial(down_kernel, n, dims, pieces, block, z_f...  9.05 us
    all_to_all x1, blocking collectives, on_device(): lax.all_to_all(jnp.broadcast_to(mine_sums[None, None, :], (devices * core...  8.84 us
    pallas_call x1, Pallas kernels, attention(): pl.pallas_call(functools.partial(attention_kernel, n, dims, pieces, block...  7.91 us
    pallas_call x1, Pallas kernels, up_layer(): pl.pallas_call(functools.partial(up_kernel, n, dims, pieces, block), out_...  6.92 us
    pallas_call x1, Pallas kernels, project(): pl.pallas_call(functools.partial(project_kernel, n, dims, pieces, block),...  5.48 us
  transfers between devices with their start and end apart: 37, of which 25 were waited for; matrix products, arithmetic and copies ran while one was open for 4% of the time, Pallas kernels for 19%

profile of v2, /device:TPU:0, one launch (start us, length us, event | category | flops | bytes accessed | tf_op | source)
XLA Modules:
  0.0 182.2 jit_solution(3422639805864083479)
XLA Ops:
  1.1 2.2 %pack.1 = (bf16[304,512]{1,0:T(8,128)(2,1)}, bf16[64,2048]{1,0:T(8,128)(2,1)}, bf16[64,2048]{1,0:T(8,128)(2,1)}) custom-call(bf16[48,512]{1,0:T(8,128)(2,1)} %rest_0_.1, bf16[3,64,512]{2,1,0:T(8,128)(2,1)} %rest_1_.1, bf16[64,512]{1,0:T(8,128)(2,1)} %bitcast.29, bf16[64,2048]{1,0:T(8,128)(2,1)} %rest_3_.1, bf16[64,2048]{1,0:T(8,128)(2,1)} %bitcast.27), custom_call_target="tpu_custom_call" | custom-call | bytes 1024 | tf_op jit(solution)/shard_map/pack/pallas_call | solution.py:259
  3.4 2.6 %collective-permute-start = (bf16[304,512]{1,0:T(8,128)(2,1)}, bf16[304,512]{1,0:T(8,128)(2,1)S(1)}, u32[]{:S(2)}, u32[]{:S(2)}) collective-permute-start(bf16[304,512]{1,0:T(8,128)(2,1)} %get-tuple-element.140), channel_id=1, source_target_pairs={{0,8},{2,10},{4,12},{6,14},{8,16},{10,18},{12,20},{14,22},{16,24},... | collective-permute-start | bytes 933896 | tf_op jit(solution)/shard_map/ppermute | solution.py:37
  9.0 5.6 %collective-permute-done.1 = bf16[64,2048]{1,0:T(8,128)(2,1)S(1)} collective-permute-done((bf16[64,2048]{1,0:T(8,128)(2,1)}, bf16[64,2048]{1,0:T(8,128)(2,1)S(1)}, u32[]{:S(2)}, u32[]{:S(2)}) %collective-permute-start.1) | collective-permute-done | bytes 262176 | tf_op jit(solution)/shard_map/ppermute | solution.py:37
  22.9 5.9 %collective-permute-done.4 = bf16[288,512]{1,0:T(8,128)(2,1)S(1)} collective-permute-done((bf16[288,512]{1,0:T(8,128)(2,1)S(1)}, bf16[288,512]{1,0:T(8,128)(2,1)S(1)}, u32[]{:S(2)}, u32[]{:S(2)}) %collective-permute-start.4) | collective-permute-done | bytes 294944 | tf_op jit(solution)/shard_map/ppermute | solution.py:37
  32.6 9.4 %collective-permute-done.9 = bf16[304,512]{1,0:T(8,128)(2,1)S(1)} collective-permute-done((bf16[304,512]{1,0:T(8,128)(2,1)S(1)}, bf16[304,512]{1,0:T(8,128)(2,1)S(1)}, u32[]{:S(2)}, u32[]{:S(2)}) %collective-permute-start.9) | collective-permute-done | bytes 311328 | tf_op jit(solution)/shard_map/ppermute | solution.py:37
  42.0 2.9 %collective-permute-done.7.rest_1_ = bf16[576,512]{1,0:T(8,128)(2,1)S(1)} collective-permute-done((bf16[576,512]{1,0:T(8,128)(2,1)S(1)}, bf16[576,512]{1,0:T(8,128)(2,1)S(1)}, u32[]{:S(2)}, u32[]{:S(2)}) %collective-permute-start.7) | collective-permute-done | bytes 589856 | tf_op jit(solution)/shard_map/ppermute | solution.py:37
  50.6 5.4 %collective-permute-done.11 = bf16[352,512]{1,0:T(8,128)(2,1)S(1)} collective-permute-done((bf16[352,512]{1,0:T(8,128)(2,1)S(1)}, bf16[352,512]{1,0:T(8,128)(2,1)S(1)}, u32[]{:S(2)}, u32[]{:S(2)}) %collective-permute-start.11) | collective-permute-done | bytes 360480 | tf_op jit(solution)/shard_map/ppermute | solution.py:37
  56.0 2.3 %collective-permute-done.13.rest_5_ = bf16[96,512]{1,0:T(8,128)(2,1)S(1)} collective-permute-done((bf16[96,512]{1,0:T(8,128)(2,1)S(1)}, bf16[96,512]{1,0:T(8,128)(2,1)S(1)}, u32[]{:S(2)}, u32[]{:S(2)}) %collective-permute-start.13) | collective-permute-done | bytes 98336 | tf_op jit(solution)/shard_map/ppermute | solution.py:37
  73.1 3.1 %collective-permute-done.14 = bf16[128,2048]{1,0:T(8,128)(2,1)} collective-permute-done((bf16[128,2048]{1,0:T(8,128)(2,1)}, bf16[128,2048]{1,0:T(8,128)(2,1)}, u32[]{:S(2)}, u32[]{:S(2)}) %collective-permute-start.14) | collective-permute-done | bytes 524320 | tf_op jit(solution)/shard_map/ppermute | solution.py:37
  83.6 5.5 %project.1 = (bf16[2,512,512]{2,1,0:T(8,128)(2,1)S(1)}, bf16[2,512,512]{2,1,0:T(8,128)(2,1)S(1)}, bf16[2,512,512]{2,1,0:T(8,128)(2,1)S(1)}) custom-call(s32[8]{0:T(128)S(1)} %stack.37.pos, bf16[2,512,512]{2,1,0:T(8,128)(2,1)S(1)} %embed.1.mine, bf16[2,512,512]{2,1,0:T(8,128)(2,1)S(1)} %collective-permute-done.20.recv, ...), custom_call_target="tpu_custom_call" | custom-call | bytes 1024 | tf_op jit(solution)/shard_map/project/pallas_call | solution.py:333
  89.1 3.7 %collective-permute-done.19.rest_3_ = bf16[128,2048]{1,0:T(8,128)(2,1)} collective-permute-done((bf16[128,2048]{1,0:T(8,128)(2,1)}, bf16[128,2048]{1,0:T(8,128)(2,1)}, u32[]{:S(2)}, u32[]{:S(2)}) %collective-permute-start.19) | collective-permute-done | bytes 524320 | tf_op jit(solution)/shard_map/ppermute | solution.py:37
  94.1 2.0 %collective-permute-done.17 = bf16[128,2048]{1,0:T(8,128)(2,1)} collective-permute-done((bf16[128,2048]{1,0:T(8,128)(2,1)}, bf16[128,2048]{1,0:T(8,128)(2,1)}, u32[]{:S(2)}, u32[]{:S(2)}) %collective-permute-start.17) | collective-permute-done | bytes 524320 | tf_op jit(solution)/shard_map/ppermute | solution.py:37
  101.5 7.9 %attention.1 = (bf16[2,256,1024]{2,1,0:T(8,128)(2,1)S(1)}, bf16[2,256,1024]{2,1,0:T(8,128)(2,1)S(1)}) custom-call(s32[8]{0:T(128)S(1)} %stack.37.pos, bf16[2,512,512]{2,1,0:T(8,128)(2,1)S(1)} %get-tuple-element.207.q, bf16[2,512,512]{2,1,0:T(8,128)(2,1)S(1)} %get-tuple-element.208.k, bf16[2,512,512]{2,1,0:T(8,128)(2,1)S(1)} %get-tuple-element.209.v, ...), custom_call_target="tpu_custom_call" | custom-call | bytes 1024 | tf_op jit(solution)/shard_map/attention/pallas_call | solution.py:384
  109.4 2.0 %collective-permute-done.23.rest_7_ = bf16[128,2048]{1,0:T(8,128)(2,1)S(1)} collective-permute-done((bf16[128,2048]{1,0:T(8,128)(2,1)S(1)}, bf16[128,2048]{1,0:T(8,128)(2,1)S(1)}, u32[]{:S(2)}, u32[]{:S(2)}) %collective-permute-start.23) | collective-permute-done | bytes 524320 | tf_op jit(solution)/shard_map/ppermute | solution.py:37
  112.5 3.1 %collective-permute-done.21 = bf16[128,2048]{1,0:T(8,128)(2,1)S(1)} collective-permute-done((bf16[128,2048]{1,0:T(8,128)(2,1)S(1)}, bf16[128,2048]{1,0:T(8,128)(2,1)S(1)}, u32[]{:S(2)}, u32[]{:S(2)}) %collective-permute-start.21) | collective-permute-done | bytes 524320 | tf_op jit(solution)/shard_map/ppermute | solution.py:37
  121.1 9.1 %collective-permute-done.26.rest_3_ = bf16[128,2048]{1,0:T(8,128)(2,1)S(1)} collective-permute-done((bf16[128,2048]{1,0:T(8,128)(2,1)S(1)}, bf16[128,2048]{1,0:T(8,128)(2,1)S(1)}, u32[]{:S(2)}, u32[]{:S(2)}) %collective-permute-start.26) | collective-permute-done | bytes 524320 | tf_op jit(solution)/shard_map/ppermute | solution.py:37
  130.7 2.1 %collective-permute-done.24 = bf16[128,2048]{1,0:T(8,128)(2,1)S(1)} collective-permute-done((bf16[128,2048]{1,0:T(8,128)(2,1)S(1)}, bf16[128,2048]{1,0:T(8,128)(2,1)S(1)}, u32[]{:S(2)}, u32[]{:S(2)}) %collective-permute-start.24) | collective-permute-done | bytes 524320 | tf_op jit(solution)/shard_map/ppermute | solution.py:37
  135.7 6.9 %up.1.hidden = bf16[2,2,256,2048]{3,2,1,0:T(8,128)(2,1)S(1)} custom-call(s32[8]{0:T(128)S(1)} %stack.37.pos, bf16[2,256,1024]{2,1,0:T(8,128)(2,1)S(1)} %get-tuple-element.242.own, bf16[2,256,1024]{2,1,0:T(8,128)(2,1)S(1)} %collective-permute-done.31.came, bf16[128,2048]{1,0:T(8,128)(2,1)} %pad_maximum_fusion.3.rest_0_, ...), custom_call_target="tpu_custom_call" | custom-call | bytes 1024 | tf_op jit(solution)/shard_map/up/pallas_call | solution.py:466
  142.8 6.1 %collective-permute-done.28 = bf16[128,2048]{1,0:T(8,128)(2,1)S(1)} collective-permute-done((bf16[128,2048]{1,0:T(8,128)(2,1)S(1)}, bf16[128,2048]{1,0:T(8,128)(2,1)S(1)}, u32[]{:S(2)}, u32[]{:S(2)}) %collective-permute-start.28) | collective-permute-done | bytes 524320 | tf_op jit(solution)/shard_map/ppermute | solution.py:37
  151.8 2.6 %down.4 = (bf16[2,256,256]{2,1,0:T(8,128)(2,1)S(1)}, bf16[2,256,256]{2,1,0:T(8,128)(2,1)}) custom-call(s32[8]{0:T(128)S(1)} %stack.37.pos, bf16[2,2,256,2048]{3,2,1,0:T(8,128)(2,1)S(1)} %up.1.hidden, bf16[64,2048]{1,0:T(8,128)(2,1)S(1)} %get-tuple-element.248.rest_0_, bf16[64,2048]{1,0:T(8,128)(2,1)S(1)} %collective-permute-done.29.rest_1_, ...), custom_call_target="tpu_custom_call" | custom-call | bytes 1024 | tf_op jit(solution)/shard_map/down/pallas_call | solution.py:490
  154.4 3.9 %down.3 = (bf16[2,256,512]{2,1,0:T(8,128)(2,1)S(1)}, bf16[2,256,512]{2,1,0:T(8,128)(2,1)}) custom-call(s32[8]{0:T(128)S(1)} %stack.37.pos, bf16[2,2,256,2048]{3,2,1,0:T(8,128)(2,1)S(1)} %up.1.hidden, bf16[128,2048]{1,0:T(8,128)(2,1)S(1)} %pad_maximum_fusion.7.rest_0_, bf16[128,2048]{1,0:T(8,128)(2,1)S(1)} %collective-permute-done.25.rest_1_, ...), custom_call_target="tpu_custom_call" | custom-call | bytes 1024 | tf_op jit(solution)/shard_map/down/pallas_call | solution.py:490
  158.4 2.6 %down.5 = (bf16[2,256,256]{2,1,0:T(8,128)(2,1)S(1)}, bf16[2,256,256]{2,1,0:T(8,128)(2,1)}) custom-call(s32[8]{0:T(128)S(1)} %stack.37.pos, bf16[2,2,256,2048]{3,2,1,0:T(8,128)(2,1)S(1)} %up.1.hidden, bf16[64,2048]{1,0:T(8,128)(2,1)S(1)} %get-tuple-element.264.rest_0_, bf16[64,2048]{1,0:T(8,128)(2,1)S(1)} %collective-permute-done.32.rest_1_, ...), custom_call_target="tpu_custom_call" | custom-call | bytes 1024 | tf_op jit(solution)/shard_map/down/pallas_call | solution.py:490
  166.1 2.8 %output.1 = (bf16[2,256,1024]{2,1,0:T(8,128)(2,1)}, f32[8,128]{1,0:T(8,128)S(1)}) custom-call(s32[8]{0:T(128)S(1)} %stack.37.pos, f32[2,256,1024]{2,1,0:T(8,128)S(1)} %copy-done.10, bf16[2,256,1024]{2,1,0:T(8,128)(2,1)S(1)} %bitcast.22, bf16[2,256,512]{2,1,0:T(8,128)(2,1)S(1)} %copy-done.18, bf16[2,256,512]{2,1,0:T(8,128)(2,1)} %collective-permute-done.34.rest_1_, ...), custom_call_target="tpu_custom_call" | custom-call | bytes 1024 | tf_op jit(solution)/shard_map/output/pallas_call | solution.py:533
  170.2 8.8 %all_to_all.5 = f32[32,1,2]{2,1,0:T(1,128)S(1)} all-to-all(f32[32,1,2]{2,1,0:T(1,128)S(1)} %broadcast_in_dim.10), channel_id=1, replica_groups=mesh['dp'=16,'mp'=2] {'dp','mp'}, dimensions={0} | all-to-all | bytes 512 | tf_op jit(solution)/shard_map/all_to_all | solution.py:668
  (176 shorter events, 66.6 us)
Async XLA Ops:
  0.6 15.6 %collective-permute-start.3 = (bf16[512,768]{1,0:T(8,128)(2,1)}, bf16[512,768]{1,0:T(8,128)(2,1)S(1)}, u32[]{:S(2)}, u32[]{:S(2)}) collective-permute-start(bf16[512,768]{1,0:T(8,128)(2,1)} %bitcast.23), channel_id=1, source_target_pairs={{0,1},{1,0},{2,3},{3,2},{4,5},{5,4},{6,7},{7,6},{8,9},{9,8},{10,11... | collective-permute-start | bytes 2359304 | tf_op jit(solution)/shard_map/ppermute | solution.py:69
  3.4 12.9 %collective-permute-start = (bf16[304,512]{1,0:T(8,128)(2,1)}, bf16[304,512]{1,0:T(8,128)(2,1)S(1)}, u32[]{:S(2)}, u32[]{:S(2)}) collective-permute-start(bf16[304,512]{1,0:T(8,128)(2,1)} %get-tuple-element.140), channel_id=1, source_target_pairs={{0,8},{2,10},{4,12},{6,14},{8,16},{10,18},{12,20},{14,22},{16,24},... | collective-permute-start | bytes 933896 | tf_op jit(solution)/shard_map/ppermute | solution.py:37
  18.4 11.0 %collective-permute-start.6 = (bf16[304,512]{1,0:T(8,128)(2,1)S(1)}, bf16[304,512]{1,0:T(8,128)(2,1)S(1)}, u32[]{:S(2)}, u32[]{:S(2)}) collective-permute-start(bf16[304,512]{1,0:T(8,128)(2,1)S(1)} %collective-permute-done), channel_id=1, source_target_pairs={{0,8},{2,10},{4,12},{6,14},{8,16},{10,18},{12,20},{14,22},{16,24},... | collective-permute-start | bytes 933896 | tf_op jit(solution)/shard_map/ppermute | solution.py:37
  19.7 9.8 %collective-permute-start.5 = (bf16[320,512]{1,0:T(8,128)(2,1)S(1)}, bf16[320,512]{1,0:T(8,128)(2,1)S(1)}, u32[]{:S(2)}, u32[]{:S(2)}) collective-permute-start(bf16[320,512]{1,0:T(8,128)(2,1)S(1)} %pad_maximum_fusion.11), channel_id=1, source_target_pairs={{0,4},{2,6},{4,0},{6,2},{8,12},{10,14},{12,8},{14,10},{16,20},{18,... | collective-permute-start | bytes 983048 | tf_op jit(solution)/shard_map/ppermute | solution.py:37
  29.5 16.2 %collective-permute-start.8 = (bf16[640,512]{1,0:T(8,128)(2,1)S(1)}, bf16[640,512]{1,0:T(8,128)(2,1)S(1)}, u32[]{:S(2)}, u32[]{:S(2)}) collective-permute-start(bf16[640,512]{1,0:T(8,128)(2,1)S(1)} %constant_dynamic-update-slice_fusion.2.rest_2_.rest_0_), channel_id=1, source_target_pairs={{0,2},{2,0},{4,6},{6,4},{8,10},{10,8},{12,14},{14,12},{16,18},{18,... | collective-permute-start | bytes 1966088 | tf_op jit(solution)/shard_map/ppermute | solution.py:37
  31.0 13.9 %collective-permute-start.7 = (bf16[576,512]{1,0:T(8,128)(2,1)S(1)}, bf16[576,512]{1,0:T(8,128)(2,1)S(1)}, u32[]{:S(2)}, u32[]{:S(2)}) collective-permute-start(bf16[576,512]{1,0:T(8,128)(2,1)S(1)} %constant_dynamic-update-slice_fusion.rest_0_), channel_id=1, source_target_pairs={{0,4},{2,6},{4,0},{6,2},{8,12},{10,14},{12,8},{14,10},{16,20},{18,... | collective-permute-start | bytes 1769480 | tf_op jit(solution)/shard_map/ppermute | solution.py:37
  32.6 9.4 %collective-permute-start.9 = (bf16[304,512]{1,0:T(8,128)(2,1)S(1)}, bf16[304,512]{1,0:T(8,128)(2,1)S(1)}, u32[]{:S(2)}, u32[]{:S(2)}) collective-permute-start(bf16[304,512]{1,0:T(8,128)(2,1)S(1)} %collective-permute-done.6), channel_id=1, source_target_pairs={{0,8},{2,10},{4,12},{6,14},{8,16},{10,18},{12,20},{14,22},{16,24},... | collective-permute-start | bytes 933896 | tf_op jit(solution)/shard_map/ppermute | solution.py:37
  46.7 13.5 %collective-permute-start.12 = (bf16[128,2048]{1,0:T(8,128)(2,1)S(1)}, bf16[128,2048]{1,0:T(8,128)(2,1)}, u32[]{:S(2)}, u32[]{:S(2)}) collective-permute-start(bf16[128,2048]{1,0:T(8,128)(2,1)S(1)} %pad_maximum_fusion.1), channel_id=1, source_target_pairs={{0,8},{2,10},{4,12},{6,14},{8,16},{10,18},{12,20},{14,22},{16,24},... | collective-permute-start | bytes 1572872 | tf_op jit(solution)/shard_map/ppermute | solution.py:37
  48.4 9.9 %collective-permute-start.10 = (bf16[352,512]{1,0:T(8,128)(2,1)S(1)}, bf16[352,512]{1,0:T(8,128)(2,1)S(1)}, u32[]{:S(2)}, u32[]{:S(2)}) collective-permute-start(bf16[352,512]{1,0:T(8,128)(2,1)S(1)} %pad_maximum_fusion.9.rest_2_), channel_id=1, source_target_pairs={{0,2},{2,0},{4,6},{6,4},{8,10},{10,8},{12,14},{14,12},{16,18},{18,... | collective-permute-start | bytes 1081352 | tf_op jit(solution)/shard_map/ppermute | solution.py:37
  60.2 12.8 %collective-permute-start.16 = (bf16[512,512]{1,0:T(8,128)(2,1)S(1)}, bf16[512,512]{1,0:T(8,128)(2,1)}, u32[]{:S(2)}, u32[]{:S(2)}) collective-permute-start(bf16[512,512]{1,0:T(8,128)(2,1)S(1)} %constant_dynamic-update-slice_fusion.4.rest_6_.rest_2_), channel_id=1, source_target_pairs={{0,2},{2,0},{4,6},{6,4},{8,10},{10,8},{12,14},{14,12},{16,18},{18,... | collective-permute-start | bytes 1572872 | tf_op jit(solution)/shard_map/ppermute | solution.py:37
  62.2 10.9 %collective-permute-start.15 = (bf16[512,512]{1,0:T(8,128)(2,1)}, bf16[512,512]{1,0:T(8,128)(2,1)}, u32[]{:S(2)}, u32[]{:S(2)}) collective-permute-start(bf16[512,512]{1,0:T(8,128)(2,1)} %bitcast.14.rest_4_), channel_id=1, source_target_pairs={{0,4},{2,6},{4,0},{6,2},{8,12},{10,14},{12,8},{14,10},{16,20},{18,... | collective-permute-start | bytes 1572872 | tf_op jit(solution)/shard_map/ppermute | solution.py:37
  63.7 12.4 %collective-permute-start.14 = (bf16[128,2048]{1,0:T(8,128)(2,1)}, bf16[128,2048]{1,0:T(8,128)(2,1)}, u32[]{:S(2)}, u32[]{:S(2)}) collective-permute-start(bf16[128,2048]{1,0:T(8,128)(2,1)} %collective-permute-done.12), channel_id=1, source_target_pairs={{0,8},{2,10},{4,12},{6,14},{8,16},{10,18},{12,20},{14,22},{16,24},... | collective-permute-start | bytes 1572872 | tf_op jit(solution)/shard_map/ppermute | solution.py:37
  78.2 14.7 %collective-permute-start.19 = (bf16[128,2048]{1,0:T(8,128)(2,1)}, bf16[128,2048]{1,0:T(8,128)(2,1)}, u32[]{:S(2)}, u32[]{:S(2)}) collective-permute-start(bf16[128,2048]{1,0:T(8,128)(2,1)} %pad_maximum_fusion.4.rest_2_), channel_id=1, source_target_pairs={{0,2},{2,0},{4,6},{6,4},{8,10},{10,8},{12,14},{14,12},{16,18},{18,... | collective-permute-start | bytes 1572872 | tf_op jit(solution)/shard_map/ppermute | solution.py:37
  79.7 14.4 %collective-permute-start.18 = (bf16[128,2048]{1,0:T(8,128)(2,1)}, bf16[128,2048]{1,0:T(8,128)(2,1)}, u32[]{:S(2)}, u32[]{:S(2)}) collective-permute-start(bf16[128,2048]{1,0:T(8,128)(2,1)} %pad_maximum_fusion.3.rest_0_), channel_id=1, source_target_pairs={{0,4},{2,6},{4,0},{6,2},{8,12},{10,14},{12,8},{14,10},{16,20},{18,... | collective-permute-start | bytes 1572872 | tf_op jit(solution)/shard_map/ppermute | solution.py:37
  80.2 15.9 %collective-permute-start.17 = (bf16[128,2048]{1,0:T(8,128)(2,1)}, bf16[128,2048]{1,0:T(8,128)(2,1)}, u32[]{:S(2)}, u32[]{:S(2)}) collective-permute-start(bf16[128,2048]{1,0:T(8,128)(2,1)} %collective-permute-done.14), channel_id=1, source_target_pairs={{0,8},{2,10},{4,12},{6,14},{8,16},{10,18},{12,20},{14,22},{16,24},... | collective-permute-start | bytes 1572872 | tf_op jit(solution)/shard_map/ppermute | solution.py:37
  98.5 13.0 %collective-permute-start.23 = (bf16[128,2048]{1,0:T(8,128)(2,1)S(1)}, bf16[128,2048]{1,0:T(8,128)(2,1)S(1)}, u32[]{:S(2)}, u32[]{:S(2)}) collective-permute-start(bf16[128,2048]{1,0:T(8,128)(2,1)S(1)} %pad_maximum_fusion.6.rest_6_), channel_id=1, source_target_pairs={{0,2},{2,0},{4,6},{6,4},{8,10},{10,8},{12,14},{14,12},{16,18},{18,... | collective-permute-start | bytes 1572872 | tf_op jit(solution)/shard_map/ppermute | solution.py:37
  99.8 12.7 %collective-permute-start.22 = (bf16[128,2048]{1,0:T(8,128)(2,1)S(1)}, bf16[128,2048]{1,0:T(8,128)(2,1)S(1)}, u32[]{:S(2)}, u32[]{:S(2)}) collective-permute-start(bf16[128,2048]{1,0:T(8,128)(2,1)S(1)} %pad_maximum_fusion.5.rest_4_), channel_id=1, source_target_pairs={{0,4},{2,6},{4,0},{6,2},{8,12},{10,14},{12,8},{14,10},{16,20},{18,... | collective-permute-start | bytes 1572872 | tf_op jit(solution)/shard_map/ppermute | solution.py:37
  101.5 14.2 %collective-permute-start.21 = (bf16[128,2048]{1,0:T(8,128)(2,1)S(1)}, bf16[128,2048]{1,0:T(8,128)(2,1)S(1)}, u32[]{:S(2)}, u32[]{:S(2)}) collective-permute-start(bf16[128,2048]{1,0:T(8,128)(2,1)S(1)} %copy-done.22), channel_id=1, source_target_pairs={{0,8},{2,10},{4,12},{6,14},{8,16},{10,18},{12,20},{14,22},{16,24},... | collective-permute-start | bytes 1572872 | tf_op jit(solution)/shard_map/ppermute | solution.py:37
  115.8 14.4 %collective-permute-start.26 = (bf16[128,2048]{1,0:T(8,128)(2,1)S(1)}, bf16[128,2048]{1,0:T(8,128)(2,1)S(1)}, u32[]{:S(2)}, u32[]{:S(2)}) collective-permute-start(bf16[128,2048]{1,0:T(8,128)(2,1)S(1)} %pad_maximum_fusion.8.rest_2_), channel_id=1, source_target_pairs={{0,2},{2,0},{4,6},{6,4},{8,10},{10,8},{12,14},{14,12},{16,18},{18,... | collective-permute-start | bytes 1572872 | tf_op jit(solution)/shard_map/ppermute | solution.py:37
  116.6 14.1 %collective-permute-start.25 = (bf16[128,2048]{1,0:T(8,128)(2,1)S(1)}, bf16[128,2048]{1,0:T(8,128)(2,1)S(1)}, u32[]{:S(2)}, u32[]{:S(2)}) collective-permute-start(bf16[128,2048]{1,0:T(8,128)(2,1)S(1)} %pad_maximum_fusion.7.rest_0_), channel_id=1, source_target_pairs={{0,4},{2,6},{4,0},{6,2},{8,12},{10,14},{12,8},{14,10},{16,20},{18,... | collective-permute-start | bytes 1572872 | tf_op jit(solution)/shard_map/ppermute | solution.py:37
  117.2 15.6 %collective-permute-start.24 = (bf16[128,2048]{1,0:T(8,128)(2,1)S(1)}, bf16[128,2048]{1,0:T(8,128)(2,1)S(1)}, u32[]{:S(2)}, u32[]{:S(2)}) collective-permute-start(bf16[128,2048]{1,0:T(8,128)(2,1)S(1)} %collective-permute-done.21), channel_id=1, source_target_pairs={{0,8},{2,10},{4,12},{6,14},{8,16},{10,18},{12,20},{14,22},{16,24},... | collective-permute-start | bytes 1572872 | tf_op jit(solution)/shard_map/ppermute | solution.py:37
  132.8 16.1 %collective-permute-start.28 = (bf16[128,2048]{1,0:T(8,128)(2,1)S(1)}, bf16[128,2048]{1,0:T(8,128)(2,1)S(1)}, u32[]{:S(2)}, u32[]{:S(2)}) collective-permute-start(bf16[128,2048]{1,0:T(8,128)(2,1)S(1)} %collective-permute-done.24), channel_id=1, source_target_pairs={{0,8},{2,10},{4,12},{6,14},{8,16},{10,18},{12,20},{14,22},{16,24},... | collective-permute-start | bytes 1572872 | tf_op jit(solution)/shard_map/ppermute | solution.py:37
  132.8 9.8 %collective-permute-start.29 = (bf16[64,2048]{1,0:T(8,128)(2,1)S(1)}, bf16[64,2048]{1,0:T(8,128)(2,1)S(1)}, u32[]{:S(2)}, u32[]{:S(2)}) collective-permute-start(bf16[64,2048]{1,0:T(8,128)(2,1)S(1)} %get-tuple-element.248.rest_0_), channel_id=1, source_target_pairs={{0,4},{2,6},{4,0},{6,2},{8,12},{10,14},{12,8},{14,10},{16,20},{18,... | collective-permute-start | bytes 786440 | tf_op jit(solution)/shard_map/ppermute | solution.py:37
  149.0 9.3 %collective-permute-start.32 = (bf16[64,2048]{1,0:T(8,128)(2,1)S(1)}, bf16[64,2048]{1,0:T(8,128)(2,1)S(1)}, u32[]{:S(2)}, u32[]{:S(2)}) collective-permute-start(bf16[64,2048]{1,0:T(8,128)(2,1)S(1)} %get-tuple-element.264.rest_0_), channel_id=1, source_target_pairs={{0,4},{2,6},{4,0},{6,2},{8,12},{10,14},{12,8},{14,10},{16,20},{18,... | collective-permute-start | bytes 786440 | tf_op jit(solution)/shard_map/ppermute | solution.py:37
  (43 other events, 210.7 us)

commit v3 on v2

--- a/solution.py
+++ b/solution.py
@@ -9,6 +9,7 @@
 
 HEAD = 64
 TILE = 16
+SPARE = 8
 Z, Y, X = 0, 1, 2
 MIB = 1 << 20
 POS_Z, POS_Y, POS_X, POS_M, POS_LEN, POS_STEP = 0, 1, 2, 3, 4, 6
@@ -38,31 +39,53 @@
 
 
 class Chunk:
-    def __init__(self, array, slots, half):
-        self.array, self.slots, self.half = array, slots, half
-        self.rows = array.shape[0] // len(slots)
-
-    def moved(self, array, axis, by=1):
-        slots = [tuple(v + by * (i == axis) for i, v in enumerate(s)) for s in self.slots]
-        return Chunk(array, slots, self.half)
-
-    def part(self, first, last):
-        return Chunk(
-            self.array[first * self.rows : last * self.rows], self.slots[first:last], self.half
-        )
-
-
-    def without(self, rows, half):
-        value = self.array.reshape(len(self.slots), self.rows, -1)[:, rows:]
-        return Chunk(value.reshape(-1, value.shape[2]), self.slots, half)
-
-
-def joined(chunks):
-    if len(chunks) == 1:
-        return chunks[0]
-    return Chunk(
-        jnp.concatenate([c.array for c in chunks], 0), sum((c.slots for c in chunks), []), chunks[0].half
-    )
+    def __init__(self, array, slots, half, rows, base=0):
+        self.array, self.slots, self.half, self.rows, self.base = array, slots, half, rows, base
+
+    def moved(self, array, axis):
+        slots = [tuple(v + (i == axis) for i, v in enumerate(s)) for s in self.slots]
+        return Chunk(array, slots, self.half, self.rows, self.base)
+
+    def block(self, i, first=0, last=None):
+        last = self.rows if last is None else last
+        return (self.array, self.base + i * self.rows + first, last - first)
+
+    def all(self, first=0, last=None):
+        return [self.block(i, first, last) for i in range(len(self.slots))]
+
+
+def stack_kernel(plan, *refs):
+    sources, results = refs[: -len(plan)], refs[-len(plan) :]
+    for result, taken in zip(results, plan, strict=True):
+        at = 0
+        for number, row, rows in taken:
+            result[pl.ds(at, rows), :] = sources[number][pl.ds(row, rows), :]
+            at += rows
+
+
+def stack(*results):
+    sources = []
+    for taken in results:
+        for array, _, _ in taken:
+            if all(array is not other for other in sources):
+                sources.append(array)
+
+    def number(array):
+        return next(i for i, other in enumerate(sources) if other is array)
+
+    plan = [[(number(array), row, rows) for array, row, rows in taken] for taken in results]
+    return pl.pallas_call(
+        functools.partial(stack_kernel, plan),
+        out_shape=tuple(
+            jax.ShapeDtypeStruct((sum(rows for _, _, rows in taken), taken[0][0].shape[1]), taken[0][0].dtype)
+            for taken in results
+        ),
+        in_specs=[vmem_spec()] * len(sources),
+        out_specs=(vmem_spec(),) * len(results),
+        compiler_params=limits(8),
+        cost_estimate=cost(0, 2 * MIB),
+        name="stack",
+    )(*sources)
 
 
 def swap_columns(value):
@@ -70,9 +93,9 @@
 
 
 class Gather:
-    def __init__(self, first, up, down, side_a, side_b, spans, dims):
-        self.dims, self.spans, self.half = dims, spans, up.shape[0] // 2
-        self.first, self.up, self.down, self.side_a, self.side_b = first, up, down, side_a, side_b
+    def __init__(self, first, side_a, side_b, spans, dims):
+        self.dims, self.spans, self.half = dims, spans, side_a.shape[0] // 2
+        self.first, self.side_a, self.side_b = first, side_a, side_b
 
     def move(self, value, axis):
         return shift(value, self.dims, axis)
@@ -80,32 +103,28 @@
     def step(self, chunk, axis):
         return chunk.moved(shift(chunk.array, self.dims, axis), axis)
 
-    def first_ends(self, blocks, low, kinds):
-        slots = [(low + i, 0, 0) for i in range(len(blocks))]
-        made = []
-        for kind in kinds:
-            begin, end = self.spans[kind]
-            made.append(Chunk(jnp.concatenate([v[begin:end] for v in blocks], 0), slots, kind))
-        return made
-
-    def whole(self, shard, k):
+    def whole(self, k):
         half = self.half
-        rows = slice(k * half, (k + 1) * half)
-        here = [(0, 0, 0)]
-        return joined(
-            [
-                Chunk(shard[:half], here, 0),
-                Chunk(self.from_x[rows], [(0, 0, 1)], 0),
-                Chunk(shard[half:], here, 1),
-                Chunk(self.from_y[rows], [(0, 1, 0)], 1),
-            ]
+        sides = (self.side_a, self.from_x, self.side_b, self.from_y)
+        return [(side, k * half, half) for side in sides] + [(self.side_a, 0, SPARE)] * (SPARE > 0)
+
+    def ends(self, low, kind):
+        first, last = self.spans[kind]
+        return [(v, first, last - first) for v in self.first_z[low : low + 2]]
+
+    def chunk(self, array, slots, kind):
+        return Chunk(array, slots, kind, self.spans[kind][1] - self.spans[kind][0])
+
+    def both(self, a, b):
+        return [a, self.step(a, Y), b, self.step(b, X)]
+
+    def last(self, blocks):
+        a, b = stack(
+            [c.block(i) for c in blocks for i in (0, 1)], [c.block(i) for c in blocks for i in (2, 3)]
         )
-
-    def halves(self, blocks):
-        a = joined([c.part(0, 2) for c in blocks])
-        b = joined([c.part(2, 4) for c in blocks])
-        b.half = 1
-        return a, b
+        a = Chunk(a, sum((c.slots[:2] for c in blocks), []), 0, self.half)
+        b = Chunk(b, sum((c.slots[2:] for c in blocks), []), 1, self.half)
+        return self.both(a, b)
 
     def slot(self, number):
         if number == 0:
@@ -113,27 +132,37 @@
             self.from_x, self.from_y = self.move(self.side_a, X), self.move(self.side_b, Y)
         elif number == 1:
             self.first_z.append(self.move(self.first_z[-1], Z))
-            self.a, self.b = self.first_ends(self.first_z[:2], 0, (0, 1))
+            near = [(0, 0, 0), (1, 0, 0)]
+            a, b = stack(self.ends(0, 0), self.ends(0, 1))
+            self.a, self.b = self.chunk(a, near, 0), self.chunk(b, near, 1)
             self.a_far, self.b_far = self.step(self.a, X), self.step(self.b, Y)
-            self.up_z, self.down_z = [self.whole(self.up, 0)], [self.whole(self.down, 1)]
+            up, down = stack(self.whole(0), self.whole(1))
+            own = [(0, 0, 0), (0, 0, 1), (0, 0, 0), (0, 1, 0)]
+            self.up_z, self.down_z = [Chunk(up, own, 0, self.half)], [Chunk(down, own, 0, self.half)]
         elif number == 2:
             self.first_z.append(self.move(self.first_z[-1], Z))
-            self.a, self.b = joined([self.a, self.a_far]), joined([self.b, self.b_far])
-            self.parts = [self.a, self.step(self.a, Y), self.b, self.step(self.b, X)]
+            del self.side_a, self.side_b, self.from_x, self.from_y
+            a, b = stack(self.a.all() + self.a_far.all(), self.b.all() + self.b_far.all())
+            self.a = self.chunk(a, self.a.slots + self.a_far.slots, 0)
+            self.b = self.chunk(b, self.b.slots + self.b_far.slots, 1)
+            self.parts = self.both(self.a, self.b)
         elif number == 3:
             self.up_z.append(self.step(self.up_z[-1], Z))
-            self.a, self.b, own = self.first_ends(self.first_z[2:], 2, (5, 3, 4))
-            corner = Chunk(shift(own.array, self.dims, X, Y), [(z, 1, 1) for z, _, _ in own.slots], 4)
-            self.a_far = self.step(self.a, X)
-            rows = self.b.array.shape[0]
-            mixed = self.move(jnp.concatenate([self.b.array, own.array], 0), Y)
-            self.b_far, own_far = self.b.moved(mixed[:rows], Y), own.moved(mixed[rows:], Y)
+            far = [(2, 0, 0), (3, 0, 0)]
+            a, b, own = stack(self.ends(2, 5), self.ends(2, 3) + self.ends(2, 4), self.ends(2, 4))
+            self.a, self.b = self.chunk(a, far, 5), self.chunk(b, far, 3)
+            self.a_far, self.b_far = self.step(self.a, X), self.step(self.b, Y)
+            corner = self.chunk(shift(own, self.dims, X, Y), [(2, 1, 1), (3, 1, 1)], 4)
+            own_far = self.chunk(self.b_far.array, [(2, 1, 0), (3, 1, 0)], 4)
+            own_far.base = 2 * self.b.rows
             self.early = self.parts[:2] + [self.a, self.a_far, own_far, corner]
         elif number == 4:
             self.up_z.append(self.step(self.up_z[-1], Z))
-            self.a, self.b = joined([self.a, self.a_far]), joined([self.b, self.b_far])
-            self.a = self.a.without(self.spans[5][1] - self.spans[2][1] + self.spans[2][0], 2)
-            self.parts += [self.a, self.step(self.a, Y), self.b, self.step(self.b, X)]
+            first = self.spans[2][0] - self.spans[5][0]
+            a, b = stack(self.a.all(first) + self.a_far.all(first), self.b.all() + self.b_far.all())
+            self.a = self.chunk(a, self.a.slots + self.a_far.slots, 2)
+            self.b = self.chunk(b, self.b.slots + self.b_far.slots, 3)
+            self.parts += self.both(self.a, self.b)
         elif number == 5:
             self.up_parts = self.last(self.up_z[:2])
             self.up_z.append(self.step(self.up_z[-1], Z))
@@ -149,10 +178,6 @@
         elif number == 9:
             self.down_parts.append(self.last(self.down_z[3:]))
 
-    def last(self, blocks):
-        a, b = self.halves(blocks)
-        return [a, self.step(a, Y), b, self.step(b, X)]
-
     def end_slot(self, *others):
         chunks, arrays = [], []
         for name, value in vars(self).items():
@@ -163,11 +188,13 @@
                             chunks.append(w)
                     elif isinstance(w, jax.Array):
                         arrays.append((name, i, w))
-        together = lax.optimization_barrier(
-            (tuple(c.array for c in chunks), tuple(w for _, _, w in arrays), others)
-        )
-        for c, new in zip(chunks, together[0], strict=True):
-            c.array = new
+        held = []
+        for c in chunks:
+            if all(c.array is not w for w in held):
+                held.append(c.array)
+        together = lax.optimization_barrier((tuple(held), tuple(w for _, _, w in arrays), others))
+        for c in chunks:
+            c.array = together[0][next(i for i, w in enumerate(held) if w is c.array)]
         for (name, i, _), new in zip(arrays, together[1], strict=True):
             if isinstance(vars(self)[name], list):
                 vars(self)[name][i] = new
@@ -183,7 +210,8 @@
         low, high = max(first, segment[0]), min(last, segment[1])
         if low < high:
             for i, slot in enumerate(chunk.slots):
-                found.append((number, i * chunk.rows + low - first, high - low, slot, low - segment[0]))
+                row = chunk.base + i * chunk.rows + low - first
+                found.append((number, row, high - low, slot, low - segment[0]))
     return found
 
 
@@ -266,11 +294,6 @@
         cost_estimate=cost(0, 2 * MIB),
         name="pack",
     )(*shards, up, down)
-
-
-def pack_order(packed, up, down):
-    first, side_a, side_b = packed
-    return first, up, down, side_a, side_b
 
 
 def embed_kernel(n, dims, pieces, block, pos, mine, other, *rest):
@@ -499,16 +522,21 @@
     )(pos, hidden, *chunks)
 
 
-def output_kernel(n, nz, starts, pos, residual, targets, *rest):
-    parts, (encoded, squares) = rest[:n], rest[n:]
+def output_kernel(n, nz, starts, ending, pos, residual, targets, *rest):
+    parts, (encoded, sums) = rest[:n], rest[-2:]
     m = pos[POS_M]
     rows = residual.shape[1]
     total = jnp.zeros((), jnp.float32)
     row_ids = m * rows + lax.broadcasted_iota(jnp.int32, (rows, 1), 0)
+    if ending:
+        before, total_before = rest[n : n + 2]
+        number = (pos[POS_LEN] + pos[POS_LEN + 1]).astype(jnp.float32) * 0.5
+        encoded[...] = before[...]
+        total = total_before[0, 0]
     for i in range(2):
         s = pos[POS_STEP] if i == 0 else 1 - pos[POS_STEP]
         usable = row_ids < pos[POS_LEN + i]
-        sums = jnp.zeros((rows, 1), jnp.float32)
+        found = jnp.zeros((rows, 1), jnp.float32)
         for j, spots in enumerate(starts):
             keep, came = parts[2 * j], parts[2 * j + 1]
             size = keep.shape[2] // len(spots)
@@ -524,24 +552,30 @@
                 )
                 encoded[s, :, place] = value.astype(encoded.dtype)
                 misfit = value - targets[s, :, place].astype(jnp.float32)
-                sums = sums + jnp.sum(misfit * misfit, axis=-1, keepdims=True)
-        total = total + jnp.sum(jnp.where(usable, sums, 0.0))
-    squares[...] = jnp.full(squares.shape, total, jnp.float32)
-
-
-def output_layer(pos, residual, targets, nz, starts, parts):
-    return pl.pallas_call(
-        functools.partial(output_kernel, len(parts), nz, starts),
+                found = found + jnp.sum(misfit * misfit, axis=-1, keepdims=True)
+        total = total + jnp.sum(jnp.where(usable, found, 0.0))
+    if ending:
+        lane = lax.broadcasted_iota(jnp.int32, sums.shape, 2)
+        sums[...] = jnp.where(lane == 0, total, number)
+    else:
+        sums[...] = jnp.full(sums.shape, total, jnp.float32)
+
+
+def output_layer(pos, residual, targets, nz, starts, parts, ending=(), devices=0):
+    sums = (devices, 1, 2) if ending else (8, 128)
+    specs = [vmem_spec(), vmem_spec()] if ending else []
+    return pl.pallas_call(
+        functools.partial(output_kernel, len(parts), nz, starts, bool(ending)),
         out_shape=(
             jax.ShapeDtypeStruct(residual.shape, targets.dtype),
-            jax.ShapeDtypeStruct((8, 128), jnp.float32),
+            jax.ShapeDtypeStruct(sums, jnp.float32),
         ),
-        in_specs=[smem_spec()] + [vmem_spec()] * (2 + len(parts)),
+        in_specs=[smem_spec()] + [vmem_spec()] * (2 + len(parts)) + specs,
         out_specs=(vmem_spec(), vmem_spec()),
         compiler_params=limits(8),
         cost_estimate=cost(8 * residual.size, 8 * MIB),
         name="output",
-    )(pos, residual, targets, *parts)
+    )(pos, residual, targets, *parts, *ending)
 
 
 def on_device(
@@ -591,7 +625,7 @@
     if dims == (4, 2, 2) and block % (2 * TILE) == 0 and block_e % TILE == 0:
         spans = ((0, cut), (cut, last), (block_e, far_cut), (far_cut, last), (0, block_e), (0, far_cut))
         halves = ((0, block // 2), (block // 2, block))
-        work = Gather(*pack_order(pack(shards, up, down), up, down), spans, dims)
+        work = Gather(*pack(shards, up, down), spans, dims)
         work.slot(0)
         other_picture = swap_columns(picture)
         (other_picture,) = work.end_slot(other_picture)
@@ -641,7 +675,7 @@
         *ready, residual, hidden = work.end_slot(*ready, residual, hidden)
         finals = [ready[0], swap_columns(ready[1]), ready[2], swap_columns(ready[3])]
         kept, sent = down_part(work.down_parts[2])
-        finals += [kept, swap_columns(sent)]
+        last = [kept, swap_columns(sent)]
     else:
         *w_three, w_last = [
             lax.all_gather(s, "dp", axis=0, tiled=True)
@@ -661,13 +695,23 @@
             pos, dims, normed, swap_columns(normed), [w_three[5]], one(w_three[5]), block, units
         )
         kept, sent = down_layer(pos, dims, hidden, [w_last], one(w_last), block, None, width)
-        finals, starts = [kept, swap_columns(sent)], [[None]]
-    encoded, squares = output_layer(pos, residual, targets[0], dims[0], starts, finals)
-    number = jnp.sum(lengths).astype(jnp.float32) / cores
-    mine_sums = jnp.stack([squares[0, 0], number])
-    sums = lax.all_to_all(
-        jnp.broadcast_to(mine_sums[None, None, :], (devices * cores, 1, 2)), ("dp", "mp"), 0, 0, tiled=True
+        finals, starts, last = [], [[None]], [kept, swap_columns(sent)]
+    wanted = targets[0]
+    if finals:
+        encoded, squares = output_layer(pos, residual, wanted, dims[0], starts[:-1], finals)
+    else:
+        encoded, squares = jnp.zeros_like(wanted), jnp.zeros((8, 128), jnp.float32)
+    encoded, sums = output_layer(
+        pos,
+        residual,
+        wanted,
+        dims[0],
+        starts[-1:],
+        last,
+        (encoded, squares),
+        devices * cores,
     )
+    sums = lax.all_to_all(sums, ("dp", "mp"), 0, 0, tiled=True)
     total_squares, total_number = jnp.sum(sums, axis=(0, 1))
     return (encoded[None], total_squares / (width * total_number))
 

time: 183 us -> 169 us (0.923)
  local copies, waits for them, and re-layouts: 22 us -> 13.3 us
  waiting for transfers between devices: 71.6 us -> 66.9 us
  other arithmetic: 4.35 us -> 0.06 us
  Pallas kernels: 37.5 us -> 41 us
    slice x24 -> x0, local copies, waits for them, and re-layouts: 7.2 us -> none  [the longest x8 3.51 us: part(): self.array[first * self.rows:last * self.rows]]
    pallas_call x1 -> x12, Pallas kernels: 2.82 us -> 7.96 us  [the longest x10 4.82 us: stack(): pl.pallas_call(functools.partial(stack_kernel, plan), out_shape=tuple((ja...]
    ppermute x30, waiting for transfers between devices: 70 us -> 66.5 us  [shift(): return lax.ppermute(value, 'dp', pairs)]
    concatenate x15 -> x0, other arithmetic: 2.92 us -> none  [the longest x9 2.8 us: joined(): jnp.concatenate([c.array for c in chunks], 0)]
    pallas_call x3, Pallas kernels: 9.05 us -> 6.81 us  [down_layer(): pl.pallas_call(functools.partial(down_kernel, n, dims, pieces, block, z_f...]
    unnamed x63 -> x48, local copies, waits for them, and re-layouts: 13.3 us -> 11.9 us
  transfers between devices with their start and end apart: 37 -> 37, of which waited for: 25 -> 23; matrix products, arithmetic and copies ran while one was open for 4% -> 0% of each run, Pallas kernels for 19% -> 23%
where the time goes in v3:
time: 169 us
  waiting for transfers between devices  66.9 us (40%)
  Pallas kernels  41 us (24%)
  starting transfers between devices  32.5 us (19%)
  local copies, waits for them, and re-layouts  13.3 us (8%)
  blocking collectives  8.86 us (5%)
  between operations  6.04 us (4%)
    ppermute x30, waiting for transfers between devices, shift(): return lax.ppermute(value, 'dp', pairs)  66.5 us
    ppermute x30, starting transfers between devices, shift(): return lax.ppermute(value, 'dp', pairs)  31.3 us
    unnamed x48, local copies, waits for them, and re-layouts  11.9 us
    all_to_all x1, blocking collectives, on_device(): sums = lax.all_to_all(sums, ('dp', 'mp'), 0, 0, tiled=True)  8.86 us
    pallas_call x1, Pallas kernels, attention(): pl.pallas_call(functools.partial(attention_kernel, n, dims, pieces, block...  8.3 us
    pallas_call x1, Pallas kernels, up_layer(): pl.pallas_call(functools.partial(up_kernel, n, dims, pieces, block), out_...  6.91 us
    pallas_call x3, Pallas kernels, down_layer(): pl.pallas_call(functools.partial(down_kernel, n, dims, pieces, block, z_f...  6.81 us
    pallas_call x1, Pallas kernels, project(): pl.pallas_call(functools.partial(project_kernel, n, dims, pieces, block),...  5.69 us
  transfers between devices with their start and end apart: 37, of which 23 were waited for; matrix products, arithmetic and copies ran while one was open for 0% of the time, Pallas kernels for 23%

profile of v3, /device:TPU:0, one launch (start us, length us, event | category | flops | bytes accessed | tf_op | source)
XLA Modules:
  0.0 168.5 jit_solution(17704253053498710210)
XLA Ops:
  1.2 2.2 %pack.1 = (bf16[304,512]{1,0:T(8,128)(2,1)}, bf16[64,2048]{1,0:T(8,128)(2,1)}, bf16[64,2048]{1,0:T(8,128)(2,1)}) custom-call(bf16[48,512]{1,0:T(8,128)(2,1)} %rest_0_.1, bf16[3,64,512]{2,1,0:T(8,128)(2,1)} %rest_1_.1, bf16[64,512]{1,0:T(8,128)(2,1)} %bitcast.24, bf16[64,2048]{1,0:T(8,128)(2,1)} %rest_3_.1, bf16[64,2048]{1,0:T(8,128)(2,1)} %bitcast.23), custom_call_target="tpu_custom_call" | custom-call | bytes 1024 | tf_op jit(solution)/shard_map/pack/pallas_call | solution.py:287
  3.4 2.6 %collective-permute-start = (bf16[304,512]{1,0:T(8,128)(2,1)}, bf16[304,512]{1,0:T(8,128)(2,1)S(1)}, u32[]{:S(2)}, u32[]{:S(2)}) collective-permute-start(bf16[304,512]{1,0:T(8,128)(2,1)} %get-tuple-element.162.refs_0_), channel_id=1, source_target_pairs={{0,8},{2,10},{4,12},{6,14},{8,16},{10,18},{12,20},{14,22},{16,24},... | collective-permute-start | bytes 933896 | tf_op jit(solution)/shard_map/ppermute | solution.py:38
  9.0 5.6 %collective-permute-done.1.refs_1_ = bf16[64,2048]{1,0:T(8,128)(2,1)S(1)} collective-permute-done((bf16[64,2048]{1,0:T(8,128)(2,1)}, bf16[64,2048]{1,0:T(8,128)(2,1)S(1)}, u32[]{:S(2)}, u32[]{:S(2)}) %collective-permute-start.1) | collective-permute-done | bytes 262176 | tf_op jit(solution)/shard_map/ppermute | solution.py:38
  22.6 4.9 %collective-permute-done.4.refs_1_ = bf16[288,512]{1,0:T(8,128)(2,1)S(1)} collective-permute-done((bf16[288,512]{1,0:T(8,128)(2,1)S(1)}, bf16[288,512]{1,0:T(8,128)(2,1)S(1)}, u32[]{:S(2)}, u32[]{:S(2)}) %collective-permute-start.4) | collective-permute-done | bytes 294944 | tf_op jit(solution)/shard_map/ppermute | solution.py:38
  27.5 2.0 %collective-permute-done.6.refs_0_ = bf16[304,512]{1,0:T(8,128)(2,1)S(1)} collective-permute-done((bf16[304,512]{1,0:T(8,128)(2,1)S(1)}, bf16[304,512]{1,0:T(8,128)(2,1)S(1)}, u32[]{:S(2)}, u32[]{:S(2)}) %collective-permute-start.6) | collective-permute-done | bytes 311328 | tf_op jit(solution)/shard_map/ppermute | solution.py:38
  31.6 9.1 %collective-permute-done.9.refs_1_ = bf16[304,512]{1,0:T(8,128)(2,1)S(1)} collective-permute-done((bf16[304,512]{1,0:T(8,128)(2,1)S(1)}, bf16[304,512]{1,0:T(8,128)(2,1)S(1)}, u32[]{:S(2)}, u32[]{:S(2)}) %collective-permute-start.9) | collective-permute-done | bytes 311328 | tf_op jit(solution)/shard_map/ppermute | solution.py:38
  40.7 3.9 %collective-permute-done.7.rest_1_ = bf16[576,512]{1,0:T(8,128)(2,1)S(1)} collective-permute-done((bf16[576,512]{1,0:T(8,128)(2,1)S(1)}, bf16[576,512]{1,0:T(8,128)(2,1)S(1)}, u32[]{:S(2)}, u32[]{:S(2)}) %collective-permute-start.7) | collective-permute-done | bytes 589856 | tf_op jit(solution)/shard_map/ppermute | solution.py:38
  47.0 2.1 %collective-permute-start.13 = (bf16[96,512]{1,0:T(8,128)(2,1)S(1)}, bf16[96,512]{1,0:T(8,128)(2,1)S(1)}, u32[]{:S(2)}, u32[]{:S(2)}) collective-permute-start(bf16[96,512]{1,0:T(8,128)(2,1)S(1)} %get-tuple-element.193), channel_id=1, source_target_pairs={{0,6},{2,4},{4,2},{6,0},{8,14},{10,12},{12,10},{14,8},{16,22},{18,... | collective-permute-start | bytes 294920 | tf_op jit(solution)/shard_map/ppermute | solution.py:38
  49.1 6.4 %collective-permute-done.13.rest_5_ = bf16[96,512]{1,0:T(8,128)(2,1)S(1)} collective-permute-done((bf16[96,512]{1,0:T(8,128)(2,1)S(1)}, bf16[96,512]{1,0:T(8,128)(2,1)S(1)}, u32[]{:S(2)}, u32[]{:S(2)}) %collective-permute-start.13) | collective-permute-done | bytes 98336 | tf_op jit(solution)/shard_map/ppermute | solution.py:38
  56.3 3.0 %collective-permute-done.12.refs_1_ = bf16[136,2048]{1,0:T(8,128)(2,1)} collective-permute-done((bf16[136,2048]{1,0:T(8,128)(2,1)S(1)}, bf16[136,2048]{1,0:T(8,128)(2,1)}, u32[]{:S(2)}, u32[]{:S(2)}) %collective-permute-start.12) | collective-permute-done | bytes 557088 | tf_op jit(solution)/shard_map/ppermute | solution.py:38
  73.2 2.1 %stack.47 = (bf16[128,2048]{1,0:T(8,128)(2,1)}, bf16[128,2048]{1,0:T(8,128)(2,1)}) custom-call(bf16[136,2048]{1,0:T(8,128)(2,1)S(1)} %copy-done.16, bf16[136,2048]{1,0:T(8,128)(2,1)} %collective-permute-done.12.refs_1_), custom_call_target="tpu_custom_call" | custom-call | bytes 1024 | tf_op jit(solution)/shard_map/stack/pallas_call | solution.py:77
  79.9 5.7 %project.1 = (bf16[2,512,512]{2,1,0:T(8,128)(2,1)S(1)}, bf16[2,512,512]{2,1,0:T(8,128)(2,1)S(1)}, bf16[2,512,512]{2,1,0:T(8,128)(2,1)S(1)}) custom-call(s32[8]{0:T(128)S(1)} %stack.41.pos, bf16[2,512,512]{2,1,0:T(8,128)(2,1)S(1)} %embed.1.mine, bf16[2,512,512]{2,1,0:T(8,128)(2,1)S(1)} %collective-permute-done.20.recv, ...), custom_call_target="tpu_custom_call" | custom-call | bytes 1024 | tf_op jit(solution)/shard_map/project/pallas_call | solution.py:356
  85.6 4.2 %collective-permute-done.18.rest_1_ = bf16[128,2048]{1,0:T(8,128)(2,1)} collective-permute-done((bf16[128,2048]{1,0:T(8,128)(2,1)}, bf16[128,2048]{1,0:T(8,128)(2,1)}, u32[]{:S(2)}, u32[]{:S(2)}) %collective-permute-start.18) | collective-permute-done | bytes 524320 | tf_op jit(solution)/shard_map/ppermute | solution.py:38
  95.4 8.3 %attention.1 = (bf16[2,256,1024]{2,1,0:T(8,128)(2,1)S(1)}, bf16[2,256,1024]{2,1,0:T(8,128)(2,1)S(1)}) custom-call(s32[8]{0:T(128)S(1)} %stack.41.pos, bf16[2,512,512]{2,1,0:T(8,128)(2,1)S(1)} %get-tuple-element.243.q, bf16[2,512,512]{2,1,0:T(8,128)(2,1)S(1)} %get-tuple-element.244.k, bf16[2,512,512]{2,1,0:T(8,128)(2,1)S(1)} %get-tuple-element.245.v, ...), custom_call_target="tpu_custom_call" | custom-call | bytes 1024 | tf_op jit(solution)/shard_map/attention/pallas_call | solution.py:407
  103.7 2.5 %collective-permute-done.22.rest_5_ = bf16[128,2048]{1,0:T(8,128)(2,1)S(1)} collective-permute-done((bf16[128,2048]{1,0:T(8,128)(2,1)S(1)}, bf16[128,2048]{1,0:T(8,128)(2,1)S(1)}, u32[]{:S(2)}, u32[]{:S(2)}) %collective-permute-start.22) | collective-permute-done | bytes 524320 | tf_op jit(solution)/shard_map/ppermute | solution.py:38
  107.0 3.2 %collective-permute-start.24 = (bf16[136,2048]{1,0:T(8,128)(2,1)S(1)}, bf16[136,2048]{1,0:T(8,128)(2,1)S(1)}, u32[]{:S(2)}, u32[]{:S(2)}) collective-permute-start(bf16[136,2048]{1,0:T(8,128)(2,1)S(1)} %collective-permute-done.21.refs_1_), channel_id=1, source_target_pairs={{0,8},{2,10},{4,12},{6,14},{8,16},{10,18},{12,20},{14,22},{16,24},... | collective-permute-start | bytes 1671176 | tf_op jit(solution)/shard_map/ppermute | solution.py:38
  114.0 10.4 %collective-permute-done.25.rest_1_ = bf16[128,2048]{1,0:T(8,128)(2,1)S(1)} collective-permute-done((bf16[128,2048]{1,0:T(8,128)(2,1)S(1)}, bf16[128,2048]{1,0:T(8,128)(2,1)S(1)}, u32[]{:S(2)}, u32[]{:S(2)}) %collective-permute-start.25) | collective-permute-done | bytes 524320 | tf_op jit(solution)/shard_map/ppermute | solution.py:38
  128.0 6.9 %up.1.hidden = bf16[2,2,256,2048]{3,2,1,0:T(8,128)(2,1)S(1)} custom-call(s32[8]{0:T(128)S(1)} %stack.41.pos, bf16[2,256,1024]{2,1,0:T(8,128)(2,1)S(1)} %get-tuple-element.282.own, bf16[2,256,1024]{2,1,0:T(8,128)(2,1)S(1)} %collective-permute-done.31.came, bf16[128,2048]{1,0:T(8,128)(2,1)} %get-tuple-element.267.rest_0_, ...), custom_call_target="tpu_custom_call" | custom-call | bytes 1024 | tf_op jit(solution)/shard_map/up/pallas_call | solution.py:489
  135.0 7.1 %collective-permute-done.28.refs_0_ = bf16[136,2048]{1,0:T(8,128)(2,1)S(1)} collective-permute-done((bf16[136,2048]{1,0:T(8,128)(2,1)S(1)}, bf16[136,2048]{1,0:T(8,128)(2,1)S(1)}, u32[]{:S(2)}, u32[]{:S(2)}) %collective-permute-start.28) | collective-permute-done | bytes 557088 | tf_op jit(solution)/shard_map/ppermute | solution.py:38
  144.0 1.9 %down.4 = (bf16[2,256,256]{2,1,0:T(8,128)(2,1)S(1)}, bf16[2,256,256]{2,1,0:T(8,128)(2,1)S(1)}) custom-call(s32[8]{0:T(128)S(1)} %stack.41.pos, bf16[2,2,256,2048]{3,2,1,0:T(8,128)(2,1)S(1)} %up.1.hidden, bf16[64,2048]{1,0:T(8,128)(2,1)S(1)} %get-tuple-element.288.rest_0_, bf16[64,2048]{1,0:T(8,128)(2,1)S(1)} %collective-permute-done.29.rest_1_, ...), custom_call_target="tpu_custom_call" | custom-call | bytes 1024 | tf_op jit(solution)/shard_map/down/pallas_call | solution.py:513
  145.9 3.1 %down.3 = (bf16[2,256,512]{2,1,0:T(8,128)(2,1)S(1)}, bf16[2,256,512]{2,1,0:T(8,128)(2,1)S(1)}) custom-call(s32[8]{0:T(128)S(1)} %stack.41.pos, bf16[2,2,256,2048]{3,2,1,0:T(8,128)(2,1)S(1)} %up.1.hidden, bf16[128,2048]{1,0:T(8,128)(2,1)S(1)} %get-tuple-element.284.rest_0_, bf16[128,2048]{1,0:T(8,128)(2,1)S(1)} %collective-permute-done.25.rest_1_, ...), custom_call_target="tpu_custom_call" | custom-call | bytes 1024 | tf_op jit(solution)/shard_map/down/pallas_call | solution.py:513
  151.3 1.9 %down.5 = (bf16[2,256,256]{2,1,0:T(8,128)(2,1)S(1)}, bf16[2,256,256]{2,1,0:T(8,128)(2,1)S(1)}) custom-call(s32[8]{0:T(128)S(1)} %stack.41.pos, bf16[2,2,256,2048]{3,2,1,0:T(8,128)(2,1)S(1)} %up.1.hidden, bf16[64,2048]{1,0:T(8,128)(2,1)S(1)} %get-tuple-element.302.rest_0_, bf16[64,2048]{1,0:T(8,128)(2,1)S(1)} %collective-permute-done.32.rest_1_, ...), custom_call_target="tpu_custom_call" | custom-call | bytes 1024 | tf_op jit(solution)/shard_map/down/pallas_call | solution.py:513
  154.7 1.9 %output.3 = (bf16[2,256,1024]{2,1,0:T(8,128)(2,1)}, f32[32,1,2]{2,1,0:T(1,128)S(1)}) custom-call(s32[8]{0:T(128)S(1)} %stack.41.pos, f32[2,256,1024]{2,1,0:T(8,128)S(1)} %get-tuple-element.300.residual, bf16[2,256,1024]{2,1,0:T(8,128)(2,1)S(1)} %bitcast.19, bf16[2,256,256]{2,1,0:T(8,128)(2,1)S(1)} %get-tuple-element.306.rest_0_, ...), custom_call_target="tpu_custom_call" | custom-call | bytes 1024 | tf_op jit(solution)/shard_map/output/pallas_call | solution.py:567
  156.6 8.9 %all_to_all.5 = f32[32,1,2]{2,1,0:T(1,128)S(1)} all-to-all(f32[32,1,2]{2,1,0:T(1,128)S(1)} %get-tuple-element.315), channel_id=1, replica_groups=mesh['dp'=16,'mp'=2] {'dp','mp'}, dimensions={0} | all-to-all | bytes 512 | tf_op jit(solution)/shard_map/all_to_all | solution.py:714
  (127 shorter events, 52.6 us)
Async XLA Ops:
  0.7 15.6 %collective-permute-start.3 = (bf16[512,768]{1,0:T(8,128)(2,1)}, bf16[512,768]{1,0:T(8,128)(2,1)S(1)}, u32[]{:S(2)}, u32[]{:S(2)}) collective-permute-start(bf16[512,768]{1,0:T(8,128)(2,1)} %bitcast.20), channel_id=1, source_target_pairs={{0,1},{1,0},{2,3},{3,2},{4,5},{5,4},{6,7},{7,6},{8,9},{9,8},{10,11... | collective-permute-start | bytes 2359304 | tf_op jit(solution)/shard_map/ppermute | solution.py:92
  3.4 12.9 %collective-permute-start = (bf16[304,512]{1,0:T(8,128)(2,1)}, bf16[304,512]{1,0:T(8,128)(2,1)S(1)}, u32[]{:S(2)}, u32[]{:S(2)}) collective-permute-start(bf16[304,512]{1,0:T(8,128)(2,1)} %get-tuple-element.162.refs_0_), channel_id=1, source_target_pairs={{0,8},{2,10},{4,12},{6,14},{8,16},{10,18},{12,20},{14,22},{16,24},... | collective-permute-start | bytes 933896 | tf_op jit(solution)/shard_map/ppermute | solution.py:38
  17.3 12.2 %collective-permute-start.5 = (bf16[320,512]{1,0:T(8,128)(2,1)S(1)}, bf16[320,512]{1,0:T(8,128)(2,1)S(1)}, u32[]{:S(2)}, u32[]{:S(2)}) collective-permute-start(bf16[320,512]{1,0:T(8,128)(2,1)S(1)} %get-tuple-element.175.refs_2_), channel_id=1, source_target_pairs={{0,4},{2,6},{4,0},{6,2},{8,12},{10,14},{12,8},{14,10},{16,20},{18,... | collective-permute-start | bytes 983048 | tf_op jit(solution)/shard_map/ppermute | solution.py:38
  18.9 10.6 %collective-permute-start.6 = (bf16[304,512]{1,0:T(8,128)(2,1)S(1)}, bf16[304,512]{1,0:T(8,128)(2,1)S(1)}, u32[]{:S(2)}, u32[]{:S(2)}) collective-permute-start(bf16[304,512]{1,0:T(8,128)(2,1)S(1)} %collective-permute-done.refs_1_), channel_id=1, source_target_pairs={{0,8},{2,10},{4,12},{6,14},{8,16},{10,18},{12,20},{14,22},{16,24},... | collective-permute-start | bytes 933896 | tf_op jit(solution)/shard_map/ppermute | solution.py:38
  29.6 15.9 %collective-permute-start.8 = (bf16[640,512]{1,0:T(8,128)(2,1)S(1)}, bf16[640,512]{1,0:T(8,128)(2,1)S(1)}, u32[]{:S(2)}, u32[]{:S(2)}) collective-permute-start(bf16[640,512]{1,0:T(8,128)(2,1)S(1)} %get-tuple-element.232.rest_2_.rest_0_), channel_id=1, source_target_pairs={{0,2},{2,0},{4,6},{6,4},{8,10},{10,8},{12,14},{14,12},{16,18},{18,... | collective-permute-start | bytes 1966088 | tf_op jit(solution)/shard_map/ppermute | solution.py:38
  31.1 13.5 %collective-permute-start.7 = (bf16[576,512]{1,0:T(8,128)(2,1)S(1)}, bf16[576,512]{1,0:T(8,128)(2,1)S(1)}, u32[]{:S(2)}, u32[]{:S(2)}) collective-permute-start(bf16[576,512]{1,0:T(8,128)(2,1)S(1)} %get-tuple-element.216.rest_0_), channel_id=1, source_target_pairs={{0,4},{2,6},{4,0},{6,2},{8,12},{10,14},{12,8},{14,10},{16,20},{18,... | collective-permute-start | bytes 1769480 | tf_op jit(solution)/shard_map/ppermute | solution.py:38
  31.6 9.1 %collective-permute-start.9 = (bf16[304,512]{1,0:T(8,128)(2,1)S(1)}, bf16[304,512]{1,0:T(8,128)(2,1)S(1)}, u32[]{:S(2)}, u32[]{:S(2)}) collective-permute-start(bf16[304,512]{1,0:T(8,128)(2,1)S(1)} %collective-permute-done.6.refs_0_), channel_id=1, source_target_pairs={{0,8},{2,10},{4,12},{6,14},{8,16},{10,18},{12,20},{14,22},{16,24},... | collective-permute-start | bytes 933896 | tf_op jit(solution)/shard_map/ppermute | solution.py:38
  45.5 13.8 %collective-permute-start.12 = (bf16[136,2048]{1,0:T(8,128)(2,1)S(1)}, bf16[136,2048]{1,0:T(8,128)(2,1)}, u32[]{:S(2)}, u32[]{:S(2)}) collective-permute-start(bf16[136,2048]{1,0:T(8,128)(2,1)S(1)} %get-tuple-element.212.refs_0_), channel_id=1, source_target_pairs={{0,8},{2,10},{4,12},{6,14},{8,16},{10,18},{12,20},{14,22},{16,24},... | collective-permute-start | bytes 1671176 | tf_op jit(solution)/shard_map/ppermute | solution.py:38
  45.6 10.0 %collective-permute-start.10 = (bf16[352,512]{1,0:T(8,128)(2,1)S(1)}, bf16[352,512]{1,0:T(8,128)(2,1)S(1)}, u32[]{:S(2)}, u32[]{:S(2)}) collective-permute-start(bf16[352,512]{1,0:T(8,128)(2,1)S(1)} %get-tuple-element.195.refs_0_.rest_2_), channel_id=1, source_target_pairs={{0,2},{2,0},{4,6},{6,4},{8,10},{10,8},{12,14},{14,12},{16,18},{18,... | collective-permute-start | bytes 1081352 | tf_op jit(solution)/shard_map/ppermute | solution.py:38
  46.5 9.8 %collective-permute-start.11 = (bf16[352,512]{1,0:T(8,128)(2,1)S(1)}, bf16[352,512]{1,0:T(8,128)(2,1)S(1)}, u32[]{:S(2)}, u32[]{:S(2)}) collective-permute-start(bf16[352,512]{1,0:T(8,128)(2,1)S(1)} %get-tuple-element.197.refs_2_), channel_id=1, source_target_pairs={{0,4},{2,6},{4,0},{6,2},{8,12},{10,14},{12,8},{14,10},{16,20},{18,... | collective-permute-start | bytes 1081352 | tf_op jit(solution)/shard_map/ppermute | solution.py:38
  59.3 13.7 %collective-permute-start.14 = (bf16[136,2048]{1,0:T(8,128)(2,1)}, bf16[136,2048]{1,0:T(8,128)(2,1)}, u32[]{:S(2)}, u32[]{:S(2)}) collective-permute-start(bf16[136,2048]{1,0:T(8,128)(2,1)} %collective-permute-done.12.refs_1_), channel_id=1, source_target_pairs={{0,8},{2,10},{4,12},{6,14},{8,16},{10,18},{12,20},{14,22},{16,24},... | collective-permute-start | bytes 1671176 | tf_op jit(solution)/shard_map/ppermute | solution.py:38
  61.1 11.9 %collective-permute-start.15 = (bf16[512,512]{1,0:T(8,128)(2,1)}, bf16[512,512]{1,0:T(8,128)(2,1)}, u32[]{:S(2)}, u32[]{:S(2)}) collective-permute-start(bf16[512,512]{1,0:T(8,128)(2,1)} %get-tuple-element.210.rest_4_), channel_id=1, source_target_pairs={{0,4},{2,6},{4,0},{6,2},{8,12},{10,14},{12,8},{14,10},{16,20},{18,... | collective-permute-start | bytes 1572872 | tf_op jit(solution)/shard_map/ppermute | solution.py:38
  61.7 11.3 %collective-permute-start.16 = (bf16[512,512]{1,0:T(8,128)(2,1)}, bf16[512,512]{1,0:T(8,128)(2,1)}, u32[]{:S(2)}, u32[]{:S(2)}) collective-permute-start(bf16[512,512]{1,0:T(8,128)(2,1)} %get-tuple-element.228.rest_6_.rest_2_), channel_id=1, source_target_pairs={{0,2},{2,0},{4,6},{6,4},{8,10},{10,8},{12,14},{14,12},{16,18},{18,... | collective-permute-start | bytes 1572872 | tf_op jit(solution)/shard_map/ppermute | solution.py:38
  73.1 18.0 %collective-permute-start.17 = (bf16[136,2048]{1,0:T(8,128)(2,1)}, bf16[136,2048]{1,0:T(8,128)(2,1)}, u32[]{:S(2)}, u32[]{:S(2)}) collective-permute-start(bf16[136,2048]{1,0:T(8,128)(2,1)} %collective-permute-done.14.refs_0_), channel_id=1, source_target_pairs={{0,8},{2,10},{4,12},{6,14},{8,16},{10,18},{12,20},{14,22},{16,24},... | collective-permute-start | bytes 1671176 | tf_op jit(solution)/shard_map/ppermute | solution.py:38
  75.2 14.6 %collective-permute-start.18 = (bf16[128,2048]{1,0:T(8,128)(2,1)}, bf16[128,2048]{1,0:T(8,128)(2,1)}, u32[]{:S(2)}, u32[]{:S(2)}) collective-permute-start(bf16[128,2048]{1,0:T(8,128)(2,1)} %get-tuple-element.267.rest_0_), channel_id=1, source_target_pairs={{0,4},{2,6},{4,0},{6,2},{8,12},{10,14},{12,8},{14,10},{16,20},{18,... | collective-permute-start | bytes 1572872 | tf_op jit(solution)/shard_map/ppermute | solution.py:38
  76.8 14.3 %collective-permute-start.19 = (bf16[128,2048]{1,0:T(8,128)(2,1)}, bf16[128,2048]{1,0:T(8,128)(2,1)}, u32[]{:S(2)}, u32[]{:S(2)}) collective-permute-start(bf16[128,2048]{1,0:T(8,128)(2,1)} %get-tuple-element.269.rest_2_), channel_id=1, source_target_pairs={{0,2},{2,0},{4,6},{6,4},{8,10},{10,8},{12,14},{14,12},{16,18},{18,... | collective-permute-start | bytes 1572872 | tf_op jit(solution)/shard_map/ppermute | solution.py:38
  91.1 15.9 %collective-permute-start.21 = (bf16[136,2048]{1,0:T(8,128)(2,1)S(1)}, bf16[136,2048]{1,0:T(8,128)(2,1)S(1)}, u32[]{:S(2)}, u32[]{:S(2)}) collective-permute-start(bf16[136,2048]{1,0:T(8,128)(2,1)S(1)} %copy-done.14), channel_id=1, source_target_pairs={{0,8},{2,10},{4,12},{6,14},{8,16},{10,18},{12,20},{14,22},{16,24},... | collective-permute-start | bytes 1671176 | tf_op jit(solution)/shard_map/ppermute | solution.py:38
  93.5 12.6 %collective-permute-start.22 = (bf16[128,2048]{1,0:T(8,128)(2,1)S(1)}, bf16[128,2048]{1,0:T(8,128)(2,1)S(1)}, u32[]{:S(2)}, u32[]{:S(2)}) collective-permute-start(bf16[128,2048]{1,0:T(8,128)(2,1)S(1)} %get-tuple-element.271.rest_4_), channel_id=1, source_target_pairs={{0,4},{2,6},{4,0},{6,2},{8,12},{10,14},{12,8},{14,10},{16,20},{18,... | collective-permute-start | bytes 1572872 | tf_op jit(solution)/shard_map/ppermute | solution.py:38
  94.5 12.3 %collective-permute-start.23 = (bf16[128,2048]{1,0:T(8,128)(2,1)S(1)}, bf16[128,2048]{1,0:T(8,128)(2,1)S(1)}, u32[]{:S(2)}, u32[]{:S(2)}) collective-permute-start(bf16[128,2048]{1,0:T(8,128)(2,1)S(1)} %get-tuple-element.273.rest_6_), channel_id=1, source_target_pairs={{0,2},{2,0},{4,6},{6,4},{8,10},{10,8},{12,14},{14,12},{16,18},{18,... | collective-permute-start | bytes 1572872 | tf_op jit(solution)/shard_map/ppermute | solution.py:38
  107.0 18.3 %collective-permute-start.24 = (bf16[136,2048]{1,0:T(8,128)(2,1)S(1)}, bf16[136,2048]{1,0:T(8,128)(2,1)S(1)}, u32[]{:S(2)}, u32[]{:S(2)}) collective-permute-start(bf16[136,2048]{1,0:T(8,128)(2,1)S(1)} %collective-permute-done.21.refs_1_), channel_id=1, source_target_pairs={{0,8},{2,10},{4,12},{6,14},{8,16},{10,18},{12,20},{14,22},{16,24},... | collective-permute-start | bytes 1671176 | tf_op jit(solution)/shard_map/ppermute | solution.py:38
  110.3 14.1 %collective-permute-start.25 = (bf16[128,2048]{1,0:T(8,128)(2,1)S(1)}, bf16[128,2048]{1,0:T(8,128)(2,1)S(1)}, u32[]{:S(2)}, u32[]{:S(2)}) collective-permute-start(bf16[128,2048]{1,0:T(8,128)(2,1)S(1)} %get-tuple-element.284.rest_0_), channel_id=1, source_target_pairs={{0,4},{2,6},{4,0},{6,2},{8,12},{10,14},{12,8},{14,10},{16,20},{18,... | collective-permute-start | bytes 1572872 | tf_op jit(solution)/shard_map/ppermute | solution.py:38
  111.5 13.8 %collective-permute-start.26 = (bf16[128,2048]{1,0:T(8,128)(2,1)S(1)}, bf16[128,2048]{1,0:T(8,128)(2,1)S(1)}, u32[]{:S(2)}, u32[]{:S(2)}) collective-permute-start(bf16[128,2048]{1,0:T(8,128)(2,1)S(1)} %get-tuple-element.286.rest_2_), channel_id=1, source_target_pairs={{0,2},{2,0},{4,6},{6,4},{8,10},{10,8},{12,14},{14,12},{16,18},{18,... | collective-permute-start | bytes 1572872 | tf_op jit(solution)/shard_map/ppermute | solution.py:38
  125.3 16.8 %collective-permute-start.28 = (bf16[136,2048]{1,0:T(8,128)(2,1)S(1)}, bf16[136,2048]{1,0:T(8,128)(2,1)S(1)}, u32[]{:S(2)}, u32[]{:S(2)}) collective-permute-start(bf16[136,2048]{1,0:T(8,128)(2,1)S(1)} %collective-permute-done.24.refs_0_), channel_id=1, source_target_pairs={{0,8},{2,10},{4,12},{6,14},{8,16},{10,18},{12,20},{14,22},{16,24},... | collective-permute-start | bytes 1671176 | tf_op jit(solution)/shard_map/ppermute | solution.py:38
  126.0 8.9 %collective-permute-start.29 = (bf16[64,2048]{1,0:T(8,128)(2,1)S(1)}, bf16[64,2048]{1,0:T(8,128)(2,1)S(1)}, u32[]{:S(2)}, u32[]{:S(2)}) collective-permute-start(bf16[64,2048]{1,0:T(8,128)(2,1)S(1)} %get-tuple-element.288.rest_0_), channel_id=1, source_target_pairs={{0,4},{2,6},{4,0},{6,2},{8,12},{10,14},{12,8},{14,10},{16,20},{18,... | collective-permute-start | bytes 786440 | tf_op jit(solution)/shard_map/ppermute | solution.py:38
  (37 other events, 476.1 us)

commit v4 on v3

--- a/solution.py
+++ b/solution.py
@@ -103,11 +103,6 @@
     def step(self, chunk, axis):
         return chunk.moved(shift(chunk.array, self.dims, axis), axis)
 
-    def whole(self, k):
-        half = self.half
-        sides = (self.side_a, self.from_x, self.side_b, self.from_y)
-        return [(side, k * half, half) for side in sides] + [(self.side_a, 0, SPARE)] * (SPARE > 0)
-
     def ends(self, low, kind):
         first, last = self.spans[kind]
         return [(v, first, last - first) for v in self.first_z[low : low + 2]]
@@ -118,13 +113,25 @@
     def both(self, a, b):
         return [a, self.step(a, Y), b, self.step(b, X)]
 
-    def last(self, blocks):
-        a, b = stack(
-            [c.block(i) for c in blocks for i in (0, 1)], [c.block(i) for c in blocks for i in (2, 3)]
-        )
-        a = Chunk(a, sum((c.slots[:2] for c in blocks), []), 0, self.half)
-        b = Chunk(b, sum((c.slots[2:] for c in blocks), []), 1, self.half)
+    def last(self, first, second):
+        a, b = stack(sum((c.all() for c in first), []), sum((c.all() for c in second), []))
+        a = Chunk(a, sum((c.slots for c in first), []), 0, self.half)
+        b = Chunk(b, sum((c.slots for c in second), []), 1, self.half)
         return self.both(a, b)
+
+    def own_halves(self, k):
+        rows = (k * self.half, self.half)
+        return ([(self.side_a, *rows), (self.from_x, *rows)], [(self.side_b, *rows), (self.from_y, *rows)])
+
+    def pair(self, b, a):
+        (value,) = stack(b.all() + a.all() + [a.block(0, 0, SPARE)])
+        return value
+
+    def pair_moved(self, value, b, a):
+        value = self.move(value, Z)
+        b, a = b.moved(value, Z), a.moved(value, Z)
+        b.base, a.base = 0, 2 * self.half
+        return b, a, value
 
     def slot(self, number):
         if number == 0:
@@ -136,9 +143,10 @@
             a, b = stack(self.ends(0, 0), self.ends(0, 1))
             self.a, self.b = self.chunk(a, near, 0), self.chunk(b, near, 1)
             self.a_far, self.b_far = self.step(self.a, X), self.step(self.b, Y)
-            up, down = stack(self.whole(0), self.whole(1))
-            own = [(0, 0, 0), (0, 0, 1), (0, 0, 0), (0, 1, 0)]
-            self.up_z, self.down_z = [Chunk(up, own, 0, self.half)], [Chunk(down, own, 0, self.half)]
+            made = stack(*self.own_halves(0), *self.own_halves(1))
+            along_x, along_y = [(0, 0, 0), (0, 0, 1)], [(0, 0, 0), (0, 1, 0)]
+            self.up_a, self.down_a = ([Chunk(v, along_x, 0, self.half)] for v in made[0::2])
+            self.up_b, self.down_b = ([Chunk(v, along_y, 1, self.half)] for v in made[1::2])
         elif number == 2:
             self.first_z.append(self.move(self.first_z[-1], Z))
             del self.side_a, self.side_b, self.from_x, self.from_y
@@ -146,8 +154,12 @@
             self.a = self.chunk(a, self.a.slots + self.a_far.slots, 0)
             self.b = self.chunk(b, self.b.slots + self.b_far.slots, 1)
             self.parts = self.both(self.a, self.b)
+            self.up_a.append(self.step(self.up_a[0], Z))
         elif number == 3:
-            self.up_z.append(self.step(self.up_z[-1], Z))
+            value = self.pair(self.up_b[0], self.up_a[1])
+            b, a, self.z_pair = self.pair_moved(value, self.up_b[0], self.up_a[1])
+            self.up_b.append(b)
+            self.up_a.append(a)
             far = [(2, 0, 0), (3, 0, 0)]
             a, b, own = stack(self.ends(2, 5), self.ends(2, 3) + self.ends(2, 4), self.ends(2, 4))
             self.a, self.b = self.chunk(a, far, 5), self.chunk(b, far, 3)
@@ -157,26 +169,40 @@
             own_far.base = 2 * self.b.rows
             self.early = self.parts[:2] + [self.a, self.a_far, own_far, corner]
         elif number == 4:
-            self.up_z.append(self.step(self.up_z[-1], Z))
+            b, a, self.z_pair = self.pair_moved(self.z_pair, self.up_b[1], self.up_a[2])
+            self.up_b.append(b)
+            self.up_a.append(a)
             first = self.spans[2][0] - self.spans[5][0]
             a, b = stack(self.a.all(first) + self.a_far.all(first), self.b.all() + self.b_far.all())
             self.a = self.chunk(a, self.a.slots + self.a_far.slots, 2)
             self.b = self.chunk(b, self.b.slots + self.b_far.slots, 3)
             self.parts += self.both(self.a, self.b)
         elif number == 5:
-            self.up_parts = self.last(self.up_z[:2])
-            self.up_z.append(self.step(self.up_z[-1], Z))
+            value = self.pair(self.up_b[2], self.down_a[0])
+            b, a, self.z_pair = self.pair_moved(value, self.up_b[2], self.down_a[0])
+            self.up_parts = self.last(self.up_a[:2], self.up_b[:2])
+            self.up_b.append(b)
+            self.down_a.append(a)
         elif number == 6:
-            self.up_parts += self.last(self.up_z[2:])
-            self.down_z.append(self.step(self.down_z[-1], Z))
+            value = self.pair(self.down_b[0], self.down_a[1])
+            b, a, self.z_pair = self.pair_moved(value, self.down_b[0], self.down_a[1])
+            self.up_parts += self.last(self.up_a[2:], self.up_b[2:])
+            self.down_b.append(b)
+            self.down_a.append(a)
         elif number == 7:
-            self.down_parts = [self.last(self.down_z[:2])]
-            self.down_z.append(self.step(self.down_z[-1], Z))
+            b, a, self.z_pair = self.pair_moved(self.z_pair, self.down_b[1], self.down_a[2])
+            self.down_parts = [self.last(self.down_a[:2], self.down_b[:2])]
+            self.down_b.append(b)
+            self.down_a.append(a)
         elif number == 8:
-            self.down_z.append(self.step(self.down_z[-1], Z))
-            self.down_parts.append(self.last(self.down_z[2:3]))
+            del self.z_pair
+            (value,) = stack(self.down_b[2].all() + [self.down_b[2].block(0, 0, SPARE)])
+            self.down_parts.append(self.last(self.down_a[2:3], self.down_b[2:3]))
+            b = self.down_b[2].moved(self.move(value, Z), Z)
+            b.base = 0
+            self.down_b.append(b)
         elif number == 9:
-            self.down_parts.append(self.last(self.down_z[3:]))
+            self.down_parts.append(self.last(self.down_a[3:], self.down_b[3:]))
 
     def end_slot(self, *others):
         chunks, arrays = [], []
@@ -215,6 +241,16 @@
     return found
 
 
+def wide_pieces(chunks, half, width):
+    found = []
+    for number, chunk in enumerate(chunks):
+        for i, slot in enumerate(chunk.slots):
+            for c in range(chunk.rows // half):
+                row = chunk.base + i * chunk.rows + c * half
+                found.append((number, row, half, slot, chunk.half * half, c * width))
+    return found
+
+
 def source(pos, slot, dims, z_first=None):
     z, y, x = (lax.rem(pos[i] - slot[i] + dims[i], dims[i]) for i in (0, 1, 2))
     if z_first is not None:
@@ -223,11 +259,12 @@
 
 
 def lay_out(pos, dims, refs, pieces, into, block, z_first=None):
-    for number, row, rows, slot, offset in pieces:
+    for number, row, rows, slot, offset, *column in pieces:
         to = offset
         if slot is not None:
             to = pl.multiple_of(source(pos, slot, dims, z_first) * block + offset, TILE)
-        into[pl.ds(to, rows), :] = refs[number][pl.ds(row, rows), :]
+        first, width = (column[0] if column else 0), refs[number].shape[1]
+        into[pl.ds(to, rows), first : first + width] = refs[number][pl.ds(row, rows), :]
 
 
 def nt_dot(left, right):
@@ -264,15 +301,18 @@
 
 def pack_kernel(*rest):
     *shards, up, down, first, side_a, side_b, sems = rest
-    half = up.shape[0] // 2
+    half, width = up.shape[0] // 2, first.shape[1]
+    wide = up.shape[1] // width
     moves, at = [], 0
     for shard in shards:
         for part in [shard] if len(shard.shape) == 2 else [shard.at[i] for i in range(shard.shape[0])]:
             moves.append((part, first.at[pl.ds(at, part.shape[0])]))
             at += part.shape[0]
     for k, shard in enumerate((up, down)):
-        moves.append((shard.at[pl.ds(0, half)], side_a.at[pl.ds(k * half, half)]))
-        moves.append((shard.at[pl.ds(half, half)], side_b.at[pl.ds(k * half, half)]))
+        for c in range(wide):
+            to, columns = pl.ds((k * wide + c) * half, half), pl.ds(c * width, width)
+            moves.append((shard.at[pl.ds(0, half), columns], side_a.at[to]))
+            moves.append((shard.at[pl.ds(half, half), columns], side_b.at[to]))
     made = [pltpu.make_async_copy(a, b, sems.at[i]) for i, (a, b) in enumerate(moves)]
     for c in made:
         c.start()
@@ -283,13 +323,14 @@
 def pack(shards, up, down):
     rows = sum(s.size for s in shards) // shards[0].shape[1]
     first = jax.ShapeDtypeStruct((rows, shards[0].shape[1]), up.dtype)
-    side = jax.ShapeDtypeStruct(up.shape, up.dtype)
+    wide = up.shape[1] // shards[0].shape[1]
+    side = jax.ShapeDtypeStruct((up.shape[0] * wide, shards[0].shape[1]), up.dtype)
     return pl.pallas_call(
         pack_kernel,
         out_shape=(first, side, side),
         in_specs=[hbm_spec()] * (len(shards) + 2),
         out_specs=(vmem_spec(),) * 3,
-        scratch_shapes=[pltpu.SemaphoreType.DMA((rows // shards[0].shape[0] + 4,))],
+        scratch_shapes=[pltpu.SemaphoreType.DMA((len(shards) + 2 + 4 * wide,))],
         compiler_params=limits(60),
         cost_estimate=cost(0, 2 * MIB),
         name="pack",
@@ -622,16 +663,18 @@
         moved = [[(used.index(p[0]), *p[1:]) for p in some] for some in lists]
         return [chunks[i].array for i in used], moved if isinstance(pieces[0], list) else moved[0]
 
-    if dims == (4, 2, 2) and block % (2 * TILE) == 0 and block_e % TILE == 0:
+    if dims == (4, 2, 2) and block % (2 * TILE) == 0 and block_e % TILE == 0 and units % columns == 0:
         spans = ((0, cut), (cut, last), (block_e, far_cut), (far_cut, last), (0, block_e), (0, far_cut))
-        halves = ((0, block // 2), (block // 2, block))
         work = Gather(*pack(shards, up, down), spans, dims)
         work.slot(0)
+        picture, pos, gain_one = work.end_slot(picture, pos, gain_one)
+        work.slot(1)
+        picture, pos, gain_one = work.end_slot(picture, pos, gain_one)
+        work.slot(2)
         other_picture = swap_columns(picture)
-        (other_picture,) = work.end_slot(other_picture)
-        for number in range(1, 4):
-            work.slot(number)
-            (other_picture,) = work.end_slot(other_picture)
+        other_picture, picture = work.end_slot(other_picture, picture)
+        work.slot(3)
+        other_picture, picture = work.end_slot(other_picture, picture)
         chunks, own_pieces = picked(work.early, pieces_of(work.early, spans, (0, block_e)))
         work.slot(4)
         mine = embed(pos, dims, picture, other_picture, chunks, own_pieces, block_e, columns)
@@ -653,7 +696,7 @@
         residual, normed = work.end_slot(residual, normed)
         work.slot(8)
         normed_came = swap_columns(normed)
-        up_pieces = pieces_of(work.up_parts, halves, (0, block))
+        up_pieces = wide_pieces(work.up_parts, block // 2, columns)
         hidden = up_layer(
             pos, dims, normed, normed_came, [c.array for c in work.up_parts], up_pieces, block, units
         )
@@ -662,7 +705,7 @@
         finals, starts = [], []
 
         def down_part(part):
-            own_pieces = pieces_of(part, halves, (0, block))
+            own_pieces = wide_pieces(part, block // 2, columns)
             spots = sorted({p[3][0] for p in own_pieces})
             starts.append(spots)
             size = width // dims[0] * len(spots)

time: 169 us -> 163 us (0.964)
  waiting for transfers between devices: 66.9 us -> 77.5 us
  local copies, waits for them, and re-layouts: 13.3 us -> 5.68 us
  Pallas kernels: 41 us -> 34.3 us
  starting transfers between devices: 32.5 us -> 29.3 us
    ppermute x30 -> x31, waiting for transfers between devices: 66.5 us -> 76.3 us  [shift(): return lax.ppermute(value, 'dp', pairs)]
    unnamed x48 -> x12, local copies, waits for them, and re-layouts: 11.9 us -> 2.89 us
    pallas_call x10 -> x14, Pallas kernels: 4.82 us -> 0.72 us  [stack(): pl.pallas_call(functools.partial(stack_kernel, plan), out_shape=tuple((ja...]
    ppermute x30 -> x31, starting transfers between devices: 31.3 us -> 28.8 us  [shift(): return lax.ppermute(value, 'dp', pairs)]
  transfers between devices with their start and end apart: 37 -> 38, of which waited for: 23 -> 28; matrix products, arithmetic and copies ran while one was open for 0% -> 1% of each run, Pallas kernels for 23% -> 18%
where the time goes in v4:
time: 163 us
  waiting for transfers between devices  77.5 us (48%)
  Pallas kernels  34.3 us (21%)
  starting transfers between devices  29.3 us (18%)
  blocking collectives  9.52 us (6%)
  between operations  6.64 us (4%)
  local copies, waits for them, and re-layouts  5.68 us (3%)
    ppermute x31, waiting for transfers between devices, shift(): return lax.ppermute(value, 'dp', pairs)  76.3 us
    ppermute x31, starting transfers between devices, shift(): return lax.ppermute(value, 'dp', pairs)  28.8 us
    all_to_all x1, blocking collectives, on_device(): sums = lax.all_to_all(sums, ('dp', 'mp'), 0, 0, tiled=True)  9.52 us
    pallas_call x1, Pallas kernels, attention(): pl.pallas_call(functools.partial(attention_kernel, n, dims, pieces, block...  7.6 us
    pallas_call x3, Pallas kernels, down_layer(): pl.pallas_call(functools.partial(down_kernel, n, dims, pieces, block, z_f...  6.85 us
    pallas_call x1, Pallas kernels, up_layer(): pl.pallas_call(functools.partial(up_kernel, n, dims, pieces, block), out_...  5.96 us
    pallas_call x1, Pallas kernels, project(): pl.pallas_call(functools.partial(project_kernel, n, dims, pieces, block),...  4.72 us
  transfers between devices with their start and end apart: 38, of which 28 were waited for; matrix products, arithmetic and copies ran while one was open for 1% of the time, Pallas kernels for 18%

profile of v4, /device:TPU:0, one launch (start us, length us, event | category | flops | bytes accessed | tf_op | source)
XLA Modules:
  0.0 163.1 jit_solution(7307729181126525546)
XLA Ops:
  0.6 2.3 %pack.1 = (bf16[304,512]{1,0:T(8,128)(2,1)}, bf16[256,512]{1,0:T(8,128)(2,1)}, bf16[256,512]{1,0:T(8,128)(2,1)}) custom-call(bf16[48,512]{1,0:T(8,128)(2,1)} %rest_0_.1, bf16[3,64,512]{2,1,0:T(8,128)(2,1)} %rest_1_.1, bf16[64,512]{1,0:T(8,128)(2,1)} %bitcast.24, bf16[64,2048]{1,0:T(8,128)(2,1)} %rest_3_.1, bf16[64,2048]{1,0:T(8,128)(2,1)} %bitcast.23), custom_call_target="tpu_custom_call" | custom-call | bytes 1024 | tf_op jit(solution)/shard_map/pack/pallas_call | solution.py:328
  2.9 3.1 %collective-permute-start = (bf16[304,512]{1,0:T(8,128)(2,1)}, bf16[304,512]{1,0:T(8,128)(2,1)S(1)}, u32[]{:S(2)}, u32[]{:S(2)}) collective-permute-start(bf16[304,512]{1,0:T(8,128)(2,1)} %get-tuple-element.189.refs_0_), channel_id=1, source_target_pairs={{0,8},{2,10},{4,12},{6,14},{8,16},{10,18},{12,20},{14,22},{16,24},... | collective-permute-start | bytes 933896 | tf_op jit(solution)/shard_map/ppermute | solution.py:38
  16.6 1.6 collective-permute-start.4
  21.9 4.2 %collective-permute-done.3.refs_1_ = bf16[288,512]{1,0:T(8,128)(2,1)S(1)} collective-permute-done((bf16[288,512]{1,0:T(8,128)(2,1)S(1)}, bf16[288,512]{1,0:T(8,128)(2,1)S(1)}, u32[]{:S(2)}, u32[]{:S(2)}) %collective-permute-start.3) | collective-permute-done | bytes 294944 | tf_op jit(solution)/shard_map/ppermute | solution.py:38
  26.1 1.9 %collective-permute-done.5.refs_0_ = bf16[304,512]{1,0:T(8,128)(2,1)S(1)} collective-permute-done((bf16[304,512]{1,0:T(8,128)(2,1)S(1)}, bf16[304,512]{1,0:T(8,128)(2,1)S(1)}, u32[]{:S(2)}, u32[]{:S(2)}) %collective-permute-start.5) | collective-permute-done | bytes 311328 | tf_op jit(solution)/shard_map/ppermute | solution.py:38
  30.5 16.2 %collective-permute-done.6.refs_1_ = bf16[256,512]{1,0:T(8,128)(2,1)S(1)} collective-permute-done((bf16[256,512]{1,0:T(8,128)(2,1)S(1)}, bf16[256,512]{1,0:T(8,128)(2,1)S(1)}, u32[]{:S(2)}, u32[]{:S(2)}) %collective-permute-start.6) | collective-permute-done | bytes 262176 | tf_op jit(solution)/shard_map/ppermute | solution.py:38
  50.5 9.0 %collective-permute-done.14.rest_5_ = bf16[96,512]{1,0:T(8,128)(2,1)S(1)} collective-permute-done((bf16[96,512]{1,0:T(8,128)(2,1)S(1)}, bf16[96,512]{1,0:T(8,128)(2,1)S(1)}, u32[]{:S(2)}, u32[]{:S(2)}) %collective-permute-start.14) | collective-permute-done | bytes 98336 | tf_op jit(solution)/shard_map/ppermute | solution.py:38
  59.5 2.3 %collective-permute-done.13.refs_3_.refs_0_ = bf16[520,512]{1,0:T(8,128)(2,1)S(1)} collective-permute-done((bf16[520,512]{1,0:T(8,128)(2,1)S(1)}, bf16[520,512]{1,0:T(8,128)(2,1)S(1)}, u32[]{:S(2)}, u32[]{:S(2)}) %collective-permute-start.13) | collective-permute-done | bytes 532512 | tf_op jit(solution)/shard_map/ppermute | solution.py:38
  61.9 1.6 collective-permute-start.16
  64.0 1.6 embed.1.mine
  65.6 8.3 %collective-permute-done.16.rest_5_ = bf16[512,512]{1,0:T(8,128)(2,1)S(1)} collective-permute-done((bf16[512,512]{1,0:T(8,128)(2,1)S(1)}, bf16[512,512]{1,0:T(8,128)(2,1)S(1)}, u32[]{:S(2)}, u32[]{:S(2)}) %collective-permute-start.16) | collective-permute-done | bytes 524320 | tf_op jit(solution)/shard_map/ppermute | solution.py:38
  78.4 4.7 %project.1 = (bf16[2,512,512]{2,1,0:T(8,128)(2,1)S(1)}, bf16[2,512,512]{2,1,0:T(8,128)(2,1)S(1)}, bf16[2,512,512]{2,1,0:T(8,128)(2,1)S(1)}) custom-call(s32[8]{0:T(128)S(1)} %stack.45.pos, bf16[2,512,512]{2,1,0:T(8,128)(2,1)S(1)} %embed.1.mine, bf16[2,512,512]{2,1,0:T(8,128)(2,1)S(1)} %collective-permute-done.21.recv, ...), custom_call_target="tpu_custom_call" | custom-call | bytes 1024 | tf_op jit(solution)/shard_map/project/pallas_call | solution.py:397
  83.2 7.2 %collective-permute-done.19.rest_1_ = bf16[512,512]{1,0:T(8,128)(2,1)S(1)} collective-permute-done((bf16[512,512]{1,0:T(8,128)(2,1)S(1)}, bf16[512,512]{1,0:T(8,128)(2,1)S(1)}, u32[]{:S(2)}, u32[]{:S(2)}) %collective-permute-start.19) | collective-permute-done | bytes 524320 | tf_op jit(solution)/shard_map/ppermute | solution.py:38
  92.6 1.6 collective-permute-start.23
  94.7 7.6 %attention.1 = (bf16[2,256,1024]{2,1,0:T(8,128)(2,1)S(1)}, bf16[2,256,1024]{2,1,0:T(8,128)(2,1)S(1)}) custom-call(s32[8]{0:T(128)S(1)} %stack.45.pos, bf16[2,512,512]{2,1,0:T(8,128)(2,1)S(1)} %get-tuple-element.292.q, bf16[2,512,512]{2,1,0:T(8,128)(2,1)S(1)} %get-tuple-element.293.k, bf16[2,512,512]{2,1,0:T(8,128)(2,1)S(1)} %get-tuple-element.294.v, ...), custom_call_target="tpu_custom_call" | custom-call | bytes 1024 | tf_op jit(solution)/shard_map/attention/pallas_call | solution.py:448
  102.3 3.9 %collective-permute-done.23.rest_5_ = bf16[512,512]{1,0:T(8,128)(2,1)S(1)} collective-permute-done((bf16[512,512]{1,0:T(8,128)(2,1)S(1)}, bf16[512,512]{1,0:T(8,128)(2,1)S(1)}, u32[]{:S(2)}, u32[]{:S(2)}) %collective-permute-start.23) | collective-permute-done | bytes 524320 | tf_op jit(solution)/shard_map/ppermute | solution.py:38
  112.2 10.7 %collective-permute-done.26.rest_1_ = bf16[512,512]{1,0:T(8,128)(2,1)S(1)} collective-permute-done((bf16[512,512]{1,0:T(8,128)(2,1)S(1)}, bf16[512,512]{1,0:T(8,128)(2,1)S(1)}, u32[]{:S(2)}, u32[]{:S(2)}) %collective-permute-start.26) | collective-permute-done | bytes 524320 | tf_op jit(solution)/shard_map/ppermute | solution.py:38
  127.0 6.0 %up.1.hidden = bf16[2,2,256,2048]{3,2,1,0:T(8,128)(2,1)S(1)} custom-call(s32[8]{0:T(128)S(1)} %stack.45.pos, bf16[2,256,1024]{2,1,0:T(8,128)(2,1)S(1)} %get-tuple-element.335.own, bf16[2,256,1024]{2,1,0:T(8,128)(2,1)S(1)} %collective-permute-done.32.came, bf16[512,512]{1,0:T(8,128)(2,1)S(1)} %get-tuple-element.320.rest_0_, ...), custom_call_target="tpu_custom_call" | custom-call | bytes 1024 | tf_op jit(solution)/shard_map/up/pallas_call | solution.py:530
  135.3 1.6 collective-permute-start.33
  137.4 1.9 %down.4 = (bf16[2,256,256]{2,1,0:T(8,128)(2,1)S(1)}, bf16[2,256,256]{2,1,0:T(8,128)(2,1)S(1)}) custom-call(s32[8]{0:T(128)S(1)} %stack.45.pos, bf16[2,2,256,2048]{3,2,1,0:T(8,128)(2,1)S(1)} %up.1.hidden, bf16[256,512]{1,0:T(8,128)(2,1)S(1)} %get-tuple-element.342.rest_0_, bf16[256,512]{1,0:T(8,128)(2,1)S(1)} %collective-permute-done.30.rest_1_, ...), custom_call_target="tpu_custom_call" | custom-call | bytes 1024 | tf_op jit(solution)/shard_map/down/pallas_call | solution.py:554
  139.3 3.1 %down.3 = (bf16[2,256,512]{2,1,0:T(8,128)(2,1)S(1)}, bf16[2,256,512]{2,1,0:T(8,128)(2,1)S(1)}) custom-call(s32[8]{0:T(128)S(1)} %stack.45.pos, bf16[2,2,256,2048]{3,2,1,0:T(8,128)(2,1)S(1)} %up.1.hidden, bf16[512,512]{1,0:T(8,128)(2,1)S(1)} %get-tuple-element.338.rest_0_, bf16[512,512]{1,0:T(8,128)(2,1)S(1)} %collective-permute-done.26.rest_1_, ...), custom_call_target="tpu_custom_call" | custom-call | bytes 1024 | tf_op jit(solution)/shard_map/down/pallas_call | solution.py:554
  145.1 1.9 %down.5 = (bf16[2,256,256]{2,1,0:T(8,128)(2,1)S(1)}, bf16[2,256,256]{2,1,0:T(8,128)(2,1)S(1)}) custom-call(s32[8]{0:T(128)S(1)} %stack.45.pos, bf16[2,2,256,2048]{3,2,1,0:T(8,128)(2,1)S(1)} %up.1.hidden, bf16[256,512]{1,0:T(8,128)(2,1)S(1)} %get-tuple-element.356.rest_0_, bf16[256,512]{1,0:T(8,128)(2,1)S(1)} %collective-permute-done.33.rest_1_, ...), custom_call_target="tpu_custom_call" | custom-call | bytes 1024 | tf_op jit(solution)/shard_map/down/pallas_call | solution.py:554
  148.6 1.9 %output.3 = (bf16[2,256,1024]{2,1,0:T(8,128)(2,1)}, f32[32,1,2]{2,1,0:T(1,128)S(1)}) custom-call(s32[8]{0:T(128)S(1)} %stack.45.pos, f32[2,256,1024]{2,1,0:T(8,128)S(1)} %get-tuple-element.354.residual, bf16[2,256,1024]{2,1,0:T(8,128)(2,1)S(1)} %bitcast.19, bf16[2,256,256]{2,1,0:T(8,128)(2,1)S(1)} %get-tuple-element.360.rest_0_, ...), custom_call_target="tpu_custom_call" | custom-call | bytes 1024 | tf_op jit(solution)/shard_map/output/pallas_call | solution.py:608
  150.4 9.5 %all_to_all.5 = f32[32,1,2]{2,1,0:T(1,128)S(1)} all-to-all(f32[32,1,2]{2,1,0:T(1,128)S(1)} %get-tuple-element.369), channel_id=1, replica_groups=mesh['dp'=16,'mp'=2] {'dp','mp'}, dimensions={0} | all-to-all | bytes 512 | tf_op jit(solution)/shard_map/all_to_all | solution.py:757
  (97 shorter events, 42.9 us)
Async XLA Ops:
  2.9 12.7 %collective-permute-start = (bf16[304,512]{1,0:T(8,128)(2,1)}, bf16[304,512]{1,0:T(8,128)(2,1)S(1)}, u32[]{:S(2)}, u32[]{:S(2)}) collective-permute-start(bf16[304,512]{1,0:T(8,128)(2,1)} %get-tuple-element.189.refs_0_), channel_id=1, source_target_pairs={{0,8},{2,10},{4,12},{6,14},{8,16},{10,18},{12,20},{14,22},{16,24},... | collective-permute-start | bytes 933896 | tf_op jit(solution)/shard_map/ppermute | solution.py:38
  16.6 11.4 %collective-permute-start.4 = (bf16[320,512]{1,0:T(8,128)(2,1)S(1)}, bf16[320,512]{1,0:T(8,128)(2,1)S(1)}, u32[]{:S(2)}, u32[]{:S(2)}) collective-permute-start(bf16[320,512]{1,0:T(8,128)(2,1)S(1)} %get-tuple-element.207.refs_2_), channel_id=1, source_target_pairs={{0,4},{2,6},{4,0},{6,2},{8,12},{10,14},{12,8},{14,10},{16,20},{18,... | collective-permute-start | bytes 983048 | tf_op jit(solution)/shard_map/ppermute | solution.py:38
  28.0 18.8 %collective-permute-start.10 = (bf16[512,768]{1,0:T(8,128)(2,1)}, bf16[512,768]{1,0:T(8,128)(2,1)S(1)}, u32[]{:S(2)}, u32[]{:S(2)}) collective-permute-start(bf16[512,768]{1,0:T(8,128)(2,1)} %bitcast.20), channel_id=1, source_target_pairs={{0,1},{1,0},{2,3},{3,2},{4,5},{5,4},{6,7},{7,6},{8,9},{9,8},{10,11... | collective-permute-start | bytes 2359304 | tf_op jit(solution)/shard_map/ppermute | solution.py:92
  28.1 18.7 %collective-permute-start.8 = (bf16[640,512]{1,0:T(8,128)(2,1)S(1)}, bf16[640,512]{1,0:T(8,128)(2,1)S(1)}, u32[]{:S(2)}, u32[]{:S(2)}) collective-permute-start(bf16[640,512]{1,0:T(8,128)(2,1)S(1)} %get-tuple-element.281.rest_2_.rest_0_), channel_id=1, source_target_pairs={{0,2},{2,0},{4,6},{6,4},{8,10},{10,8},{12,14},{14,12},{16,18},{18,... | collective-permute-start | bytes 1966088 | tf_op jit(solution)/shard_map/ppermute | solution.py:38
  29.7 17.1 %collective-permute-start.7 = (bf16[576,512]{1,0:T(8,128)(2,1)S(1)}, bf16[576,512]{1,0:T(8,128)(2,1)S(1)}, u32[]{:S(2)}, u32[]{:S(2)}) collective-permute-start(bf16[576,512]{1,0:T(8,128)(2,1)S(1)} %get-tuple-element.262.rest_0_), channel_id=1, source_target_pairs={{0,4},{2,6},{4,0},{6,2},{8,12},{10,14},{12,8},{14,10},{16,20},{18,... | collective-permute-start | bytes 1769480 | tf_op jit(solution)/shard_map/ppermute | solution.py:38
  30.2 16.6 %collective-permute-start.9 = (bf16[304,512]{1,0:T(8,128)(2,1)S(1)}, bf16[304,512]{1,0:T(8,128)(2,1)S(1)}, u32[]{:S(2)}, u32[]{:S(2)}) collective-permute-start(bf16[304,512]{1,0:T(8,128)(2,1)S(1)} %collective-permute-done.5.refs_0_), channel_id=1, source_target_pairs={{0,8},{2,10},{4,12},{6,14},{8,16},{10,18},{12,20},{14,22},{16,24},... | collective-permute-start | bytes 933896 | tf_op jit(solution)/shard_map/ppermute | solution.py:38
  30.2 16.6 %collective-permute-start.6 = (bf16[256,512]{1,0:T(8,128)(2,1)S(1)}, bf16[256,512]{1,0:T(8,128)(2,1)S(1)}, u32[]{:S(2)}, u32[]{:S(2)}) collective-permute-start(bf16[256,512]{1,0:T(8,128)(2,1)S(1)} %get-tuple-element.255.refs_0_), channel_id=1, source_target_pairs={{0,8},{2,10},{4,12},{6,14},{8,16},{10,18},{12,20},{14,22},{16,24},... | collective-permute-start | bytes 786440 | tf_op jit(solution)/shard_map/ppermute | solution.py:38
  46.9 14.9 %collective-permute-start.13 = (bf16[520,512]{1,0:T(8,128)(2,1)S(1)}, bf16[520,512]{1,0:T(8,128)(2,1)S(1)}, u32[]{:S(2)}, u32[]{:S(2)}) collective-permute-start(bf16[520,512]{1,0:T(8,128)(2,1)S(1)} %stack.50), channel_id=1, source_target_pairs={{0,8},{2,10},{4,12},{6,14},{8,16},{10,18},{12,20},{14,22},{16,24},... | collective-permute-start | bytes 1597448 | tf_op jit(solution)/shard_map/ppermute | solution.py:38
  47.0 12.5 %collective-permute-start.11 = (bf16[352,512]{1,0:T(8,128)(2,1)S(1)}, bf16[352,512]{1,0:T(8,128)(2,1)S(1)}, u32[]{:S(2)}, u32[]{:S(2)}) collective-permute-start(bf16[352,512]{1,0:T(8,128)(2,1)S(1)} %get-tuple-element.233.refs_0_.rest_2_), channel_id=1, source_target_pairs={{0,2},{2,0},{4,6},{6,4},{8,10},{10,8},{12,14},{14,12},{16,18},{18,... | collective-permute-start | bytes 1081352 | tf_op jit(solution)/shard_map/ppermute | solution.py:38
  47.8 11.7 %collective-permute-start.12 = (bf16[352,512]{1,0:T(8,128)(2,1)S(1)}, bf16[352,512]{1,0:T(8,128)(2,1)S(1)}, u32[]{:S(2)}, u32[]{:S(2)}) collective-permute-start(bf16[352,512]{1,0:T(8,128)(2,1)S(1)} %get-tuple-element.235.refs_2_), channel_id=1, source_target_pairs={{0,4},{2,6},{4,0},{6,2},{8,12},{10,14},{12,8},{14,10},{16,20},{18,... | collective-permute-start | bytes 1081352 | tf_op jit(solution)/shard_map/ppermute | solution.py:38
  49.1 10.4 %collective-permute-start.14 = (bf16[96,512]{1,0:T(8,128)(2,1)S(1)}, bf16[96,512]{1,0:T(8,128)(2,1)S(1)}, u32[]{:S(2)}, u32[]{:S(2)}) collective-permute-start(bf16[96,512]{1,0:T(8,128)(2,1)S(1)} %get-tuple-element.230), channel_id=1, source_target_pairs={{0,6},{2,4},{4,2},{6,0},{8,14},{10,12},{12,10},{14,8},{16,22},{18,... | collective-permute-start | bytes 294920 | tf_op jit(solution)/shard_map/ppermute | solution.py:38
  61.8 14.0 %collective-permute-start.15 = (bf16[520,512]{1,0:T(8,128)(2,1)S(1)}, bf16[520,512]{1,0:T(8,128)(2,1)S(1)}, u32[]{:S(2)}, u32[]{:S(2)}) collective-permute-start(bf16[520,512]{1,0:T(8,128)(2,1)S(1)} %collective-permute-done.13.refs_3_.refs_0_), channel_id=1, source_target_pairs={{0,8},{2,10},{4,12},{6,14},{8,16},{10,18},{12,20},{14,22},{16,24},... | collective-permute-start | bytes 1597448 | tf_op jit(solution)/shard_map/ppermute | solution.py:38
  61.9 12.1 %collective-permute-start.16 = (bf16[512,512]{1,0:T(8,128)(2,1)S(1)}, bf16[512,512]{1,0:T(8,128)(2,1)S(1)}, u32[]{:S(2)}, u32[]{:S(2)}) collective-permute-start(bf16[512,512]{1,0:T(8,128)(2,1)S(1)} %get-tuple-element.253.rest_4_), channel_id=1, source_target_pairs={{0,4},{2,6},{4,0},{6,2},{8,12},{10,14},{12,8},{14,10},{16,20},{18,... | collective-permute-start | bytes 1572872 | tf_op jit(solution)/shard_map/ppermute | solution.py:38
  63.5 11.7 %collective-permute-start.17 = (bf16[512,512]{1,0:T(8,128)(2,1)S(1)}, bf16[512,512]{1,0:T(8,128)(2,1)S(1)}, u32[]{:S(2)}, u32[]{:S(2)}) collective-permute-start(bf16[512,512]{1,0:T(8,128)(2,1)S(1)} %get-tuple-element.275.rest_6_.rest_2_), channel_id=1, source_target_pairs={{0,2},{2,0},{4,6},{6,4},{8,10},{10,8},{12,14},{14,12},{16,18},{18,... | collective-permute-start | bytes 1572872 | tf_op jit(solution)/shard_map/ppermute | solution.py:38
  75.8 16.4 %collective-permute-start.18 = (bf16[520,512]{1,0:T(8,128)(2,1)S(1)}, bf16[520,512]{1,0:T(8,128)(2,1)S(1)}, u32[]{:S(2)}, u32[]{:S(2)}) collective-permute-start(bf16[520,512]{1,0:T(8,128)(2,1)S(1)} %stack.52), channel_id=1, source_target_pairs={{0,8},{2,10},{4,12},{6,14},{8,16},{10,18},{12,20},{14,22},{16,24},... | collective-permute-start | bytes 1597448 | tf_op jit(solution)/shard_map/ppermute | solution.py:38
  76.0 14.4 %collective-permute-start.19 = (bf16[512,512]{1,0:T(8,128)(2,1)S(1)}, bf16[512,512]{1,0:T(8,128)(2,1)S(1)}, u32[]{:S(2)}, u32[]{:S(2)}) collective-permute-start(bf16[512,512]{1,0:T(8,128)(2,1)S(1)} %get-tuple-element.320.rest_0_), channel_id=1, source_target_pairs={{0,4},{2,6},{4,0},{6,2},{8,12},{10,14},{12,8},{14,10},{16,20},{18,... | collective-permute-start | bytes 1572872 | tf_op jit(solution)/shard_map/ppermute | solution.py:38
  77.5 14.1 %collective-permute-start.20 = (bf16[512,512]{1,0:T(8,128)(2,1)S(1)}, bf16[512,512]{1,0:T(8,128)(2,1)S(1)}, u32[]{:S(2)}, u32[]{:S(2)}) collective-permute-start(bf16[512,512]{1,0:T(8,128)(2,1)S(1)} %get-tuple-element.322.rest_2_), channel_id=1, source_target_pairs={{0,2},{2,0},{4,6},{6,4},{8,10},{10,8},{12,14},{14,12},{16,18},{18,... | collective-permute-start | bytes 1572872 | tf_op jit(solution)/shard_map/ppermute | solution.py:38
  92.2 15.8 %collective-permute-start.22 = (bf16[520,512]{1,0:T(8,128)(2,1)S(1)}, bf16[520,512]{1,0:T(8,128)(2,1)S(1)}, u32[]{:S(2)}, u32[]{:S(2)}) collective-permute-start(bf16[520,512]{1,0:T(8,128)(2,1)S(1)} %stack.54), channel_id=1, source_target_pairs={{0,8},{2,10},{4,12},{6,14},{8,16},{10,18},{12,20},{14,22},{16,24},... | collective-permute-start | bytes 1597448 | tf_op jit(solution)/shard_map/ppermute | solution.py:38
  92.6 13.6 %collective-permute-start.23 = (bf16[512,512]{1,0:T(8,128)(2,1)S(1)}, bf16[512,512]{1,0:T(8,128)(2,1)S(1)}, u32[]{:S(2)}, u32[]{:S(2)}) collective-permute-start(bf16[512,512]{1,0:T(8,128)(2,1)S(1)} %get-tuple-element.324.rest_4_), channel_id=1, source_target_pairs={{0,4},{2,6},{4,0},{6,2},{8,12},{10,14},{12,8},{14,10},{16,20},{18,... | collective-permute-start | bytes 1572872 | tf_op jit(solution)/shard_map/ppermute | solution.py:38
  94.1 13.3 %collective-permute-start.24 = (bf16[512,512]{1,0:T(8,128)(2,1)S(1)}, bf16[512,512]{1,0:T(8,128)(2,1)S(1)}, u32[]{:S(2)}, u32[]{:S(2)}) collective-permute-start(bf16[512,512]{1,0:T(8,128)(2,1)S(1)} %get-tuple-element.326.rest_6_), channel_id=1, source_target_pairs={{0,2},{2,0},{4,6},{6,4},{8,10},{10,8},{12,14},{14,12},{16,18},{18,... | collective-permute-start | bytes 1572872 | tf_op jit(solution)/shard_map/ppermute | solution.py:38
  108.0 16.3 %collective-permute-start.25 = (bf16[520,512]{1,0:T(8,128)(2,1)S(1)}, bf16[520,512]{1,0:T(8,128)(2,1)S(1)}, u32[]{:S(2)}, u32[]{:S(2)}) collective-permute-start(bf16[520,512]{1,0:T(8,128)(2,1)S(1)} %collective-permute-done.22.refs_3_.refs_0_), channel_id=1, source_target_pairs={{0,8},{2,10},{4,12},{6,14},{8,16},{10,18},{12,20},{14,22},{16,24},... | collective-permute-start | bytes 1597448 | tf_op jit(solution)/shard_map/ppermute | solution.py:38
  108.8 14.1 %collective-permute-start.26 = (bf16[512,512]{1,0:T(8,128)(2,1)S(1)}, bf16[512,512]{1,0:T(8,128)(2,1)S(1)}, u32[]{:S(2)}, u32[]{:S(2)}) collective-permute-start(bf16[512,512]{1,0:T(8,128)(2,1)S(1)} %get-tuple-element.338.rest_0_), channel_id=1, source_target_pairs={{0,4},{2,6},{4,0},{6,2},{8,12},{10,14},{12,8},{14,10},{16,20},{18,... | collective-permute-start | bytes 1572872 | tf_op jit(solution)/shard_map/ppermute | solution.py:38
  109.7 14.1 %collective-permute-start.27 = (bf16[512,512]{1,0:T(8,128)(2,1)S(1)}, bf16[512,512]{1,0:T(8,128)(2,1)S(1)}, u32[]{:S(2)}, u32[]{:S(2)}) collective-permute-start(bf16[512,512]{1,0:T(8,128)(2,1)S(1)} %get-tuple-element.340.rest_2_), channel_id=1, source_target_pairs={{0,2},{2,0},{4,6},{6,4},{8,10},{10,8},{12,14},{14,12},{16,18},{18,... | collective-permute-start | bytes 1572872 | tf_op jit(solution)/shard_map/ppermute | solution.py:38
  124.3 11.0 %collective-permute-start.29 = (bf16[264,512]{1,0:T(8,128)(2,1)S(1)}, bf16[264,512]{1,0:T(8,128)(2,1)S(1)}, u32[]{:S(2)}, u32[]{:S(2)}) collective-permute-start(bf16[264,512]{1,0:T(8,128)(2,1)S(1)} %stack.57), channel_id=1, source_target_pairs={{0,8},{2,10},{4,12},{6,14},{8,16},{10,18},{12,20},{14,22},{16,24},... | collective-permute-start | bytes 811016 | tf_op jit(solution)/shard_map/ppermute | solution.py:38
  (20 other events, 169.2 us)

commit v5 on v4

--- a/solution.py
+++ b/solution.py
@@ -140,9 +140,10 @@
         elif number == 1:
             self.first_z.append(self.move(self.first_z[-1], Z))
             near = [(0, 0, 0), (1, 0, 0)]
-            a, b = stack(self.ends(0, 0), self.ends(0, 1))
-            self.a, self.b = self.chunk(a, near, 0), self.chunk(b, near, 1)
-            self.a_far, self.b_far = self.step(self.a, X), self.step(self.b, Y)
+            a, *b = stack(self.ends(0, 0), self.ends(0, 1)[:1], self.ends(0, 1)[1:])
+            self.a = self.chunk(a, near, 0)
+            self.b = [self.chunk(v, near[i : i + 1], 1) for i, v in enumerate(b)]
+            self.a_far, self.b_far = self.step(self.a, X), [self.step(c, Y) for c in self.b]
             made = stack(*self.own_halves(0), *self.own_halves(1))
             along_x, along_y = [(0, 0, 0), (0, 0, 1)], [(0, 0, 0), (0, 1, 0)]
             self.up_a, self.down_a = ([Chunk(v, along_x, 0, self.half)] for v in made[0::2])
@@ -150,9 +151,10 @@
         elif number == 2:
             self.first_z.append(self.move(self.first_z[-1], Z))
             del self.side_a, self.side_b, self.from_x, self.from_y
-            a, b = stack(self.a.all() + self.a_far.all(), self.b.all() + self.b_far.all())
+            from_b = self.b + self.b_far
+            a, b = stack(self.a.all() + self.a_far.all(), sum((c.all() for c in from_b), []))
             self.a = self.chunk(a, self.a.slots + self.a_far.slots, 0)
-            self.b = self.chunk(b, self.b.slots + self.b_far.slots, 1)
+            self.b = self.chunk(b, sum((c.slots for c in from_b), []), 1)
             self.parts = self.both(self.a, self.b)
             self.up_a.append(self.step(self.up_a[0], Z))
         elif number == 3:
@@ -196,13 +198,17 @@
             self.down_a.append(a)
         elif number == 8:
             del self.z_pair
-            (value,) = stack(self.down_b[2].all() + [self.down_b[2].block(0, 0, SPARE)])
-            self.down_parts.append(self.last(self.down_a[2:3], self.down_b[2:3]))
-            b = self.down_b[2].moved(self.move(value, Z), Z)
-            b.base = 0
-            self.down_b.append(b)
-        elif number == 9:
-            self.down_parts.append(self.last(self.down_a[3:], self.down_b[3:]))
+            far_a, far_b = self.down_a[2:], self.down_b[2]
+            value, near = stack(*(c.all() + [c.block(0, 0, SPARE)] for c in (far_b, far_a[0])))
+            ahead, near = Chunk(value, far_b.slots, 1, self.half), Chunk(near, far_a[0].slots, 0, self.half)
+            corner = ahead.moved(shift(value, self.dims, Z, X), Z)
+            corner = corner.moved(corner.array, X)
+            near_far = self.step(near, Y)
+            b, a = stack(far_b.all(), far_a[1].all())
+            b, a = Chunk(b, far_b.slots, 1, self.half), Chunk(a, far_a[1].slots, 0, self.half)
+            self.down_parts.append(
+                [near, near_far, b, self.step(b, X), a, self.step(a, Y), self.step(b, Z), corner]
+            )
 
     def end_slot(self, *others):
         chunks, arrays = [], []
@@ -571,8 +577,8 @@
     row_ids = m * rows + lax.broadcasted_iota(jnp.int32, (rows, 1), 0)
     if ending:
         before, total_before = rest[n : n + 2]
+        encoded[...] = before[...]
         number = (pos[POS_LEN] + pos[POS_LEN + 1]).astype(jnp.float32) * 0.5
-        encoded[...] = before[...]
         total = total_before[0, 0]
     for i in range(2):
         s = pos[POS_STEP] if i == 0 else 1 - pos[POS_STEP]
@@ -685,39 +691,36 @@
         recv = swap_columns(mine)
         chunks, own_pieces = picked(work.parts, pieces[1:4])
         q, k, v = project(pos, dims, mine, recv, gain_one, chunks, own_pieces, block, width)
-        mine, recv, q, k, v = work.end_slot(mine, recv, q, k, v)
-        work.slot(6)
         chunks, own_pieces = picked(work.parts, pieces[4])
         keep, send = attention(pos, dims, q, k, v, chunks, own_pieces, block, width)
         mine, recv, keep, send = work.end_slot(mine, recv, keep, send)
-        work.slot(7)
+        work.slot(6)
         came = swap_columns(send)
         residual, normed = residual_and_norm(pos, mine, recv, keep, came, gain_two)
         residual, normed = work.end_slot(residual, normed)
-        work.slot(8)
+        work.slot(7)
         normed_came = swap_columns(normed)
         up_pieces = wide_pieces(work.up_parts, block // 2, columns)
         hidden = up_layer(
             pos, dims, normed, normed_came, [c.array for c in work.up_parts], up_pieces, block, units
         )
         residual, hidden = work.end_slot(residual, hidden)
-        work.slot(9)
-        finals, starts = [], []
+        work.slot(8)
+        starts = []
 
         def down_part(part):
             own_pieces = wide_pieces(part, block // 2, columns)
             spots = sorted({p[3][0] for p in own_pieces})
             starts.append(spots)
             size = width // dims[0] * len(spots)
-            kept, sent = down_layer(
+            return down_layer(
                 pos, dims, hidden, [c.array for c in part], own_pieces, block, spots[0], size
             )
-            return [kept, sent]
-
-        ready = down_part(work.down_parts[0]) + down_part(work.down_parts[1])
-        *ready, residual, hidden = work.end_slot(*ready, residual, hidden)
-        finals = [ready[0], swap_columns(ready[1]), ready[2], swap_columns(ready[3])]
-        kept, sent = down_part(work.down_parts[2])
+
+        kept, sent = down_part(work.down_parts[0])
+        kept, sent, residual, hidden = work.end_slot(kept, sent, residual, hidden)
+        finals = [kept, swap_columns(sent)]
+        kept, sent = down_part(work.down_parts[1])
         last = [kept, swap_columns(sent)]
     else:
         *w_three, w_last = [

time: 163 us -> 160 us (0.982)
  waiting for transfers between devices: 77.5 us -> 71.2 us
  starting transfers between devices: 29.3 us -> 33.6 us
    ppermute x31 -> x32, waiting for transfers between devices: 76.3 us -> 69.8 us  [shift(): return lax.ppermute(value, 'dp', pairs)]
    ppermute x31 -> x32, starting transfers between devices: 28.8 us -> 33.1 us  [shift(): return lax.ppermute(value, 'dp', pairs)]
    pallas_call x3 -> x2, Pallas kernels: 6.85 us -> 6.12 us  [down_layer(): pl.pallas_call(functools.partial(down_kernel, n, dims, pieces, block, z_f...]
  transfers between devices with their start and end apart: 38 -> 38, of which waited for: 28 -> 23; matrix products, arithmetic and copies ran while one was open for 1% -> 1% of each run, Pallas kernels for 18% -> 18%
where the time goes in v5:
time: 160 us
  waiting for transfers between devices  71.2 us (44%)
  starting transfers between devices  33.6 us (21%)
  Pallas kernels  33.5 us (21%)
  blocking collectives  9.05 us (6%)
  between operations  6.5 us (4%)
  local copies, waits for them, and re-layouts  5.67 us (4%)
    ppermute x32, waiting for transfers between devices, shift(): return lax.ppermute(value, 'dp', pairs)  69.8 us
    ppermute x32, starting transfers between devices, shift(): return lax.ppermute(value, 'dp', pairs)  33.1 us
    all_to_all x1, blocking collectives, on_device(): sums = lax.all_to_all(sums, ('dp', 'mp'), 0, 0, tiled=True)  9.05 us
    pallas_call x1, Pallas kernels, attention(): pl.pallas_call(functools.partial(attention_kernel, n, dims, pieces, block...  7.59 us
    pallas_call x2, Pallas kernels, down_layer(): pl.pallas_call(functools.partial(down_kernel, n, dims, pieces, block, z_f...  6.12 us
    pallas_call x1, Pallas kernels, up_layer(): pl.pallas_call(functools.partial(up_kernel, n, dims, pieces, block), out_...  5.97 us
    pallas_call x1, Pallas kernels, project(): pl.pallas_call(functools.partial(project_kernel, n, dims, pieces, block),...  4.72 us
  transfers between devices with their start and end apart: 38, of which 23 were waited for; matrix products, arithmetic and copies ran while one was open for 1% of the time, Pallas kernels for 18%

profile of v5, /device:TPU:0, one launch (start us, length us, event | category | flops | bytes accessed | tf_op | source)
XLA Modules:
  0.0 159.6 jit_solution(9017538948857080379)
XLA Ops:
  0.6 2.3 %pack.1 = (bf16[304,512]{1,0:T(8,128)(2,1)}, bf16[256,512]{1,0:T(8,128)(2,1)}, bf16[256,512]{1,0:T(8,128)(2,1)}) custom-call(bf16[48,512]{1,0:T(8,128)(2,1)} %rest_0_.1, bf16[3,64,512]{2,1,0:T(8,128)(2,1)} %rest_1_.1, bf16[64,512]{1,0:T(8,128)(2,1)} %bitcast.24, bf16[64,2048]{1,0:T(8,128)(2,1)} %rest_3_.1, bf16[64,2048]{1,0:T(8,128)(2,1)} %bitcast.23), custom_call_target="tpu_custom_call" | custom-call | bytes 1024 | tf_op jit(solution)/shard_map/pack/pallas_call | solution.py:334
  2.9 3.1 %collective-permute-start = (bf16[304,512]{1,0:T(8,128)(2,1)}, bf16[304,512]{1,0:T(8,128)(2,1)S(1)}, u32[]{:S(2)}, u32[]{:S(2)}) collective-permute-start(bf16[304,512]{1,0:T(8,128)(2,1)} %get-tuple-element.165.refs_0_), channel_id=1, source_target_pairs={{0,8},{2,10},{4,12},{6,14},{8,16},{10,18},{12,20},{14,22},{16,24},... | collective-permute-start | bytes 933896 | tf_op jit(solution)/shard_map/ppermute | solution.py:38
  22.4 2.4 %collective-permute-done.4.refs_4_ = bf16[160,512]{1,0:T(8,128)(2,1)S(1)} collective-permute-done((bf16[160,512]{1,0:T(8,128)(2,1)S(1)}, bf16[160,512]{1,0:T(8,128)(2,1)S(1)}, u32[]{:S(2)}, u32[]{:S(2)}) %collective-permute-start.4) | collective-permute-done | bytes 163872 | tf_op jit(solution)/shard_map/ppermute | solution.py:38
  24.8 1.8 %collective-permute-done.5.refs_5_ = bf16[160,512]{1,0:T(8,128)(2,1)S(1)} collective-permute-done((bf16[160,512]{1,0:T(8,128)(2,1)S(1)}, bf16[160,512]{1,0:T(8,128)(2,1)S(1)}, u32[]{:S(2)}, u32[]{:S(2)}) %collective-permute-start.5) | collective-permute-done | bytes 163872 | tf_op jit(solution)/shard_map/ppermute | solution.py:38
  29.0 1.6 %collective-permute-start.10 = (bf16[304,512]{1,0:T(8,128)(2,1)S(1)}, bf16[304,512]{1,0:T(8,128)(2,1)S(1)}, u32[]{:S(2)}, u32[]{:S(2)}) collective-permute-start(bf16[304,512]{1,0:T(8,128)(2,1)S(1)} %collective-permute-done.6.refs_0_), channel_id=1, source_target_pairs={{0,8},{2,10},{4,12},{6,14},{8,16},{10,18},{12,20},{14,22},{16,24},... | collective-permute-start | bytes 933896 | tf_op jit(solution)/shard_map/ppermute | solution.py:38
  31.3 14.3 %collective-permute-done.7.refs_1_ = bf16[256,512]{1,0:T(8,128)(2,1)S(1)} collective-permute-done((bf16[256,512]{1,0:T(8,128)(2,1)S(1)}, bf16[256,512]{1,0:T(8,128)(2,1)S(1)}, u32[]{:S(2)}, u32[]{:S(2)}) %collective-permute-start.7) | collective-permute-done | bytes 262176 | tf_op jit(solution)/shard_map/ppermute | solution.py:38
  49.3 8.6 %collective-permute-done.15.rest_5_ = bf16[96,512]{1,0:T(8,128)(2,1)S(1)} collective-permute-done((bf16[96,512]{1,0:T(8,128)(2,1)S(1)}, bf16[96,512]{1,0:T(8,128)(2,1)S(1)}, u32[]{:S(2)}, u32[]{:S(2)}) %collective-permute-start.15) | collective-permute-done | bytes 98336 | tf_op jit(solution)/shard_map/ppermute | solution.py:38
  58.3 2.2 %collective-permute-done.14.refs_3_.refs_0_ = bf16[520,512]{1,0:T(8,128)(2,1)S(1)} collective-permute-done((bf16[520,512]{1,0:T(8,128)(2,1)S(1)}, bf16[520,512]{1,0:T(8,128)(2,1)S(1)}, u32[]{:S(2)}, u32[]{:S(2)}) %collective-permute-start.14) | collective-permute-done | bytes 532512 | tf_op jit(solution)/shard_map/ppermute | solution.py:38
  62.5 1.6 embed.1.mine
  64.1 8.6 %collective-permute-done.17.rest_5_ = bf16[512,512]{1,0:T(8,128)(2,1)S(1)} collective-permute-done((bf16[512,512]{1,0:T(8,128)(2,1)S(1)}, bf16[512,512]{1,0:T(8,128)(2,1)S(1)}, u32[]{:S(2)}, u32[]{:S(2)}) %collective-permute-start.17) | collective-permute-done | bytes 524320 | tf_op jit(solution)/shard_map/ppermute | solution.py:38
  73.0 1.6 collective-permute-done.16.refs_0_.refs_1_
  77.2 4.7 %project.1 = (bf16[2,512,512]{2,1,0:T(8,128)(2,1)S(1)}, bf16[2,512,512]{2,1,0:T(8,128)(2,1)S(1)}, bf16[2,512,512]{2,1,0:T(8,128)(2,1)S(1)}) custom-call(s32[8]{0:T(128)S(1)} %stack.44.pos, bf16[2,512,512]{2,1,0:T(8,128)(2,1)S(1)} %embed.1.mine, bf16[2,512,512]{2,1,0:T(8,128)(2,1)S(1)} %collective-permute-done.22.recv, ...), custom_call_target="tpu_custom_call" | custom-call | bytes 1024 | tf_op jit(solution)/shard_map/project/pallas_call | solution.py:403
  81.9 7.6 %attention.1 = (bf16[2,256,1024]{2,1,0:T(8,128)(2,1)S(1)}, bf16[2,256,1024]{2,1,0:T(8,128)(2,1)S(1)}) custom-call(s32[8]{0:T(128)S(1)} %stack.44.pos, bf16[2,512,512]{2,1,0:T(8,128)(2,1)S(1)} %get-tuple-element.251.q, bf16[2,512,512]{2,1,0:T(8,128)(2,1)S(1)} %get-tuple-element.252.k, bf16[2,512,512]{2,1,0:T(8,128)(2,1)S(1)} %get-tuple-element.253.v, ...), custom_call_target="tpu_custom_call" | custom-call | bytes 1024 | tf_op jit(solution)/shard_map/attention/pallas_call | solution.py:454
  89.6 1.5 collective-permute-done.19.refs_1_.refs_2_
  95.3 10.4 %collective-permute-done.24.rest_5_ = bf16[512,512]{1,0:T(8,128)(2,1)S(1)} collective-permute-done((bf16[512,512]{1,0:T(8,128)(2,1)S(1)}, bf16[512,512]{1,0:T(8,128)(2,1)S(1)}, u32[]{:S(2)}, u32[]{:S(2)}) %collective-permute-start.24) | collective-permute-done | bytes 524320 | tf_op jit(solution)/shard_map/ppermute | solution.py:38
  110.8 6.0 %up.1.hidden = bf16[2,2,256,2048]{3,2,1,0:T(8,128)(2,1)S(1)} custom-call(s32[8]{0:T(128)S(1)} %stack.44.pos, bf16[2,256,1024]{2,1,0:T(8,128)(2,1)S(1)} %get-tuple-element.289.own, bf16[2,256,1024]{2,1,0:T(8,128)(2,1)S(1)} %collective-permute-done.30.came, bf16[512,512]{1,0:T(8,128)(2,1)S(1)} %get-tuple-element.278.rest_0_, ...), custom_call_target="tpu_custom_call" | custom-call | bytes 1024 | tf_op jit(solution)/shard_map/up/pallas_call | solution.py:536
  116.8 5.3 %collective-permute-done.28.rest_1_ = bf16[512,512]{1,0:T(8,128)(2,1)S(1)} collective-permute-done((bf16[512,512]{1,0:T(8,128)(2,1)S(1)}, bf16[512,512]{1,0:T(8,128)(2,1)S(1)}, u32[]{:S(2)}, u32[]{:S(2)}) %collective-permute-start.28) | collective-permute-done | bytes 524320 | tf_op jit(solution)/shard_map/ppermute | solution.py:38
  124.5 2.0 %collective-permute-start.35 = (bf16[264,512]{1,0:T(8,128)(2,1)S(1)}, bf16[264,512]{1,0:T(8,128)(2,1)S(1)}, u32[]{:S(2)}, u32[]{:S(2)}) collective-permute-start(bf16[264,512]{1,0:T(8,128)(2,1)S(1)} %get-tuple-element.299), channel_id=1, source_target_pairs={{0,10},{2,8},{4,14},{6,12},{8,18},{10,16},{12,22},{14,20},{16,26},... | collective-permute-start | bytes 811016 | tf_op jit(solution)/shard_map/ppermute | solution.py:38
  127.9 1.8 %collective-permute-start.34 = (bf16[256,512]{1,0:T(8,128)(2,1)S(1)}, bf16[256,512]{1,0:T(8,128)(2,1)S(1)}, u32[]{:S(2)}, u32[]{:S(2)}) collective-permute-start(bf16[256,512]{1,0:T(8,128)(2,1)S(1)} %get-tuple-element.308.rest_2_), channel_id=1, source_target_pairs={{0,8},{2,10},{4,12},{6,14},{8,16},{10,18},{12,20},{14,22},{16,24},... | collective-permute-start | bytes 786440 | tf_op jit(solution)/shard_map/ppermute | solution.py:38
  129.7 3.1 %down.2 = (bf16[2,256,512]{2,1,0:T(8,128)(2,1)S(1)}, bf16[2,256,512]{2,1,0:T(8,128)(2,1)S(1)}) custom-call(s32[8]{0:T(128)S(1)} %stack.44.pos, bf16[2,2,256,2048]{3,2,1,0:T(8,128)(2,1)S(1)} %up.1.hidden, bf16[512,512]{1,0:T(8,128)(2,1)S(1)} %get-tuple-element.292.rest_0_, bf16[512,512]{1,0:T(8,128)(2,1)S(1)} %collective-permute-done.28.rest_1_, ...), custom_call_target="tpu_custom_call" | custom-call | bytes 1024 | tf_op jit(solution)/shard_map/down/pallas_call | solution.py:560
  132.8 6.3 %collective-permute-done.32.rest_3_ = bf16[256,512]{1,0:T(8,128)(2,1)S(1)} collective-permute-done((bf16[256,512]{1,0:T(8,128)(2,1)S(1)}, bf16[256,512]{1,0:T(8,128)(2,1)S(1)}, u32[]{:S(2)}, u32[]{:S(2)}) %collective-permute-start.32) | collective-permute-done | bytes 262176 | tf_op jit(solution)/shard_map/ppermute | solution.py:38
  140.5 3.1 %down.3 = (bf16[2,256,512]{2,1,0:T(8,128)(2,1)S(1)}, bf16[2,256,512]{2,1,0:T(8,128)(2,1)S(1)}) custom-call(s32[8]{0:T(128)S(1)} %stack.44.pos, bf16[2,2,256,2048]{3,2,1,0:T(8,128)(2,1)S(1)} %up.1.hidden, bf16[264,512]{1,0:T(8,128)(2,1)S(1)} %get-tuple-element.306.rest_0_, bf16[264,512]{1,0:T(8,128)(2,1)S(1)} %collective-permute-done.31.rest_1_, ...), custom_call_target="tpu_custom_call" | custom-call | bytes 1024 | tf_op jit(solution)/shard_map/down/pallas_call | solution.py:560
  145.6 1.9 %output.3 = (bf16[2,256,1024]{2,1,0:T(8,128)(2,1)}, f32[32,1,2]{2,1,0:T(1,128)S(1)}) custom-call(s32[8]{0:T(128)S(1)} %stack.44.pos, f32[2,256,1024]{2,1,0:T(8,128)S(1)} %get-tuple-element.304.residual, bf16[2,256,1024]{2,1,0:T(8,128)(2,1)S(1)} %bitcast.19, bf16[2,256,512]{2,1,0:T(8,128)(2,1)S(1)} %get-tuple-element.314.rest_0_, ...), custom_call_target="tpu_custom_call" | custom-call | bytes 1024 | tf_op jit(solution)/shard_map/output/pallas_call | solution.py:614
  147.6 9.0 %all_to_all.5 = f32[32,1,2]{2,1,0:T(1,128)S(1)} all-to-all(f32[32,1,2]{2,1,0:T(1,128)S(1)} %get-tuple-element.321), channel_id=1, replica_groups=mesh['dp'=16,'mp'=2] {'dp','mp'}, dimensions={0} | all-to-all | bytes 512 | tf_op jit(solution)/shard_map/all_to_all | solution.py:760
  (95 shorter events, 42.3 us)
Async XLA Ops:
  2.9 12.7 %collective-permute-start = (bf16[304,512]{1,0:T(8,128)(2,1)}, bf16[304,512]{1,0:T(8,128)(2,1)S(1)}, u32[]{:S(2)}, u32[]{:S(2)}) collective-permute-start(bf16[304,512]{1,0:T(8,128)(2,1)} %get-tuple-element.165.refs_0_), channel_id=1, source_target_pairs={{0,8},{2,10},{4,12},{6,14},{8,16},{10,18},{12,20},{14,22},{16,24},... | collective-permute-start | bytes 933896 | tf_op jit(solution)/shard_map/ppermute | solution.py:38
  26.5 19.1 %collective-permute-start.11 = (bf16[512,768]{1,0:T(8,128)(2,1)}, bf16[512,768]{1,0:T(8,128)(2,1)S(1)}, u32[]{:S(2)}, u32[]{:S(2)}) collective-permute-start(bf16[512,768]{1,0:T(8,128)(2,1)} %bitcast.20), channel_id=1, source_target_pairs={{0,1},{1,0},{2,3},{3,2},{4,5},{5,4},{6,7},{7,6},{8,9},{9,8},{10,11... | collective-permute-start | bytes 2359304 | tf_op jit(solution)/shard_map/ppermute | solution.py:92
  26.6 18.9 %collective-permute-start.9 = (bf16[640,512]{1,0:T(8,128)(2,1)S(1)}, bf16[640,512]{1,0:T(8,128)(2,1)S(1)}, u32[]{:S(2)}, u32[]{:S(2)}) collective-permute-start(bf16[640,512]{1,0:T(8,128)(2,1)S(1)} %get-tuple-element.243.rest_2_.rest_0_), channel_id=1, source_target_pairs={{0,2},{2,0},{4,6},{6,4},{8,10},{10,8},{12,14},{14,12},{16,18},{18,... | collective-permute-start | bytes 1966088 | tf_op jit(solution)/shard_map/ppermute | solution.py:38
  27.5 18.1 %collective-permute-start.8 = (bf16[576,512]{1,0:T(8,128)(2,1)S(1)}, bf16[576,512]{1,0:T(8,128)(2,1)S(1)}, u32[]{:S(2)}, u32[]{:S(2)}) collective-permute-start(bf16[576,512]{1,0:T(8,128)(2,1)S(1)} %get-tuple-element.241.rest_0_), channel_id=1, source_target_pairs={{0,4},{2,6},{4,0},{6,2},{8,12},{10,14},{12,8},{14,10},{16,20},{18,... | collective-permute-start | bytes 1769480 | tf_op jit(solution)/shard_map/ppermute | solution.py:38
  29.0 16.6 %collective-permute-start.10 = (bf16[304,512]{1,0:T(8,128)(2,1)S(1)}, bf16[304,512]{1,0:T(8,128)(2,1)S(1)}, u32[]{:S(2)}, u32[]{:S(2)}) collective-permute-start(bf16[304,512]{1,0:T(8,128)(2,1)S(1)} %collective-permute-done.6.refs_0_), channel_id=1, source_target_pairs={{0,8},{2,10},{4,12},{6,14},{8,16},{10,18},{12,20},{14,22},{16,24},... | collective-permute-start | bytes 933896 | tf_op jit(solution)/shard_map/ppermute | solution.py:38
  30.6 15.0 %collective-permute-start.7 = (bf16[256,512]{1,0:T(8,128)(2,1)S(1)}, bf16[256,512]{1,0:T(8,128)(2,1)S(1)}, u32[]{:S(2)}, u32[]{:S(2)}) collective-permute-start(bf16[256,512]{1,0:T(8,128)(2,1)S(1)} %get-tuple-element.234.refs_0_), channel_id=1, source_target_pairs={{0,8},{2,10},{4,12},{6,14},{8,16},{10,18},{12,20},{14,22},{16,24},... | collective-permute-start | bytes 786440 | tf_op jit(solution)/shard_map/ppermute | solution.py:38
  45.6 14.9 %collective-permute-start.14 = (bf16[520,512]{1,0:T(8,128)(2,1)S(1)}, bf16[520,512]{1,0:T(8,128)(2,1)S(1)}, u32[]{:S(2)}, u32[]{:S(2)}) collective-permute-start(bf16[520,512]{1,0:T(8,128)(2,1)S(1)} %stack.49), channel_id=1, source_target_pairs={{0,8},{2,10},{4,12},{6,14},{8,16},{10,18},{12,20},{14,22},{16,24},... | collective-permute-start | bytes 1597448 | tf_op jit(solution)/shard_map/ppermute | solution.py:38
  45.8 12.1 %collective-permute-start.12 = (bf16[352,512]{1,0:T(8,128)(2,1)S(1)}, bf16[352,512]{1,0:T(8,128)(2,1)S(1)}, u32[]{:S(2)}, u32[]{:S(2)}) collective-permute-start(bf16[352,512]{1,0:T(8,128)(2,1)S(1)} %get-tuple-element.212.refs_0_.rest_2_), channel_id=1, source_target_pairs={{0,2},{2,0},{4,6},{6,4},{8,10},{10,8},{12,14},{14,12},{16,18},{18,... | collective-permute-start | bytes 1081352 | tf_op jit(solution)/shard_map/ppermute | solution.py:38
  60.6 14.0 %collective-permute-start.16 = (bf16[520,512]{1,0:T(8,128)(2,1)S(1)}, bf16[520,512]{1,0:T(8,128)(2,1)S(1)}, u32[]{:S(2)}, u32[]{:S(2)}) collective-permute-start(bf16[520,512]{1,0:T(8,128)(2,1)S(1)} %collective-permute-done.14.refs_3_.refs_0_), channel_id=1, source_target_pairs={{0,8},{2,10},{4,12},{6,14},{8,16},{10,18},{12,20},{14,22},{16,24},... | collective-permute-start | bytes 1597448 | tf_op jit(solution)/shard_map/ppermute | solution.py:38
  60.6 12.0 %collective-permute-start.17 = (bf16[512,512]{1,0:T(8,128)(2,1)S(1)}, bf16[512,512]{1,0:T(8,128)(2,1)S(1)}, u32[]{:S(2)}, u32[]{:S(2)}) collective-permute-start(bf16[512,512]{1,0:T(8,128)(2,1)S(1)} %get-tuple-element.232.rest_4_), channel_id=1, source_target_pairs={{0,4},{2,6},{4,0},{6,2},{8,12},{10,14},{12,8},{14,10},{16,20},{18,... | collective-permute-start | bytes 1572872 | tf_op jit(solution)/shard_map/ppermute | solution.py:38
  74.6 16.5 %collective-permute-start.19 = (bf16[520,512]{1,0:T(8,128)(2,1)S(1)}, bf16[520,512]{1,0:T(8,128)(2,1)S(1)}, u32[]{:S(2)}, u32[]{:S(2)}) collective-permute-start(bf16[520,512]{1,0:T(8,128)(2,1)S(1)} %stack.51), channel_id=1, source_target_pairs={{0,8},{2,10},{4,12},{6,14},{8,16},{10,18},{12,20},{14,22},{16,24},... | collective-permute-start | bytes 1597448 | tf_op jit(solution)/shard_map/ppermute | solution.py:38
  74.9 14.6 %collective-permute-start.20 = (bf16[512,512]{1,0:T(8,128)(2,1)S(1)}, bf16[512,512]{1,0:T(8,128)(2,1)S(1)}, u32[]{:S(2)}, u32[]{:S(2)}) collective-permute-start(bf16[512,512]{1,0:T(8,128)(2,1)S(1)} %get-tuple-element.278.rest_0_), channel_id=1, source_target_pairs={{0,4},{2,6},{4,0},{6,2},{8,12},{10,14},{12,8},{14,10},{16,20},{18,... | collective-permute-start | bytes 1572872 | tf_op jit(solution)/shard_map/ppermute | solution.py:38
  75.7 13.9 %collective-permute-start.21 = (bf16[512,512]{1,0:T(8,128)(2,1)S(1)}, bf16[512,512]{1,0:T(8,128)(2,1)S(1)}, u32[]{:S(2)}, u32[]{:S(2)}) collective-permute-start(bf16[512,512]{1,0:T(8,128)(2,1)S(1)} %get-tuple-element.280.rest_2_), channel_id=1, source_target_pairs={{0,2},{2,0},{4,6},{6,4},{8,10},{10,8},{12,14},{14,12},{16,18},{18,... | collective-permute-start | bytes 1572872 | tf_op jit(solution)/shard_map/ppermute | solution.py:38
  91.2 16.4 %collective-permute-start.23 = (bf16[520,512]{1,0:T(8,128)(2,1)S(1)}, bf16[520,512]{1,0:T(8,128)(2,1)S(1)}, u32[]{:S(2)}, u32[]{:S(2)}) collective-permute-start(bf16[520,512]{1,0:T(8,128)(2,1)S(1)} %stack.53), channel_id=1, source_target_pairs={{0,8},{2,10},{4,12},{6,14},{8,16},{10,18},{12,20},{14,22},{16,24},... | collective-permute-start | bytes 1597448 | tf_op jit(solution)/shard_map/ppermute | solution.py:38
  91.3 14.4 %collective-permute-start.24 = (bf16[512,512]{1,0:T(8,128)(2,1)S(1)}, bf16[512,512]{1,0:T(8,128)(2,1)S(1)}, u32[]{:S(2)}, u32[]{:S(2)}) collective-permute-start(bf16[512,512]{1,0:T(8,128)(2,1)S(1)} %get-tuple-element.282.rest_4_), channel_id=1, source_target_pairs={{0,4},{2,6},{4,0},{6,2},{8,12},{10,14},{12,8},{14,10},{16,20},{18,... | collective-permute-start | bytes 1572872 | tf_op jit(solution)/shard_map/ppermute | solution.py:38
  92.5 13.8 %collective-permute-start.25 = (bf16[512,512]{1,0:T(8,128)(2,1)S(1)}, bf16[512,512]{1,0:T(8,128)(2,1)S(1)}, u32[]{:S(2)}, u32[]{:S(2)}) collective-permute-start(bf16[512,512]{1,0:T(8,128)(2,1)S(1)} %get-tuple-element.284.rest_6_), channel_id=1, source_target_pairs={{0,2},{2,0},{4,6},{6,4},{8,10},{10,8},{12,14},{14,12},{16,18},{18,... | collective-permute-start | bytes 1572872 | tf_op jit(solution)/shard_map/ppermute | solution.py:38
  107.5 16.3 %collective-permute-start.27 = (bf16[520,512]{1,0:T(8,128)(2,1)S(1)}, bf16[520,512]{1,0:T(8,128)(2,1)S(1)}, u32[]{:S(2)}, u32[]{:S(2)}) collective-permute-start(bf16[520,512]{1,0:T(8,128)(2,1)S(1)} %collective-permute-done.23.refs_3_.refs_1_), channel_id=1, source_target_pairs={{0,8},{2,10},{4,12},{6,14},{8,16},{10,18},{12,20},{14,22},{16,24},... | collective-permute-start | bytes 1597448 | tf_op jit(solution)/shard_map/ppermute | solution.py:38
  108.1 14.0 %collective-permute-start.28 = (bf16[512,512]{1,0:T(8,128)(2,1)S(1)}, bf16[512,512]{1,0:T(8,128)(2,1)S(1)}, u32[]{:S(2)}, u32[]{:S(2)}) collective-permute-start(bf16[512,512]{1,0:T(8,128)(2,1)S(1)} %get-tuple-element.292.rest_0_), channel_id=1, source_target_pairs={{0,4},{2,6},{4,0},{6,2},{8,12},{10,14},{12,8},{14,10},{16,20},{18,... | collective-permute-start | bytes 1572872 | tf_op jit(solution)/shard_map/ppermute | solution.py:38
  109.5 13.8 %collective-permute-start.29 = (bf16[512,512]{1,0:T(8,128)(2,1)S(1)}, bf16[512,512]{1,0:T(8,128)(2,1)S(1)}, u32[]{:S(2)}, u32[]{:S(2)}) collective-permute-start(bf16[512,512]{1,0:T(8,128)(2,1)S(1)} %get-tuple-element.294.rest_2_), channel_id=1, source_target_pairs={{0,2},{2,0},{4,6},{6,4},{8,10},{10,8},{12,14},{14,12},{16,18},{18,... | collective-permute-start | bytes 1572872 | tf_op jit(solution)/shard_map/ppermute | solution.py:38
  123.9 16.6 %collective-permute-start.31 = (bf16[264,512]{1,0:T(8,128)(2,1)S(1)}, bf16[264,512]{1,0:T(8,128)(2,1)S(1)}, u32[]{:S(2)}, u32[]{:S(2)}) collective-permute-start(bf16[264,512]{1,0:T(8,128)(2,1)S(1)} %get-tuple-element.306.rest_0_), channel_id=1, source_target_pairs={{0,4},{2,6},{4,0},{6,2},{8,12},{10,14},{12,8},{14,10},{16,20},{18,... | collective-permute-start | bytes 811016 | tf_op jit(solution)/shard_map/ppermute | solution.py:38
  124.5 16.0 %collective-permute-start.35 = (bf16[264,512]{1,0:T(8,128)(2,1)S(1)}, bf16[264,512]{1,0:T(8,128)(2,1)S(1)}, u32[]{:S(2)}, u32[]{:S(2)}) collective-permute-start(bf16[264,512]{1,0:T(8,128)(2,1)S(1)} %get-tuple-element.299), channel_id=1, source_target_pairs={{0,10},{2,8},{4,14},{6,12},{8,18},{10,16},{12,22},{14,20},{16,26},... | collective-permute-start | bytes 811016 | tf_op jit(solution)/shard_map/ppermute | solution.py:38
  126.5 12.6 %collective-permute-start.32 = (bf16[256,512]{1,0:T(8,128)(2,1)S(1)}, bf16[256,512]{1,0:T(8,128)(2,1)S(1)}, u32[]{:S(2)}, u32[]{:S(2)}) collective-permute-start(bf16[256,512]{1,0:T(8,128)(2,1)S(1)} %get-tuple-element.308.rest_2_), channel_id=1, source_target_pairs={{0,2},{2,0},{4,6},{6,4},{8,10},{10,8},{12,14},{14,12},{16,18},{18,... | collective-permute-start | bytes 786440 | tf_op jit(solution)/shard_map/ppermute | solution.py:38
  127.3 11.8 %collective-permute-start.33 = (bf16[256,512]{1,0:T(8,128)(2,1)S(1)}, bf16[256,512]{1,0:T(8,128)(2,1)S(1)}, u32[]{:S(2)}, u32[]{:S(2)}) collective-permute-start(bf16[256,512]{1,0:T(8,128)(2,1)S(1)} %get-tuple-element.310.rest_4_), channel_id=1, source_target_pairs={{0,4},{2,6},{4,0},{6,2},{8,12},{10,14},{12,8},{14,10},{16,20},{18,... | collective-permute-start | bytes 786440 | tf_op jit(solution)/shard_map/ppermute | solution.py:38
  127.9 12.6 %collective-permute-start.34 = (bf16[256,512]{1,0:T(8,128)(2,1)S(1)}, bf16[256,512]{1,0:T(8,128)(2,1)S(1)}, u32[]{:S(2)}, u32[]{:S(2)}) collective-permute-start(bf16[256,512]{1,0:T(8,128)(2,1)S(1)} %get-tuple-element.308.rest_2_), channel_id=1, source_target_pairs={{0,8},{2,10},{4,12},{6,14},{8,16},{10,18},{12,20},{14,22},{16,24},... | collective-permute-start | bytes 786440 | tf_op jit(solution)/shard_map/ppermute | solution.py:38
  (20 other events, 184.1 us)

commit v6 on v5

--- a/solution.py
+++ b/solution.py
@@ -673,11 +673,11 @@
         spans = ((0, cut), (cut, last), (block_e, far_cut), (far_cut, last), (0, block_e), (0, far_cut))
         work = Gather(*pack(shards, up, down), spans, dims)
         work.slot(0)
-        picture, pos, gain_one = work.end_slot(picture, pos, gain_one)
+        other_picture = swap_columns(picture)
+        other_picture, picture, pos, gain_one = work.end_slot(other_picture, picture, pos, gain_one)
         work.slot(1)
-        picture, pos, gain_one = work.end_slot(picture, pos, gain_one)
+        other_picture, picture, pos, gain_one = work.end_slot(other_picture, picture, pos, gain_one)
         work.slot(2)
-        other_picture = swap_columns(picture)
         other_picture, picture = work.end_slot(other_picture, picture)
         work.slot(3)
         other_picture, picture = work.end_slot(other_picture, picture)

time: 160 us -> 156 us (0.975)
  starting transfers between devices: 33.6 us -> 30.3 us
  waiting for transfers between devices: 71.2 us -> 69.6 us
    ppermute x32, starting transfers between devices: 33.1 us -> 29.2 us  [shift(): return lax.ppermute(value, 'dp', pairs)]
    ppermute x32, waiting for transfers between devices: 69.8 us -> 66 us  [shift(): return lax.ppermute(value, 'dp', pairs)]
    ppermute x6, waiting for transfers between devices: 1.44 us -> 3.61 us  [swap_columns(): return lax.ppermute(value, 'mp', [(0, 1), (1, 0)])]
  transfers between devices with their start and end apart: 38 -> 38, of which waited for: 23 -> 24; matrix products, arithmetic and copies ran while one was open for 1% -> 1% of each run, Pallas kernels for 18% -> 20%
where the time goes in v6:
time: 156 us
  waiting for transfers between devices  69.6 us (45%)
  Pallas kernels  33.4 us (21%)
  starting transfers between devices  30.3 us (19%)
  blocking collectives  10.1 us (6%)
  between operations  6.48 us (4%)
  local copies, waits for them, and re-layouts  5.66 us (4%)
    ppermute x32, waiting for transfers between devices, shift(): return lax.ppermute(value, 'dp', pairs)  66 us
    ppermute x32, starting transfers between devices, shift(): return lax.ppermute(value, 'dp', pairs)  29.2 us
    all_to_all x1, blocking collectives, on_device(): sums = lax.all_to_all(sums, ('dp', 'mp'), 0, 0, tiled=True)  10.1 us
    pallas_call x1, Pallas kernels, attention(): pl.pallas_call(functools.partial(attention_kernel, n, dims, pieces, block...  7.61 us
    pallas_call x2, Pallas kernels, down_layer(): pl.pallas_call(functools.partial(down_kernel, n, dims, pieces, block, z_f...  6.13 us
    pallas_call x1, Pallas kernels, up_layer(): pl.pallas_call(functools.partial(up_kernel, n, dims, pieces, block), out_...  5.96 us
    pallas_call x1, Pallas kernels, project(): pl.pallas_call(functools.partial(project_kernel, n, dims, pieces, block),...  4.71 us
    ppermute x6, waiting for transfers between devices, swap_columns(): return lax.ppermute(value, 'mp', [(0, 1), (1, 0)])  3.61 us
  transfers between devices with their start and end apart: 38, of which 24 were waited for; matrix products, arithmetic and copies ran while one was open for 1% of the time, Pallas kernels for 20%

profile of v6, /device:TPU:0, one launch (start us, length us, event | category | flops | bytes accessed | tf_op | source)
XLA Modules:
  0.0 155.5 jit_solution(18146409581719173793)
XLA Ops:
  1.2 2.2 %pack.1 = (bf16[304,512]{1,0:T(8,128)(2,1)}, bf16[256,512]{1,0:T(8,128)(2,1)}, bf16[256,512]{1,0:T(8,128)(2,1)}) custom-call(bf16[48,512]{1,0:T(8,128)(2,1)} %rest_0_.1, bf16[3,64,512]{2,1,0:T(8,128)(2,1)} %rest_1_.1, bf16[64,512]{1,0:T(8,128)(2,1)} %bitcast.24, bf16[64,2048]{1,0:T(8,128)(2,1)} %rest_3_.1, bf16[64,2048]{1,0:T(8,128)(2,1)} %bitcast.23), custom_call_target="tpu_custom_call" | custom-call | bytes 1024 | tf_op jit(solution)/shard_map/pack/pallas_call | solution.py:334
  3.4 2.7 %collective-permute-start = (bf16[304,512]{1,0:T(8,128)(2,1)}, bf16[304,512]{1,0:T(8,128)(2,1)S(1)}, u32[]{:S(2)}, u32[]{:S(2)}) collective-permute-start(bf16[304,512]{1,0:T(8,128)(2,1)} %get-tuple-element.167.refs_0_), channel_id=1, source_target_pairs={{0,8},{2,10},{4,12},{6,14},{8,16},{10,18},{12,20},{14,22},{16,24},... | collective-permute-start | bytes 933896 | tf_op jit(solution)/shard_map/ppermute | solution.py:38
  23.0 3.1 %collective-permute-done.5.refs_4_ = bf16[160,512]{1,0:T(8,128)(2,1)S(1)} collective-permute-done((bf16[160,512]{1,0:T(8,128)(2,1)S(1)}, bf16[160,512]{1,0:T(8,128)(2,1)S(1)}, u32[]{:S(2)}, u32[]{:S(2)}) %collective-permute-start.5) | collective-permute-done | bytes 163872 | tf_op jit(solution)/shard_map/ppermute | solution.py:38
  26.1 1.8 %collective-permute-done.6.refs_5_ = bf16[160,512]{1,0:T(8,128)(2,1)S(1)} collective-permute-done((bf16[160,512]{1,0:T(8,128)(2,1)S(1)}, bf16[160,512]{1,0:T(8,128)(2,1)S(1)}, u32[]{:S(2)}, u32[]{:S(2)}) %collective-permute-start.6) | collective-permute-done | bytes 163872 | tf_op jit(solution)/shard_map/ppermute | solution.py:38
  32.6 12.5 %collective-permute-done.8.refs_1_ = bf16[256,512]{1,0:T(8,128)(2,1)S(1)} collective-permute-done((bf16[256,512]{1,0:T(8,128)(2,1)S(1)}, bf16[256,512]{1,0:T(8,128)(2,1)S(1)}, u32[]{:S(2)}, u32[]{:S(2)}) %collective-permute-start.8) | collective-permute-done | bytes 262176 | tf_op jit(solution)/shard_map/ppermute | solution.py:38
  46.8 2.1 %collective-permute-start.15 = (bf16[96,512]{1,0:T(8,128)(2,1)S(1)}, bf16[96,512]{1,0:T(8,128)(2,1)S(1)}, u32[]{:S(2)}, u32[]{:S(2)}) collective-permute-start(bf16[96,512]{1,0:T(8,128)(2,1)S(1)} %get-tuple-element.213), channel_id=1, source_target_pairs={{0,6},{2,4},{4,2},{6,0},{8,14},{10,12},{12,10},{14,8},{16,22},{18,... | collective-permute-start | bytes 294920 | tf_op jit(solution)/shard_map/ppermute | solution.py:38
  48.9 6.2 %collective-permute-done.15.rest_5_ = bf16[96,512]{1,0:T(8,128)(2,1)S(1)} collective-permute-done((bf16[96,512]{1,0:T(8,128)(2,1)S(1)}, bf16[96,512]{1,0:T(8,128)(2,1)S(1)}, u32[]{:S(2)}, u32[]{:S(2)}) %collective-permute-start.15) | collective-permute-done | bytes 98336 | tf_op jit(solution)/shard_map/ppermute | solution.py:38
  55.5 2.9 %collective-permute-done.14.refs_3_.refs_0_ = bf16[520,512]{1,0:T(8,128)(2,1)S(1)} collective-permute-done((bf16[520,512]{1,0:T(8,128)(2,1)S(1)}, bf16[520,512]{1,0:T(8,128)(2,1)S(1)}, u32[]{:S(2)}, u32[]{:S(2)}) %collective-permute-start.14) | collective-permute-done | bytes 532512 | tf_op jit(solution)/shard_map/ppermute | solution.py:38
  59.5 1.6 %embed.1.mine = bf16[2,512,512]{2,1,0:T(8,128)(2,1)S(1)} custom-call(s32[8]{0:T(128)S(1)} %stack.44.pos, bf16[512,768]{1,0:T(8,128)(2,1)S(1)} %bitcast.21, bf16[512,768]{1,0:T(8,128)(2,1)S(1)} %collective-permute-done.3.other, bf16[576,512]{1,0:T(8,128)(2,1)S(1)} %get-tuple-element.245.rest_0_, bf16[576,512]{1,0:T(8,128)(2,1)S(1)} %collective-permute-done.9.rest_1_, ...), custom_call_target="tpu_custom_call" | custom-call | bytes 1024 | tf_op jit(solution)/shard_map/embed/pallas_call | solution.py:356
  61.1 7.5 %collective-permute-done.17.rest_5_ = bf16[512,512]{1,0:T(8,128)(2,1)S(1)} collective-permute-done((bf16[512,512]{1,0:T(8,128)(2,1)S(1)}, bf16[512,512]{1,0:T(8,128)(2,1)S(1)}, u32[]{:S(2)}, u32[]{:S(2)}) %collective-permute-start.17) | collective-permute-done | bytes 524320 | tf_op jit(solution)/shard_map/ppermute | solution.py:38
  68.9 1.6 %collective-permute-done.16.refs_0_.refs_1_ = bf16[520,512]{1,0:T(8,128)(2,1)S(1)} collective-permute-done((bf16[520,512]{1,0:T(8,128)(2,1)S(1)}, bf16[520,512]{1,0:T(8,128)(2,1)S(1)}, u32[]{:S(2)}, u32[]{:S(2)}) %collective-permute-start.16) | collective-permute-done | bytes 532512 | tf_op jit(solution)/shard_map/ppermute | solution.py:38
  73.1 4.7 %project.1 = (bf16[2,512,512]{2,1,0:T(8,128)(2,1)S(1)}, bf16[2,512,512]{2,1,0:T(8,128)(2,1)S(1)}, bf16[2,512,512]{2,1,0:T(8,128)(2,1)S(1)}) custom-call(s32[8]{0:T(128)S(1)} %stack.44.pos, bf16[2,512,512]{2,1,0:T(8,128)(2,1)S(1)} %embed.1.mine, bf16[2,512,512]{2,1,0:T(8,128)(2,1)S(1)} %collective-permute-done.22.recv, ...), custom_call_target="tpu_custom_call" | custom-call | bytes 1024 | tf_op jit(solution)/shard_map/project/pallas_call | solution.py:403
  77.9 7.6 %attention.1 = (bf16[2,256,1024]{2,1,0:T(8,128)(2,1)S(1)}, bf16[2,256,1024]{2,1,0:T(8,128)(2,1)S(1)}) custom-call(s32[8]{0:T(128)S(1)} %stack.44.pos, bf16[2,512,512]{2,1,0:T(8,128)(2,1)S(1)} %get-tuple-element.255.q, bf16[2,512,512]{2,1,0:T(8,128)(2,1)S(1)} %get-tuple-element.256.k, bf16[2,512,512]{2,1,0:T(8,128)(2,1)S(1)} %get-tuple-element.257.v, ...), custom_call_target="tpu_custom_call" | custom-call | bytes 1024 | tf_op jit(solution)/shard_map/attention/pallas_call | solution.py:454
  88.1 1.7 %collective-permute-done.26.came = bf16[2,256,1024]{2,1,0:T(8,128)(2,1)S(1)} collective-permute-done((bf16[2,256,1024]{2,1,0:T(8,128)(2,1)S(1)}, bf16[2,256,1024]{2,1,0:T(8,128)(2,1)S(1)}, u32[]{:S(2)}, u32[]{:S(2)}) %collective-permute-start.26) | collective-permute-done | bytes 1048608 | tf_op jit(solution)/shard_map/ppermute | solution.py:92
  91.2 10.4 %collective-permute-done.24.rest_5_ = bf16[512,512]{1,0:T(8,128)(2,1)S(1)} collective-permute-done((bf16[512,512]{1,0:T(8,128)(2,1)S(1)}, bf16[512,512]{1,0:T(8,128)(2,1)S(1)}, u32[]{:S(2)}, u32[]{:S(2)}) %collective-permute-start.24) | collective-permute-done | bytes 524320 | tf_op jit(solution)/shard_map/ppermute | solution.py:38
  101.9 1.6 %collective-permute-done.23.refs_3_.refs_1_ = bf16[520,512]{1,0:T(8,128)(2,1)S(1)} collective-permute-done((bf16[520,512]{1,0:T(8,128)(2,1)S(1)}, bf16[520,512]{1,0:T(8,128)(2,1)S(1)}, u32[]{:S(2)}, u32[]{:S(2)}) %collective-permute-start.23) | collective-permute-done | bytes 532512 | tf_op jit(solution)/shard_map/ppermute | solution.py:38
  106.1 6.0 %up.1.hidden = bf16[2,2,256,2048]{3,2,1,0:T(8,128)(2,1)S(1)} custom-call(s32[8]{0:T(128)S(1)} %stack.44.pos, bf16[2,256,1024]{2,1,0:T(8,128)(2,1)S(1)} %get-tuple-element.293.own, bf16[2,256,1024]{2,1,0:T(8,128)(2,1)S(1)} %collective-permute-done.30.came, bf16[512,512]{1,0:T(8,128)(2,1)S(1)} %get-tuple-element.282.rest_0_, ...), custom_call_target="tpu_custom_call" | custom-call | bytes 1024 | tf_op jit(solution)/shard_map/up/pallas_call | solution.py:536
  112.1 5.9 %collective-permute-done.28.rest_1_ = bf16[512,512]{1,0:T(8,128)(2,1)S(1)} collective-permute-done((bf16[512,512]{1,0:T(8,128)(2,1)S(1)}, bf16[512,512]{1,0:T(8,128)(2,1)S(1)}, u32[]{:S(2)}, u32[]{:S(2)}) %collective-permute-start.28) | collective-permute-done | bytes 524320 | tf_op jit(solution)/shard_map/ppermute | solution.py:38
  123.8 1.9 %collective-permute-start.34 = (bf16[256,512]{1,0:T(8,128)(2,1)S(1)}, bf16[256,512]{1,0:T(8,128)(2,1)S(1)}, u32[]{:S(2)}, u32[]{:S(2)}) collective-permute-start(bf16[256,512]{1,0:T(8,128)(2,1)S(1)} %get-tuple-element.312.rest_2_), channel_id=1, source_target_pairs={{0,8},{2,10},{4,12},{6,14},{8,16},{10,18},{12,20},{14,22},{16,24},... | collective-permute-start | bytes 786440 | tf_op jit(solution)/shard_map/ppermute | solution.py:38
  125.7 3.1 %down.2 = (bf16[2,256,512]{2,1,0:T(8,128)(2,1)S(1)}, bf16[2,256,512]{2,1,0:T(8,128)(2,1)S(1)}) custom-call(s32[8]{0:T(128)S(1)} %stack.44.pos, bf16[2,2,256,2048]{3,2,1,0:T(8,128)(2,1)S(1)} %up.1.hidden, bf16[512,512]{1,0:T(8,128)(2,1)S(1)} %get-tuple-element.296.rest_0_, bf16[512,512]{1,0:T(8,128)(2,1)S(1)} %collective-permute-done.28.rest_1_, ...), custom_call_target="tpu_custom_call" | custom-call | bytes 1024 | tf_op jit(solution)/shard_map/down/pallas_call | solution.py:560
  128.8 5.7 %collective-permute-done.32.rest_3_ = bf16[256,512]{1,0:T(8,128)(2,1)S(1)} collective-permute-done((bf16[256,512]{1,0:T(8,128)(2,1)S(1)}, bf16[256,512]{1,0:T(8,128)(2,1)S(1)}, u32[]{:S(2)}, u32[]{:S(2)}) %collective-permute-start.32) | collective-permute-done | bytes 262176 | tf_op jit(solution)/shard_map/ppermute | solution.py:38
  135.4 3.1 %down.3 = (bf16[2,256,512]{2,1,0:T(8,128)(2,1)S(1)}, bf16[2,256,512]{2,1,0:T(8,128)(2,1)S(1)}) custom-call(s32[8]{0:T(128)S(1)} %stack.44.pos, bf16[2,2,256,2048]{3,2,1,0:T(8,128)(2,1)S(1)} %up.1.hidden, bf16[264,512]{1,0:T(8,128)(2,1)S(1)} %get-tuple-element.310.rest_0_, bf16[264,512]{1,0:T(8,128)(2,1)S(1)} %collective-permute-done.31.rest_1_, ...), custom_call_target="tpu_custom_call" | custom-call | bytes 1024 | tf_op jit(solution)/shard_map/down/pallas_call | solution.py:560
  140.5 1.9 %output.3 = (bf16[2,256,1024]{2,1,0:T(8,128)(2,1)}, f32[32,1,2]{2,1,0:T(1,128)S(1)}) custom-call(s32[8]{0:T(128)S(1)} %stack.44.pos, f32[2,256,1024]{2,1,0:T(8,128)S(1)} %get-tuple-element.308.residual, bf16[2,256,1024]{2,1,0:T(8,128)(2,1)S(1)} %bitcast.19, bf16[2,256,512]{2,1,0:T(8,128)(2,1)S(1)} %get-tuple-element.318.rest_0_, ...), custom_call_target="tpu_custom_call" | custom-call | bytes 1024 | tf_op jit(solution)/shard_map/output/pallas_call | solution.py:614
  142.5 10.1 %all_to_all.5 = f32[32,1,2]{2,1,0:T(1,128)S(1)} all-to-all(f32[32,1,2]{2,1,0:T(1,128)S(1)} %get-tuple-element.325), channel_id=1, replica_groups=mesh['dp'=16,'mp'=2] {'dp','mp'}, dimensions={0} | all-to-all | bytes 512 | tf_op jit(solution)/shard_map/all_to_all | solution.py:760
  (95 shorter events, 41.3 us)
Async XLA Ops:
  0.6 15.6 %collective-permute-start.3 = (bf16[512,768]{1,0:T(8,128)(2,1)}, bf16[512,768]{1,0:T(8,128)(2,1)S(1)}, u32[]{:S(2)}, u32[]{:S(2)}) collective-permute-start(bf16[512,768]{1,0:T(8,128)(2,1)} %bitcast.20), channel_id=1, source_target_pairs={{0,1},{1,0},{2,3},{3,2},{4,5},{5,4},{6,7},{7,6},{8,9},{9,8},{10,11... | collective-permute-start | bytes 2359304 | tf_op jit(solution)/shard_map/ppermute | solution.py:92
  3.4 12.9 %collective-permute-start = (bf16[304,512]{1,0:T(8,128)(2,1)}, bf16[304,512]{1,0:T(8,128)(2,1)S(1)}, u32[]{:S(2)}, u32[]{:S(2)}) collective-permute-start(bf16[304,512]{1,0:T(8,128)(2,1)} %get-tuple-element.167.refs_0_), channel_id=1, source_target_pairs={{0,8},{2,10},{4,12},{6,14},{8,16},{10,18},{12,20},{14,22},{16,24},... | collective-permute-start | bytes 933896 | tf_op jit(solution)/shard_map/ppermute | solution.py:38
  16.3 11.6 %collective-permute-start.7 = (bf16[304,512]{1,0:T(8,128)(2,1)S(1)}, bf16[304,512]{1,0:T(8,128)(2,1)S(1)}, u32[]{:S(2)}, u32[]{:S(2)}) collective-permute-start(bf16[304,512]{1,0:T(8,128)(2,1)S(1)} %collective-permute-done.refs_1_), channel_id=1, source_target_pairs={{0,8},{2,10},{4,12},{6,14},{8,16},{10,18},{12,20},{14,22},{16,24},... | collective-permute-start | bytes 933896 | tf_op jit(solution)/shard_map/ppermute | solution.py:38
  28.0 17.2 %collective-permute-start.10 = (bf16[640,512]{1,0:T(8,128)(2,1)S(1)}, bf16[640,512]{1,0:T(8,128)(2,1)S(1)}, u32[]{:S(2)}, u32[]{:S(2)}) collective-permute-start(bf16[640,512]{1,0:T(8,128)(2,1)S(1)} %get-tuple-element.247.rest_2_.rest_0_), channel_id=1, source_target_pairs={{0,2},{2,0},{4,6},{6,4},{8,10},{10,8},{12,14},{14,12},{16,18},{18,... | collective-permute-start | bytes 1966088 | tf_op jit(solution)/shard_map/ppermute | solution.py:38
  28.8 16.4 %collective-permute-start.9 = (bf16[576,512]{1,0:T(8,128)(2,1)S(1)}, bf16[576,512]{1,0:T(8,128)(2,1)S(1)}, u32[]{:S(2)}, u32[]{:S(2)}) collective-permute-start(bf16[576,512]{1,0:T(8,128)(2,1)S(1)} %get-tuple-element.245.rest_0_), channel_id=1, source_target_pairs={{0,4},{2,6},{4,0},{6,2},{8,12},{10,14},{12,8},{14,10},{16,20},{18,... | collective-permute-start | bytes 1769480 | tf_op jit(solution)/shard_map/ppermute | solution.py:38
  30.3 14.9 %collective-permute-start.11 = (bf16[304,512]{1,0:T(8,128)(2,1)S(1)}, bf16[304,512]{1,0:T(8,128)(2,1)S(1)}, u32[]{:S(2)}, u32[]{:S(2)}) collective-permute-start(bf16[304,512]{1,0:T(8,128)(2,1)S(1)} %collective-permute-done.7.refs_0_), channel_id=1, source_target_pairs={{0,8},{2,10},{4,12},{6,14},{8,16},{10,18},{12,20},{14,22},{16,24},... | collective-permute-start | bytes 933896 | tf_op jit(solution)/shard_map/ppermute | solution.py:38
  31.9 13.3 %collective-permute-start.8 = (bf16[256,512]{1,0:T(8,128)(2,1)S(1)}, bf16[256,512]{1,0:T(8,128)(2,1)S(1)}, u32[]{:S(2)}, u32[]{:S(2)}) collective-permute-start(bf16[256,512]{1,0:T(8,128)(2,1)S(1)} %get-tuple-element.238.refs_0_), channel_id=1, source_target_pairs={{0,8},{2,10},{4,12},{6,14},{8,16},{10,18},{12,20},{14,22},{16,24},... | collective-permute-start | bytes 786440 | tf_op jit(solution)/shard_map/ppermute | solution.py:38
  45.2 13.1 %collective-permute-start.14 = (bf16[520,512]{1,0:T(8,128)(2,1)S(1)}, bf16[520,512]{1,0:T(8,128)(2,1)S(1)}, u32[]{:S(2)}, u32[]{:S(2)}) collective-permute-start(bf16[520,512]{1,0:T(8,128)(2,1)S(1)} %stack.49), channel_id=1, source_target_pairs={{0,8},{2,10},{4,12},{6,14},{8,16},{10,18},{12,20},{14,22},{16,24},... | collective-permute-start | bytes 1597448 | tf_op jit(solution)/shard_map/ppermute | solution.py:38
  58.3 12.1 %collective-permute-start.16 = (bf16[520,512]{1,0:T(8,128)(2,1)S(1)}, bf16[520,512]{1,0:T(8,128)(2,1)S(1)}, u32[]{:S(2)}, u32[]{:S(2)}) collective-permute-start(bf16[520,512]{1,0:T(8,128)(2,1)S(1)} %collective-permute-done.14.refs_3_.refs_0_), channel_id=1, source_target_pairs={{0,8},{2,10},{4,12},{6,14},{8,16},{10,18},{12,20},{14,22},{16,24},... | collective-permute-start | bytes 1597448 | tf_op jit(solution)/shard_map/ppermute | solution.py:38
  58.4 10.2 %collective-permute-start.17 = (bf16[512,512]{1,0:T(8,128)(2,1)S(1)}, bf16[512,512]{1,0:T(8,128)(2,1)S(1)}, u32[]{:S(2)}, u32[]{:S(2)}) collective-permute-start(bf16[512,512]{1,0:T(8,128)(2,1)S(1)} %get-tuple-element.236.rest_4_), channel_id=1, source_target_pairs={{0,4},{2,6},{4,0},{6,2},{8,12},{10,14},{12,8},{14,10},{16,20},{18,... | collective-permute-start | bytes 1572872 | tf_op jit(solution)/shard_map/ppermute | solution.py:38
  70.5 16.5 %collective-permute-start.19 = (bf16[520,512]{1,0:T(8,128)(2,1)S(1)}, bf16[520,512]{1,0:T(8,128)(2,1)S(1)}, u32[]{:S(2)}, u32[]{:S(2)}) collective-permute-start(bf16[520,512]{1,0:T(8,128)(2,1)S(1)} %stack.51), channel_id=1, source_target_pairs={{0,8},{2,10},{4,12},{6,14},{8,16},{10,18},{12,20},{14,22},{16,24},... | collective-permute-start | bytes 1597448 | tf_op jit(solution)/shard_map/ppermute | solution.py:38
  70.8 14.6 %collective-permute-start.20 = (bf16[512,512]{1,0:T(8,128)(2,1)S(1)}, bf16[512,512]{1,0:T(8,128)(2,1)S(1)}, u32[]{:S(2)}, u32[]{:S(2)}) collective-permute-start(bf16[512,512]{1,0:T(8,128)(2,1)S(1)} %get-tuple-element.282.rest_0_), channel_id=1, source_target_pairs={{0,4},{2,6},{4,0},{6,2},{8,12},{10,14},{12,8},{14,10},{16,20},{18,... | collective-permute-start | bytes 1572872 | tf_op jit(solution)/shard_map/ppermute | solution.py:38
  71.4 14.1 %collective-permute-start.21 = (bf16[512,512]{1,0:T(8,128)(2,1)S(1)}, bf16[512,512]{1,0:T(8,128)(2,1)S(1)}, u32[]{:S(2)}, u32[]{:S(2)}) collective-permute-start(bf16[512,512]{1,0:T(8,128)(2,1)S(1)} %get-tuple-element.284.rest_2_), channel_id=1, source_target_pairs={{0,2},{2,0},{4,6},{6,4},{8,10},{10,8},{12,14},{14,12},{16,18},{18,... | collective-permute-start | bytes 1572872 | tf_op jit(solution)/shard_map/ppermute | solution.py:38
  87.1 16.4 %collective-permute-start.23 = (bf16[520,512]{1,0:T(8,128)(2,1)S(1)}, bf16[520,512]{1,0:T(8,128)(2,1)S(1)}, u32[]{:S(2)}, u32[]{:S(2)}) collective-permute-start(bf16[520,512]{1,0:T(8,128)(2,1)S(1)} %stack.53), channel_id=1, source_target_pairs={{0,8},{2,10},{4,12},{6,14},{8,16},{10,18},{12,20},{14,22},{16,24},... | collective-permute-start | bytes 1597448 | tf_op jit(solution)/shard_map/ppermute | solution.py:38
  87.3 14.4 %collective-permute-start.24 = (bf16[512,512]{1,0:T(8,128)(2,1)S(1)}, bf16[512,512]{1,0:T(8,128)(2,1)S(1)}, u32[]{:S(2)}, u32[]{:S(2)}) collective-permute-start(bf16[512,512]{1,0:T(8,128)(2,1)S(1)} %get-tuple-element.286.rest_4_), channel_id=1, source_target_pairs={{0,4},{2,6},{4,0},{6,2},{8,12},{10,14},{12,8},{14,10},{16,20},{18,... | collective-permute-start | bytes 1572872 | tf_op jit(solution)/shard_map/ppermute | solution.py:38
  87.8 14.1 %collective-permute-start.25 = (bf16[512,512]{1,0:T(8,128)(2,1)S(1)}, bf16[512,512]{1,0:T(8,128)(2,1)S(1)}, u32[]{:S(2)}, u32[]{:S(2)}) collective-permute-start(bf16[512,512]{1,0:T(8,128)(2,1)S(1)} %get-tuple-element.288.rest_6_), channel_id=1, source_target_pairs={{0,2},{2,0},{4,6},{6,4},{8,10},{10,8},{12,14},{14,12},{16,18},{18,... | collective-permute-start | bytes 1572872 | tf_op jit(solution)/shard_map/ppermute | solution.py:38
  103.5 16.3 %collective-permute-start.27 = (bf16[520,512]{1,0:T(8,128)(2,1)S(1)}, bf16[520,512]{1,0:T(8,128)(2,1)S(1)}, u32[]{:S(2)}, u32[]{:S(2)}) collective-permute-start(bf16[520,512]{1,0:T(8,128)(2,1)S(1)} %collective-permute-done.23.refs_3_.refs_1_), channel_id=1, source_target_pairs={{0,8},{2,10},{4,12},{6,14},{8,16},{10,18},{12,20},{14,22},{16,24},... | collective-permute-start | bytes 1597448 | tf_op jit(solution)/shard_map/ppermute | solution.py:38
  104.0 14.0 %collective-permute-start.28 = (bf16[512,512]{1,0:T(8,128)(2,1)S(1)}, bf16[512,512]{1,0:T(8,128)(2,1)S(1)}, u32[]{:S(2)}, u32[]{:S(2)}) collective-permute-start(bf16[512,512]{1,0:T(8,128)(2,1)S(1)} %get-tuple-element.296.rest_0_), channel_id=1, source_target_pairs={{0,4},{2,6},{4,0},{6,2},{8,12},{10,14},{12,8},{14,10},{16,20},{18,... | collective-permute-start | bytes 1572872 | tf_op jit(solution)/shard_map/ppermute | solution.py:38
  105.4 13.8 %collective-permute-start.29 = (bf16[512,512]{1,0:T(8,128)(2,1)S(1)}, bf16[512,512]{1,0:T(8,128)(2,1)S(1)}, u32[]{:S(2)}, u32[]{:S(2)}) collective-permute-start(bf16[512,512]{1,0:T(8,128)(2,1)S(1)} %get-tuple-element.298.rest_2_), channel_id=1, source_target_pairs={{0,2},{2,0},{4,6},{6,4},{8,10},{10,8},{12,14},{14,12},{16,18},{18,... | collective-permute-start | bytes 1572872 | tf_op jit(solution)/shard_map/ppermute | solution.py:38
  119.8 15.5 %collective-permute-start.31 = (bf16[264,512]{1,0:T(8,128)(2,1)S(1)}, bf16[264,512]{1,0:T(8,128)(2,1)S(1)}, u32[]{:S(2)}, u32[]{:S(2)}) collective-permute-start(bf16[264,512]{1,0:T(8,128)(2,1)S(1)} %get-tuple-element.310.rest_0_), channel_id=1, source_target_pairs={{0,4},{2,6},{4,0},{6,2},{8,12},{10,14},{12,8},{14,10},{16,20},{18,... | collective-permute-start | bytes 811016 | tf_op jit(solution)/shard_map/ppermute | solution.py:38
  120.4 15.0 %collective-permute-start.35 = (bf16[264,512]{1,0:T(8,128)(2,1)S(1)}, bf16[264,512]{1,0:T(8,128)(2,1)S(1)}, u32[]{:S(2)}, u32[]{:S(2)}) collective-permute-start(bf16[264,512]{1,0:T(8,128)(2,1)S(1)} %get-tuple-element.303), channel_id=1, source_target_pairs={{0,10},{2,8},{4,14},{6,12},{8,18},{10,16},{12,22},{14,20},{16,26},... | collective-permute-start | bytes 811016 | tf_op jit(solution)/shard_map/ppermute | solution.py:38
  121.9 12.6 %collective-permute-start.32 = (bf16[256,512]{1,0:T(8,128)(2,1)S(1)}, bf16[256,512]{1,0:T(8,128)(2,1)S(1)}, u32[]{:S(2)}, u32[]{:S(2)}) collective-permute-start(bf16[256,512]{1,0:T(8,128)(2,1)S(1)} %get-tuple-element.312.rest_2_), channel_id=1, source_target_pairs={{0,2},{2,0},{4,6},{6,4},{8,10},{10,8},{12,14},{14,12},{16,18},{18,... | collective-permute-start | bytes 786440 | tf_op jit(solution)/shard_map/ppermute | solution.py:38
  123.3 11.2 %collective-permute-start.33 = (bf16[256,512]{1,0:T(8,128)(2,1)S(1)}, bf16[256,512]{1,0:T(8,128)(2,1)S(1)}, u32[]{:S(2)}, u32[]{:S(2)}) collective-permute-start(bf16[256,512]{1,0:T(8,128)(2,1)S(1)} %get-tuple-element.314.rest_4_), channel_id=1, source_target_pairs={{0,4},{2,6},{4,0},{6,2},{8,12},{10,14},{12,8},{14,10},{16,20},{18,... | collective-permute-start | bytes 786440 | tf_op jit(solution)/shard_map/ppermute | solution.py:38
  123.8 11.6 %collective-permute-start.34 = (bf16[256,512]{1,0:T(8,128)(2,1)S(1)}, bf16[256,512]{1,0:T(8,128)(2,1)S(1)}, u32[]{:S(2)}, u32[]{:S(2)}) collective-permute-start(bf16[256,512]{1,0:T(8,128)(2,1)S(1)} %get-tuple-element.312.rest_2_), channel_id=1, source_target_pairs={{0,8},{2,10},{4,12},{6,14},{8,16},{10,18},{12,20},{14,22},{16,24},... | collective-permute-start | bytes 786440 | tf_op jit(solution)/shard_map/ppermute | solution.py:38
  (20 other events, 175.6 us)
